TPU v7x, 128 devices: a whole 4x4x4 slice. The times are simulated.
128 devices in a mesh: gx: 8 (over y, core), gy: 16 (over x, z).
Axes of the slice: x: 4, y: 4, z: 4, core: 2. Of those that a mesh axis runs over, the one named last changes fastest.
Arguments:
- source_blocks: bfloat16 [4096, 128, 128], P(('gx', 'gy')), may hold values from -8 to 8
- block_scale: float32 [4096], P(('gx', 'gy')), may hold values from 0.5 to 4
- block_list: int32 [128, 36], replicated, may hold values from 0 to 4095, as said below
- block_count: int32 [128], replicated, may hold values from 27 to 36, as said below
- row_weights: bfloat16 [4608, 128, 128], P(('gx', 'gy')), may hold values from -1 to 1.2
- col_weights: bfloat16 [4608, 128, 128], P(('gx', 'gy')), may hold values from -1 to 1.2
Outputs:
- relief: float32 [12288, 6144], P('gy', 'gx')
- slope_factor: float32 [12288, 6144], P('gy', 'gx')
- flow: bfloat16 [8, 12288, 6144], P(None, 'gy', 'gx')
Inputs may be any that keep to these rules, and one draw needn't show every extreme that they name: `block_list`: every block named in row t is held by a tile of the same gx index as t (holder of b is b // 32). Among the first block_count[t] entries of row t, at most 4 name blocks of one holder; every row reaches 4 for some holder. Entries past the count are valid block numbers and are ignored. `block_count`: some output tile has exactly 36 live windows.
All inputs are finite; a program needn't handle non-finite values.
Results may differ from a plain program's by a relative error of at most 0.03.
Values may be sent and summed in bfloat16 or wider, within the bound.
No kernel may reach another device: no remote copies, remote signals or barrier semaphores. Data moves between devices by JAX's collectives and lax.ppermute only.
A program may use at most 128 MiB of HBM per device.

v0:
```python
import jax
import jax.numpy as jnp
import ml_dtypes
import numpy as np
from jax import lax
from jax.experimental import pallas as pl
from jax.experimental.pallas import tpu as pltpu
from jax.sharding import PartitionSpec as P

W = 6
CAP = 4
RIM = 24
PAD = 32
SIGMA = 10.0
FLAT = 0.05
DIAG = 0.5**0.5
F32 = jnp.float32
BF16 = jnp.bfloat16
MIB = 1 << 20

SMEM = pl.BlockSpec(memory_space=pltpu.SMEM)
VMEM = pl.BlockSpec(memory_space=pltpu.VMEM)
ANY = pl.BlockSpec(memory_space=pl.ANY)


def gather_kernel(
    list_hbm, count_hbm, scale_hbm, blocks_hbm, out_hbm,
    listed, counted, scale, blocks, found, table, staged, sems, out_sems,
):
    holders = lax.axis_size("gy")
    first = lax.axis_index("gx") * holders
    held = blocks.shape[0]
    base = (first + lax.axis_index("gy")) * held
    slots = listed.shape[0]
    copies = [
        pltpu.make_async_copy(list_hbm, listed, sems.at[0]),
        pltpu.make_async_copy(count_hbm, counted, sems.at[1]),
        pltpu.make_async_copy(scale_hbm, scale, sems.at[2]),
        pltpu.make_async_copy(blocks_hbm, blocks, sems.at[3]),
    ]
    for copy in copies:
        copy.start()
    copies[0].wait()
    copies[1].wait()
    shape = found.shape
    row = lax.broadcasted_iota(jnp.int32, shape, 0)
    live = jnp.broadcast_to(counted[...], shape)
    rank = jnp.zeros(shape, jnp.int32)
    chosen = jnp.zeros(shape, jnp.int32)
    for k in range(slots):
        block = jnp.broadcast_to(listed[k : k + 1, :], shape) - base
        hit = (block >= 0) & (block < held) & (k < live)
        chosen = jnp.where(hit & (rank == row), block, chosen)
        rank = rank + hit.astype(jnp.int32)
    found[...] = chosen
    handed = pltpu.make_async_copy(found, table, sems.at[4])
    handed.start()
    handed.wait()
    copies[2].wait()
    copies[3].wait()

    def one_tile(t, carry):
        for j in range(CAP):
            block = table[j, first + t]
            value = blocks[block].astype(F32) * scale[block]
            staged[t, j] = value.astype(BF16)
        pltpu.make_async_copy(staged.at[t], out_hbm.at[t], out_sems.at[t]).start()
        return carry

    lax.fori_loop(0, holders, one_tile, 0)
    for t in range(out_hbm.shape[0]):
        pltpu.make_async_copy(staged.at[t], out_hbm.at[t], out_sems.at[t]).wait()


def gather(block_list, block_count, block_scale, source_blocks):
    held, edge, _ = source_blocks.shape
    holders = lax.axis_size("gy")
    slots, tiles = block_list.shape
    return pl.pallas_call(
        gather_kernel,
        out_shape=jax.ShapeDtypeStruct((holders, CAP, edge, edge), BF16),
        in_specs=[ANY] * 4,
        out_specs=ANY,
        scratch_shapes=[
            pltpu.VMEM((slots, tiles), jnp.int32),
            pltpu.VMEM((1, tiles), jnp.int32),
            pltpu.SMEM((held,), F32),
            pltpu.VMEM((held, edge, edge), BF16),
            pltpu.VMEM((8, tiles), jnp.int32),
            pltpu.SMEM((8, tiles), jnp.int32),
            pltpu.VMEM((holders, CAP, edge, edge), BF16),
            pltpu.SemaphoreType.DMA((5,)),
            pltpu.SemaphoreType.DMA((holders,)),
        ],
        compiler_params=pltpu.CompilerParams(vmem_limit_bytes=56 * MIB),
        name="gather_blocks",
    )(block_list, block_count.reshape(1, tiles), block_scale, source_blocks)


def resample_kernel(
    list_ref, count_ref, arrived_ref, row_ref, col_ref,
    elev_ref, band_ref, left_ref, right_ref, source, seen,
):
    holders = lax.axis_size("gy")
    first = lax.axis_index("gx") * holders
    tile = first + lax.axis_index("gy")
    held = 32
    slots = list_ref.shape[0]
    edge = row_ref.shape[1]
    live = count_ref[tile]
    for h in range(holders):
        seen[h] = 0
    for k in range(slots):
        owner = (list_ref[k, tile] - first * held) // held
        owner = jnp.clip(owner, 0, holders - 1)
        rank = seen[owner]
        source[k] = owner * CAP + jnp.minimum(rank, CAP - 1)
        seen[owner] = rank + (k < live).astype(jnp.int32)

    def one_row(i, carry):
        for j in range(W):
            k = i * W + j
            part = jnp.dot(row_ref[k], arrived_ref[source[k]], preferred_element_type=F32)
            part = jnp.where(k < live, part, 0.0).astype(BF16)
            window = jnp.dot(part, col_ref[k], preferred_element_type=F32)
            span = pl.ds(pl.multiple_of(i * edge, edge), edge)
            elev_ref[j, span, :] = window
            band_ref[span, j * edge : (j + 1) * edge] = window.astype(BF16)
        return carry

    lax.fori_loop(0, W, one_row, 0)

    rows = elev_ref.shape[1]
    chunk = rows // 4
    lane = lax.broadcasted_iota(jnp.int32, (chunk, 128), 1)
    left = jnp.zeros((chunk, 128), F32)
    right = jnp.zeros((chunk, 128), F32)
    for q in range(4):
        mine = (lane >= PAD * q) & (lane < PAD * (q + 1))
        part = elev_ref[0, q * chunk : (q + 1) * chunk, :]
        if q:
            part = pltpu.roll(part, PAD * q, 1)
        left = jnp.where(mine, part, left)
        part = elev_ref[W - 1, q * chunk : (q + 1) * chunk, :]
        if q != 3:
            part = pltpu.roll(part, PAD * (q + 1), 1)
        right = jnp.where(mine, part, right)
    left_ref[...] = left.astype(BF16)
    right_ref[...] = right.astype(BF16)


def resample(block_list, block_count, arrived, row_weights, col_weights):
    slots, edge, _ = row_weights.shape
    side = W * edge
    shapes = [
        ((W, side, edge), F32),
        ((side, side), BF16),
        ((side // 4, 128), BF16),
        ((side // 4, 128), BF16),
    ]
    return pl.pallas_call(
        resample_kernel,
        out_shape=[jax.ShapeDtypeStruct(s, d) for s, d in shapes],
        in_specs=[SMEM, SMEM, VMEM, VMEM, VMEM],
        out_specs=[VMEM] * len(shapes),
        scratch_shapes=[
            pltpu.SMEM((slots,), jnp.int32),
            pltpu.SMEM((lax.axis_size("gy"),), jnp.int32),
        ],
        compiler_params=pltpu.CompilerParams(vmem_limit_bytes=24 * MIB),
        name="resample",
    )(block_list, block_count, arrived, row_weights, col_weights)


def tap(offset):
    value = np.exp(-(offset * offset).astype(np.float32) / np.float32(2.0 * SIGMA * SIGMA))
    return np.where(np.abs(offset) <= RIM, value, 0.0).astype(ml_dtypes.bfloat16)


def tap_total():
    return float(np.sum(tap(np.arange(-RIM, RIM + 1)).astype(np.float64)))


def across_taps(wide, out):
    return jnp.asarray(tap(np.arange(wide)[:, None] - np.arange(out)[None, :] - 128))


def down_taps(step):
    return jnp.asarray(tap(np.arange(step + 2 * PAD)[None, :] - np.arange(step)[:, None] - PAD))


def cells(mid, low, high):
    centre = mid(0)
    ul, uc, ur = low(-1), mid(-1), high(-1)
    cl, cr = low(0), high(0)
    dl, dc, dr = low(1), mid(1), high(1)
    one = dr - ul
    two = ur - dl
    grad_x = one + two + 2.0 * (cr - cl)
    grad_y = one - two + 2.0 * (dc - uc)
    square = 1.0 + (grad_x * grad_x + grad_y * grad_y) * (1.0 / 64.0)
    slope = square * lax.rsqrt(square)
    raised = centre + FLAT
    slant = centre * DIAG + FLAT
    flows = []
    for value, diagonal in (
        (ul, True), (uc, False), (ur, True), (cl, False),
        (cr, False), (dl, True), (dc, False), (dr, True),
    ):
        drop = slant - value * DIAG if diagonal else raised - value
        flows.append(jnp.maximum(drop, FLAT))
    total = (
        ((flows[0] + flows[1]) + (flows[2] + flows[3]))
        + ((flows[4] + flows[5]) + (flows[6] + flows[7]))
    )
    share = pl.reciprocal(total, approx=True)
    return slope, [(flow * share).astype(BF16) for flow in flows]


def sideways(centre, before, after):
    lane = lax.broadcasted_iota(jnp.int32, centre.shape, 1)
    low = jnp.where(lane == 0, pltpu.roll(before, 1, 1), pltpu.roll(centre, 1, 1))
    high = jnp.where(lane == 127, pltpu.roll(after, 127, 1), pltpu.roll(centre, 127, 1))
    return low, high


def dot(a, b):
    return jnp.dot(a, b, preferred_element_type=F32)


STEP = 176


def inner_kernel(
    elev_ref, band_ref, across, down, relief_hbm, slope_hbm, flow_hbm,
    relief, slope, flow, low_ref, high_ref, sems,
):
    lanes, rows, _ = elev_ref.shape
    steps = (rows - 2 * PAD) // STEP
    count = lanes - 2
    inverse = 1.0 / (tap_total() ** 2)

    def copies(i):
        slot = lax.rem(i, 2)
        at = pl.multiple_of(PAD + i * STEP, 16)
        place = (pl.ds(at, STEP), pl.ds(128, count * 128))
        return (
            pltpu.make_async_copy(relief.at[slot], relief_hbm.at[place], sems.at[slot, 0]),
            pltpu.make_async_copy(slope.at[slot], slope_hbm.at[place], sems.at[slot, 1]),
            pltpu.make_async_copy(
                flow.at[slot], flow_hbm.at[(slice(None),) + place], sems.at[slot, 2]
            ),
        )

    def one_step(i, carry):
        slot = lax.rem(i, 2)
        base = pl.multiple_of(i * STEP, 16)

        @pl.when(i >= 2)
        def drain():
            for copy in copies(i - 2):
                copy.wait()

        smooth = dot(down[...], band_ref[pl.ds(base, STEP + 2 * PAD), :]).astype(BF16)
        for j in range(count // 2):
            value = dot(smooth[:, j * 256 : j * 256 + 512], across[...])
            for h in range(2):
                at = j * 256 + h * 128
                centre = elev_ref[j * 2 + h + 1, pl.ds(base + PAD, STEP), :]
                relief[slot, :, at : at + 128] = (
                    centre - value[:, h * 128 : h * 128 + 128] * inverse
                )
        span = pl.ds(base + PAD - 8, STEP + 16)
        for j in range(count):
            low, high = sideways(elev_ref[j + 1, span, :], elev_ref[j, span, :], elev_ref[j + 2, span, :])
            low_ref[j] = low
            high_ref[j] = high

        for at in range(0, STEP, 16):
            for j in range(count):
                value, parts = cells(
                    lambda d: elev_ref[j + 1, pl.ds(base + at + PAD + d, 16), :],
                    lambda d: low_ref[j, pl.ds(at + 8 + d, 16), :],
                    lambda d: high_ref[j, pl.ds(at + 8 + d, 16), :],
                )
                place = (pl.ds(at, 16), slice(j * 128, (j + 1) * 128))
                slope[(slot,) + place] = value
                for n, part in enumerate(parts):
                    flow[(slot, n) + place] = part
        for copy in copies(i):
            copy.start()
        return carry

    lax.fori_loop(0, steps, one_step, 0)
    for i in (steps - 2, steps - 1):
        for copy in copies(i):
            copy.wait()


def out_shapes(rows, cols):
    return [
        jax.ShapeDtypeStruct((rows, cols), F32),
        jax.ShapeDtypeStruct((rows, cols), F32),
        jax.ShapeDtypeStruct((8, rows, cols), BF16),
    ]


def cost(cells_done):
    return pl.CostEstimate(
        flops=cells_done * 4000, bytes_accessed=cells_done * 24, transcendentals=cells_done * 2
    )


def inner(elevation, band):
    lanes, rows, _ = elevation.shape
    cols = lanes * 128
    wide = (lanes - 2) * 128
    return pl.pallas_call(
        inner_kernel,
        out_shape=out_shapes(rows, cols),
        in_specs=[VMEM] * 4,
        out_specs=[ANY] * 3,
        scratch_shapes=[
            pltpu.VMEM((2, STEP, wide), F32),
            pltpu.VMEM((2, STEP, wide), F32),
            pltpu.VMEM((2, 8, STEP, wide), BF16),
            pltpu.VMEM((lanes - 2, STEP + 16, 128), F32),
            pltpu.VMEM((lanes - 2, STEP + 16, 128), F32),
            pltpu.SemaphoreType.DMA((2, 3)),
        ],
        cost_estimate=cost((rows - 2 * PAD) * wide),
        compiler_params=pltpu.CompilerParams(vmem_limit_bytes=16 * MIB),
        name="inner_cells",
    )(elevation, band, across_taps(512, 256), down_taps(STEP))


def unpack_left(value, q):
    value = value.astype(F32)
    return value if q == 3 else pltpu.roll(value, 96 - PAD * q, 1)


def unpack_right(value, q):
    value = value.astype(F32)
    return value if q == 0 else pltpu.roll(value, 128 - PAD * q, 1)


def sides_kernel(
    elev_ref, band_ref, left_ref, right_ref, across, down, relief_in, slope_in, flow_in,
    relief_hbm, slope_hbm, flow_hbm,
    relief, slope, flow, halo, halo_band, low_ref, high_ref, sems,
):
    lanes, rows, _ = elev_ref.shape
    steps = (rows - 2 * PAD) // STEP
    chunk = rows // 4
    inverse = 1.0 / (tap_total() ** 2)
    for q in range(4):
        span = slice(q * chunk, (q + 1) * chunk)
        for s, value in enumerate((unpack_left(left_ref[...], q), unpack_right(right_ref[...], q))):
            halo[s, span, :] = value
            halo_band[s, span, :] = value.astype(BF16)

    def copies(i, s):
        slot = lax.rem(i, 2)
        at = pl.multiple_of(PAD + i * STEP, 16)
        place = (pl.ds(at, STEP), pl.ds(s * (lanes - 1) * 128, 128))
        return (
            pltpu.make_async_copy(relief.at[slot, s], relief_hbm.at[place], sems.at[slot, s, 0]),
            pltpu.make_async_copy(slope.at[slot, s], slope_hbm.at[place], sems.at[slot, s, 1]),
            pltpu.make_async_copy(
                flow.at[slot, s], flow_hbm.at[(slice(None),) + place], sems.at[slot, s, 2]
            ),
        )

    def one_step(i, carry):
        slot = lax.rem(i, 2)
        base = pl.multiple_of(i * STEP, 16)

        @pl.when(i >= 2)
        def drain():
            for s in range(2):
                for copy in copies(i - 2, s):
                    copy.wait()

        tall = pl.ds(base, STEP + 2 * PAD)
        span = pl.ds(base + PAD - 8, STEP + 16)
        for s in range(2):
            own = dot(down[...], band_ref[tall, s * (lanes - 2) * 128 : s * (lanes - 2) * 128 + 256])
            far = dot(down[...], halo_band[s, tall, :])
            smooth = jnp.concatenate([own, far] if s else [far, own], axis=1).astype(BF16)
            value = dot(smooth, across[...])
            j = s * (lanes - 1)
            relief[slot, s] = elev_ref[j, pl.ds(base + PAD, STEP), :] - value * inverse
            before = elev_ref[j - 1, span, :] if s else halo[0, span, :]
            after = halo[1, span, :] if s else elev_ref[1, span, :]
            low, high = sideways(elev_ref[j, span, :], before, after)
            low_ref[s] = low
            high_ref[s] = high

        for at in range(0, STEP, 16):
            for s in range(2):
                value, parts = cells(
                    lambda d: elev_ref[s * (lanes - 1), pl.ds(base + at + PAD + d, 16), :],
                    lambda d: low_ref[s, pl.ds(at + 8 + d, 16), :],
                    lambda d: high_ref[s, pl.ds(at + 8 + d, 16), :],
                )
                slope[slot, s, pl.ds(at, 16), :] = value
                for n, part in enumerate(parts):
                    flow[slot, s, n, pl.ds(at, 16), :] = part
        for s in range(2):
            for copy in copies(i, s):
                copy.start()
        return carry

    lax.fori_loop(0, steps, one_step, 0)
    for i in (steps - 2, steps - 1):
        for s in range(2):
            for copy in copies(i, s):
                copy.wait()


def sides(elevation, band, left, right, outs):
    lanes, rows, _ = elevation.shape
    return pl.pallas_call(
        sides_kernel,
        out_shape=out_shapes(rows, lanes * 128),
        in_specs=[VMEM] * 6 + [ANY] * 3,
        out_specs=[ANY] * 3,
        input_output_aliases={6: 0, 7: 1, 8: 2},
        scratch_shapes=[
            pltpu.VMEM((2, 2, STEP, 128), F32),
            pltpu.VMEM((2, 2, STEP, 128), F32),
            pltpu.VMEM((2, 2, 8, STEP, 128), BF16),
            pltpu.VMEM((2, rows, 128), F32),
            pltpu.VMEM((2, rows, 128), BF16),
            pltpu.VMEM((2, STEP + 16, 128), F32),
            pltpu.VMEM((2, STEP + 16, 128), F32),
            pltpu.SemaphoreType.DMA((2, 2, 3)),
        ],
        cost_estimate=cost((rows - 2 * PAD) * 256),
        compiler_params=pltpu.CompilerParams(vmem_limit_bytes=16 * MIB),
        name="side_cells",
    )(elevation, band, left, right, across_taps(384, 128), down_taps(STEP), *outs)


def ends_kernel(
    elev_ref, band_ref, left_ref, right_ref, up_ref, down_ref, across, down,
    relief_in, slope_in, flow_in, relief_hbm, slope_hbm, flow_hbm,
    relief, slope, flow, wide, band, low_ref, high_ref, sems,
):
    lanes, rows, _ = elev_ref.shape
    cols = lanes * 128
    near = 2 * PAD
    inverse = 1.0 / (tap_total() ** 2)
    packed = left_ref.shape[0]
    for e in range(2):
        here = slice(PAD, PAD + near) if e == 0 else slice(0, near)
        there = slice(0, PAD) if e == 0 else slice(near, near + PAD)
        other = down_ref if e else up_ref
        own_rows = slice(rows - near, rows) if e else slice(0, near)
        pack_rows = slice(packed - near, packed) if e else slice(0, near)
        band[e, here, 128 : 128 + cols] = band_ref[own_rows, :]
        band[e, there, 128 : 128 + cols] = other[:, 0:cols]
        far_left = unpack_left(left_ref[pack_rows, :], 3 * e)
        far_right = unpack_right(right_ref[pack_rows, :], 3 * e)
        corner_left = unpack_left(other[:, cols : cols + 128], 0 if e else 3)
        corner_right = unpack_right(other[:, cols + 128 : cols + 256], 0 if e else 3)
        band[e, here, 0:128] = far_left.astype(BF16)
        band[e, there, 0:128] = corner_left.astype(BF16)
        band[e, here, 128 + cols :] = far_right.astype(BF16)
        band[e, there, 128 + cols :] = corner_right.astype(BF16)
        if e == 0:
            wide[e, 0, 0:8, :] = corner_left[PAD - 8 : PAD]
            wide[e, 0, 8:48, :] = far_left[0:40]
            wide[e, lanes + 1, 0:8, :] = corner_right[PAD - 8 : PAD]
            wide[e, lanes + 1, 8:48, :] = far_right[0:40]
        else:
            wide[e, 0, 0:40, :] = far_left[near - 40 : near]
            wide[e, 0, 40:48, :] = corner_left[0:8]
            wide[e, lanes + 1, 0:40, :] = far_right[near - 40 : near]
            wide[e, lanes + 1, 40:48, :] = corner_right[0:8]
        for j in range(lanes):
            part = other[:, j * 128 : (j + 1) * 128].astype(F32)
            if e == 0:
                wide[e, j + 1, 0:8, :] = part[PAD - 8 : PAD]
                wide[e, j + 1, 8:48, :] = elev_ref[j, 0:40, :]
            else:
                wide[e, j + 1, 0:40, :] = elev_ref[j, rows - 40 : rows, :]
                wide[e, j + 1, 40:48, :] = part[0:8]

    for e in range(2):
        smooth = dot(down[...], band[e]).astype(BF16)
        for j in range(lanes // 2):
            value = dot(smooth[:, j * 256 : j * 256 + 512], across[...])
            for h in range(2):
                at = j * 256 + h * 128
                relief[e, :, at : at + 128] = (
                    wide[e, j * 2 + h + 1, 8 : 8 + PAD, :] - value[:, h * 128 : h * 128 + 128] * inverse
                )
        for j in range(lanes):
            low, high = sideways(wide[e, j + 1], wide[e, j], wide[e, j + 2])
            low_ref[e, j] = low
            high_ref[e, j] = high
            column = slice(j * 128, (j + 1) * 128)
            for at in range(0, PAD, 16):
                value, parts = cells(
                    lambda d: wide[e, j + 1, at + 8 + d : at + 24 + d, :],
                    lambda d: low_ref[e, j, at + 8 + d : at + 24 + d, :],
                    lambda d: high_ref[e, j, at + 8 + d : at + 24 + d, :],
                )
                slope[e, at : at + 16, column] = value
                for n, part in enumerate(parts):
                    flow[e, n, at : at + 16, column] = part
        place = pl.ds(e * (rows - PAD), PAD)
        pltpu.make_async_copy(relief.at[e], relief_hbm.at[place], sems.at[e, 0]).start()
        pltpu.make_async_copy(slope.at[e], slope_hbm.at[place], sems.at[e, 1]).start()
        pltpu.make_async_copy(flow.at[e], flow_hbm.at[:, place], sems.at[e, 2]).start()
    for e in range(2):
        place = pl.ds(e * (rows - PAD), PAD)
        pltpu.make_async_copy(relief.at[e], relief_hbm.at[place], sems.at[e, 0]).wait()
        pltpu.make_async_copy(slope.at[e], slope_hbm.at[place], sems.at[e, 1]).wait()
        pltpu.make_async_copy(flow.at[e], flow_hbm.at[:, place], sems.at[e, 2]).wait()


def ends(elevation, band, left, right, up, down, outs):
    lanes, rows, _ = elevation.shape
    cols = lanes * 128
    return pl.pallas_call(
        ends_kernel,
        out_shape=out_shapes(rows, cols),
        in_specs=[VMEM] * 8 + [ANY] * 3,
        out_specs=[ANY] * 3,
        input_output_aliases={8: 0, 9: 1, 10: 2},
        scratch_shapes=[
            pltpu.VMEM((2, PAD, cols), F32),
            pltpu.VMEM((2, PAD, cols), F32),
            pltpu.VMEM((2, 8, PAD, cols), BF16),
            pltpu.VMEM((2, lanes + 2, PAD + 16, 128), F32),
            pltpu.VMEM((2, 3 * PAD, cols + 256), BF16),
            pltpu.VMEM((2, lanes, PAD + 16, 128), F32),
            pltpu.VMEM((2, lanes, PAD + 16, 128), F32),
            pltpu.SemaphoreType.DMA((2, 3)),
        ],
        cost_estimate=cost(2 * PAD * cols),
        compiler_params=pltpu.CompilerParams(vmem_limit_bytes=16 * MIB),
        name="end_cells",
    )(elevation, band, left, right, up, down, across_taps(512, 256), down_taps(PAD), *outs)


def exchange(low, high, axis):
    devices = lax.axis_size(axis)
    up = [(i, i + 1) for i in range(devices - 1)]
    down = [(j, i) for i, j in up]
    return lax.ppermute(high, axis, up), lax.ppermute(low, axis, down)


def local(source_blocks, block_scale, block_list, block_count, row_weights, col_weights):
    holders = lax.axis_size("gy")
    edge = source_blocks.shape[1]
    block_list = block_list.T
    outgoing = gather(block_list, block_count, block_scale, source_blocks)
    arrived = lax.all_to_all(
        outgoing, "gy", split_axis=0, concat_axis=0, tiled=True
    ).reshape(holders * CAP, edge, edge)
    elevation, band, left, right = resample(
        block_list, block_count, arrived, row_weights, col_weights
    )
    before, after = exchange(left, right, "gx")
    outs = inner(elevation, band)
    top = jnp.concatenate([band[:PAD], before[:PAD], after[:PAD]], axis=1)
    bottom = jnp.concatenate([band[-PAD:], before[-PAD:], after[-PAD:]], axis=1)
    above, below = exchange(top, bottom, "gy")
    outs = sides(elevation, band, before, after, outs)
    return tuple(ends(elevation, band, before, after, above, below, outs))


def solution(mesh):
    in_specs = (
        P(("gx", "gy"), None, None),
        P(("gx", "gy")),
        P(),
        P(),
        P(("gx", "gy"), None, None),
        P(("gx", "gy"), None, None),
    )
    out_specs = (P("gy", "gx"), P("gy", "gx"), P(None, "gy", "gx"))
    return jax.shard_map(local, mesh=mesh, in_specs=in_specs, out_specs=out_specs, check_vma=False)
```

profile of v0, /device:TPU:11, one launch (start us, length us, event | category | flops | bytes accessed | tf_op | source)
XLA Modules:
  0.0 68.2 jit_solution(4492682239975422488)
XLA Ops:
  0.6 2.9 %gather_blocks.1 = bf16[16,4,128,128]{3,2,1,0:T(8,128)(2,1)} custom-call(s32[36,128]{1,0:T(8,128)} %bitcast.4, s32[1,128]{1,0:T(1,128)} %bitcast.6, f32[32]{0:T(128)} %scale_hbm.1, bf16[32,128,128]{2,1,0:T(8,128)(2,1)} %blocks_hbm.1), custom_call_target="tpu_custom_call" | custom-call | tf_op jit(solution)/shard_map/gather_blocks/pallas_call | solution.py:79
  3.5 0.0 copy-start
  3.5 0.0 copy-start.1
  3.6 0.0 copy-start.5
  3.6 0.0 copy-start.7
  3.6 33.1 %all_to_all.5 = bf16[16,4,128,128]{3,2,1,0:T(8,128)(2,1)S(1)} all-to-all(bf16[16,4,128,128]{3,2,1,0:T(8,128)(2,1)} %gather_blocks.1), channel_id=1, replica_groups=mesh['gx'=8,'gy'=16] {'gy'}, dimensions={0} | all-to-all | bytes 4194304 | tf_op jit(solution)/shard_map/all_to_all | solution.py:561
  36.7 0.0 copy-start.2
  36.7 0.0 copy-start.4
  36.7 0.0 copy-done
  36.7 0.0 copy-done.1
  36.7 0.0 copy-done.5
  36.7 0.0 copy-done.7
  36.7 3.5 %resample.1 = (f32[6,768,128]{2,1,0:T(8,128)S(1)}, bf16[768,768]{1,0:T(8,128)(2,1)S(1)}, bf16[192,128]{1,0:T(8,128)(2,1)S(1)}, bf16[192,128]{1,0:T(8,128)(2,1)S(1)}) custom-call(s32[36,128]{1,0:T(8,128)S(1)} %bitcast.5, s32[128]{0:T(128)S(1)} %copy-done.7, bf16[64,128,128]{2,1,0:T(8,128)(2,1)S(1)} %bitcast.3, bf16[36,128,128]{2,1,0:T(8,128)(2,1)S(1)} %copy-done, ...), custom_call_target="tpu_custom_call" | custom-call | tf_op jit(solution)/shard_map/resample/pallas_call | solution.py:161
  40.2 5.6 %collective-permute-start = (bf16[192,128]{1,0:T(8,128)(2,1)S(1)}, bf16[192,128]{1,0:T(8,128)(2,1)S(1)}, u32[]{:S(2)}, u32[]{:S(2)}) collective-permute-start(bf16[192,128]{1,0:T(8,128)(2,1)S(1)} %get-tuple-element.15), channel_id=1, source_target_pairs={{0,16},{16,32},{32,48},{48,64},{64,80},{80,96},{96,112},{1,17},{17... | collective-permute-start | bytes 147464 | tf_op jit(solution)/shard_map/ppermute | solution.py:553
  45.9 1.9 %collective-permute-start.1 = (bf16[192,128]{1,0:T(8,128)(2,1)S(1)}, bf16[192,128]{1,0:T(8,128)(2,1)S(1)}, u32[]{:S(2)}, u32[]{:S(2)}) collective-permute-start(bf16[192,128]{1,0:T(8,128)(2,1)S(1)} %get-tuple-element.16), channel_id=1, source_target_pairs={{16,0},{32,16},{48,32},{64,48},{80,64},{96,80},{112,96},{17,1},{33... | collective-permute-start | bytes 147464 | tf_op jit(solution)/shard_map/ppermute | solution.py:553
  47.8 0.0 copy-done.2
  47.8 0.0 copy-done.4
  47.8 0.0 copy-start.3
  47.8 6.6 %inner_cells.1 = (f32[768,768]{1,0:T(8,128)}, f32[768,768]{1,0:T(8,128)}, bf16[8,768,768]{2,1,0:T(8,128)(2,1)}) custom-call(f32[6,768,128]{2,1,0:T(8,128)S(1)} %get-tuple-element.13.elev_ref, bf16[768,768]{1,0:T(8,128)(2,1)S(1)} %get-tuple-element.14.band_ref, bf16[512,256]{1,0:T(8,128)(2,1)S(1)} %copy-done.2, bf16[176,240]{1,0:T(8,128)(2,1)S(1)} %copy-done.4), custom_call_target="tpu_custom_call" | custom-call | flops 1441792000 | bytes 8650752 | tf_op jit(solution)/shard_map/inner_cells/pallas_call | solution.py:318
  54.4 0.0 collective-permute-done.left_ref
  54.5 0.0 collective-permute-done.1.right_ref
  54.5 2.0 %collective-permute-start.2 = (bf16[32,1024]{1,0:T(8,128)(2,1)S(1)}, bf16[32,1024]{1,0:T(8,128)(2,1)S(1)}, u32[]{:S(2)}, u32[]{:S(2)}) collective-permute-start(bf16[32,1024]{1,0:T(8,128)(2,1)S(1)} %pad_maximum_fusion), channel_id=1, source_target_pairs={{0,1},{1,2},{2,3},{3,4},{4,5},{5,6},{6,7},{7,8},{8,9},{9,10},{10,1... | collective-permute-start | bytes 196616 | tf_op jit(solution)/shard_map/ppermute | solution.py:553
  56.5 5.4 %collective-permute-start.3 = (bf16[32,1024]{1,0:T(8,128)(2,1)S(1)}, bf16[32,1024]{1,0:T(8,128)(2,1)S(1)}, u32[]{:S(2)}, u32[]{:S(2)}) collective-permute-start(bf16[32,1024]{1,0:T(8,128)(2,1)S(1)} %pad_maximum_fusion.1), channel_id=1, source_target_pairs={{1,0},{2,1},{3,2},{4,3},{5,4},{6,5},{7,6},{8,7},{9,8},{10,9},{11,1... | collective-permute-start | bytes 196616 | tf_op jit(solution)/shard_map/ppermute | solution.py:553
  61.9 0.0 copy-done.3
  61.9 0.0 copy-start.6
  61.9 4.5 %side_cells.1 = (f32[768,768]{1,0:T(8,128)}, f32[768,768]{1,0:T(8,128)}, bf16[8,768,768]{2,1,0:T(8,128)(2,1)}) custom-call(f32[6,768,128]{2,1,0:T(8,128)S(1)} %get-tuple-element.13.elev_ref, bf16[768,768]{1,0:T(8,128)(2,1)S(1)} %get-tuple-element.14.band_ref, ...), custom_call_target="tpu_custom_call", output_to_operand_aliasing={{0}: (6, {}), {1}: (7, {}), {2}: (8, {})} | custom-call | flops 720896000 | bytes 4325376 | tf_op jit(solution)/shard_map/side_cells/pallas_call | solution.py:423
  66.4 0.0 collective-permute-done.2.up_ref
  66.4 0.0 collective-permute-done.3.down_ref
  66.5 0.0 copy-done.6
  66.5 1.8 %end_cells.1 = (f32[768,768]{1,0:T(8,128)}, f32[768,768]{1,0:T(8,128)}, bf16[8,768,768]{2,1,0:T(8,128)(2,1)}) custom-call(f32[6,768,128]{2,1,0:T(8,128)S(1)} %get-tuple-element.13.elev_ref, bf16[768,768]{1,0:T(8,128)(2,1)S(1)} %get-tuple-element.14.band_ref, ...), custom_call_target="tpu_custom_call", output_to_operand_aliasing={{0}: (8, {}), {1}: (9, {}), {2}: (10, {})} | custom-call | flops 196608000 | bytes 1179648 | tf_op jit(solution)/shard_map/end_cells/pallas_call | solution.py:527
  (5 shorter events, 0.0 us)
Async XLA Ops:
  3.5 33.2 %copy-start = (bf16[36,128,128]{2,1,0:T(8,128)(2,1)S(1)}, bf16[36,128,128]{2,1,0:T(8,128)(2,1)}, u32[]{:S(2)}) copy-start(bf16[36,128,128]{2,1,0:T(8,128)(2,1)} %row_ref.1) | copy-start | bytes 3538948
  3.5 33.2 %copy-start.1 = (bf16[36,128,128]{2,1,0:T(8,128)(2,1)S(1)}, bf16[36,128,128]{2,1,0:T(8,128)(2,1)}, u32[]{:S(2)}) copy-start(bf16[36,128,128]{2,1,0:T(8,128)(2,1)} %col_ref.1) | copy-start | bytes 3538948
  3.6 33.2 %copy-start.5 = (s32[128,36]{0,1:T(8,128)S(1)}, s32[128,36]{0,1:T(8,128)}, u32[]{:S(2)}) copy-start(s32[128,36]{0,1:T(8,128)} %param.14) | copy-start | bytes 55300
  3.6 33.2 %copy-start.7 = (s32[128]{0:T(128)S(1)}, s32[128]{0:T(128)}, u32[]{:S(2)}) copy-start(s32[128]{0:T(128)} %count_ref.1) | copy-start | bytes 1540
  36.7 11.1 %copy-start.2 = (bf16[512,256]{1,0:T(8,128)(2,1)S(1)}, bf16[512,256]{1,0:T(8,128)(2,1)}, u32[]{:S(2)}) copy-start(bf16[512,256]{1,0:T(8,128)(2,1)} %constant.8.clone.across) | copy-start | bytes 786436
  36.7 11.1 %copy-start.4 = (bf16[176,240]{1,0:T(8,128)(2,1)S(1)}, bf16[176,240]{1,0:T(8,128)(2,1)}, u32[]{:S(2)}) copy-start(bf16[176,240]{1,0:T(8,128)(2,1)} %constant.9.clone.down) | copy-start | bytes 253444
  40.2 14.2 %collective-permute-start = (bf16[192,128]{1,0:T(8,128)(2,1)S(1)}, bf16[192,128]{1,0:T(8,128)(2,1)S(1)}, u32[]{:S(2)}, u32[]{:S(2)}) collective-permute-start(bf16[192,128]{1,0:T(8,128)(2,1)S(1)} %get-tuple-element.15), channel_id=1, source_target_pairs={{0,16},{16,32},{32,48},{48,64},{64,80},{80,96},{96,112},{1,17},{17... | collective-permute-start | bytes 147464 | tf_op jit(solution)/shard_map/ppermute | solution.py:553
  45.9 8.6 %collective-permute-start.1 = (bf16[192,128]{1,0:T(8,128)(2,1)S(1)}, bf16[192,128]{1,0:T(8,128)(2,1)S(1)}, u32[]{:S(2)}, u32[]{:S(2)}) collective-permute-start(bf16[192,128]{1,0:T(8,128)(2,1)S(1)} %get-tuple-element.16), channel_id=1, source_target_pairs={{16,0},{32,16},{48,32},{64,48},{80,64},{96,80},{112,96},{17,1},{33... | collective-permute-start | bytes 147464 | tf_op jit(solution)/shard_map/ppermute | solution.py:553
  47.8 14.1 %copy-start.3 = (bf16[384,128]{1,0:T(8,128)(2,1)S(1)}, bf16[384,128]{1,0:T(8,128)(2,1)}, u32[]{:S(2)}) copy-start(bf16[384,128]{1,0:T(8,128)(2,1)} %constant.10.clone.across) | copy-start | bytes 294916
  54.5 11.9 %collective-permute-start.2 = (bf16[32,1024]{1,0:T(8,128)(2,1)S(1)}, bf16[32,1024]{1,0:T(8,128)(2,1)S(1)}, u32[]{:S(2)}, u32[]{:S(2)}) collective-permute-start(bf16[32,1024]{1,0:T(8,128)(2,1)S(1)} %pad_maximum_fusion), channel_id=1, source_target_pairs={{0,1},{1,2},{2,3},{3,4},{4,5},{5,6},{6,7},{7,8},{8,9},{9,10},{10,1... | collective-permute-start | bytes 196616 | tf_op jit(solution)/shard_map/ppermute | solution.py:553
  56.5 9.9 %collective-permute-start.3 = (bf16[32,1024]{1,0:T(8,128)(2,1)S(1)}, bf16[32,1024]{1,0:T(8,128)(2,1)S(1)}, u32[]{:S(2)}, u32[]{:S(2)}) collective-permute-start(bf16[32,1024]{1,0:T(8,128)(2,1)S(1)} %pad_maximum_fusion.1), channel_id=1, source_target_pairs={{1,0},{2,1},{3,2},{4,3},{5,4},{6,5},{7,6},{8,7},{9,8},{10,9},{11,1... | collective-permute-start | bytes 196616 | tf_op jit(solution)/shard_map/ppermute | solution.py:553
  61.9 4.5 %copy-start.6 = (bf16[32,96]{1,0:T(8,128)(2,1)S(1)}, bf16[32,96]{1,0:T(8,128)(2,1)}, u32[]{:S(2)}) copy-start(bf16[32,96]{1,0:T(8,128)(2,1)} %constant.11.clone.down) | copy-start | bytes 18436
where the time goes:
time: 69 us; the launch traced here: 68.2 us
  blocking collectives  33.1 us (48%)
  Pallas kernels  19.2 us (28%)
  starting transfers between devices  14.9 us (22%)
  between operations  0.86 us (1%)
    all_to_all x1, blocking collectives, local(): lax.all_to_all(outgoing, 'gy', split_axis=0, concat_axis=0, tiled=True)  33.1 us
    ppermute x4, starting transfers between devices, exchange(): return (lax.ppermute(high, axis, up), lax.ppermute(low, axis, down))  14.9 us
    pallas_call x1, Pallas kernels, inner(): pl.pallas_call(inner_kernel, out_shape=out_shapes(rows, cols), in_specs=[...  6.59 us
    pallas_call x1, Pallas kernels, sides(): pl.pallas_call(sides_kernel, out_shape=out_shapes(rows, lanes * 128), in_...  4.49 us
    pallas_call x1, Pallas kernels, resample(): pl.pallas_call(resample_kernel, out_shape=[jax.ShapeDtypeStruct(s, d) for...  3.5 us
    pallas_call x1, Pallas kernels, gather(): pl.pallas_call(gather_kernel, out_shape=jax.ShapeDtypeStruct((holders, CA...  2.89 us
    pallas_call x1, Pallas kernels, ends(): pl.pallas_call(ends_kernel, out_shape=out_shapes(rows, cols), in_specs=[V...  1.77 us
  transfers between devices with their start and end apart: 4, of which 0 were waited for; matrix products, arithmetic and copies ran while one was open for 0% of the time, Pallas kernels for 16%

commit v1 on v0

v1 whole, which is shorter than its diff:
```python
import jax
import jax.numpy as jnp
import ml_dtypes
import numpy as np
from jax import lax
from jax.experimental import pallas as pl
from jax.experimental.pallas import tpu as pltpu
from jax.sharding import PartitionSpec as P

W = 6
CAP = 4
RIM = 24
PAD = 32
SIGMA = 10.0
FLAT = 0.05
DIAG = 0.5**0.5
F32 = jnp.float32
BF16 = jnp.bfloat16
MIB = 1 << 20

SMEM = pl.BlockSpec(memory_space=pltpu.SMEM)
VMEM = pl.BlockSpec(memory_space=pltpu.VMEM)
ANY = pl.BlockSpec(memory_space=pl.ANY)


def gather_kernel(
    list_hbm, count_hbm, scale_hbm, blocks_hbm, out_hbm,
    listed, counted, scale, blocks, found, table, staged, sems, out_sems,
):
    holders = lax.axis_size("gy")
    first = lax.axis_index("gx") * holders
    held = blocks.shape[0]
    base = (first + lax.axis_index("gy")) * held
    slots = listed.shape[0]
    copies = [
        pltpu.make_async_copy(list_hbm, listed, sems.at[0]),
        pltpu.make_async_copy(count_hbm, counted, sems.at[1]),
        pltpu.make_async_copy(scale_hbm, scale, sems.at[2]),
        pltpu.make_async_copy(blocks_hbm, blocks, sems.at[3]),
    ]
    for copy in copies:
        copy.start()
    copies[0].wait()
    copies[1].wait()
    shape = found.shape
    row = lax.broadcasted_iota(jnp.int32, shape, 0)
    live = jnp.broadcast_to(counted[...], shape)
    rank = jnp.zeros(shape, jnp.int32)
    chosen = jnp.zeros(shape, jnp.int32)
    for k in range(slots):
        block = jnp.broadcast_to(listed[k : k + 1, :], shape) - base
        hit = (block >= 0) & (block < held) & (k < live)
        chosen = jnp.where(hit & (rank == row), block, chosen)
        rank = rank + hit.astype(jnp.int32)
    found[...] = chosen
    handed = pltpu.make_async_copy(found, table, sems.at[4])
    handed.start()
    handed.wait()
    copies[2].wait()
    copies[3].wait()

    def one_tile(t, carry):
        for j in range(CAP):
            block = table[j, first + t]
            value = blocks[block].astype(F32) * scale[block]
            staged[t, j] = value.astype(BF16)
        pltpu.make_async_copy(staged.at[t], out_hbm.at[t], out_sems.at[t]).start()
        return carry

    lax.fori_loop(0, holders, one_tile, 0)
    for t in range(out_hbm.shape[0]):
        pltpu.make_async_copy(staged.at[t], out_hbm.at[t], out_sems.at[t]).wait()


def gather(block_list, block_count, block_scale, source_blocks):
    held, edge, _ = source_blocks.shape
    holders = lax.axis_size("gy")
    slots, tiles = block_list.shape
    return pl.pallas_call(
        gather_kernel,
        out_shape=jax.ShapeDtypeStruct((holders, CAP, edge, edge), BF16),
        in_specs=[ANY] * 4,
        out_specs=ANY,
        scratch_shapes=[
            pltpu.VMEM((slots, tiles), jnp.int32),
            pltpu.VMEM((1, tiles), jnp.int32),
            pltpu.SMEM((held,), F32),
            pltpu.VMEM((held, edge, edge), BF16),
            pltpu.VMEM((8, tiles), jnp.int32),
            pltpu.SMEM((8, tiles), jnp.int32),
            pltpu.VMEM((holders, CAP, edge, edge), BF16),
            pltpu.SemaphoreType.DMA((5,)),
            pltpu.SemaphoreType.DMA((holders,)),
        ],
        compiler_params=pltpu.CompilerParams(vmem_limit_bytes=56 * MIB),
        name="gather_blocks",
    )(block_list, block_count.reshape(1, tiles), block_scale, source_blocks)


def find_sources(list_ref, count_ref, source, seen):
    holders = lax.axis_size("gy")
    first = lax.axis_index("gx") * holders
    tile = first + lax.axis_index("gy")
    held = 32
    live = count_ref[tile]
    for h in range(holders):
        seen[h] = 0
    for k in range(list_ref.shape[0]):
        owner = (list_ref[k, tile] - first * held) // held
        owner = jnp.clip(owner, 0, holders - 1)
        rank = seen[owner]
        source[k] = owner * CAP + jnp.minimum(rank, CAP - 1)
        seen[owner] = rank + (k < live).astype(jnp.int32)
    return live


def window(k, live, source, arrived_ref, row_ref, col_ref):
    part = dot(row_ref[k], arrived_ref[source[k]])
    part = jnp.where(k < live, part, 0.0).astype(BF16)
    return dot(part, col_ref[k])


def edges_kernel(
    list_ref, count_ref, arrived_ref, row_ref, col_ref, edge_ref, left_ref, right_ref, source, seen
):
    edge = row_ref.shape[1]
    live = find_sources(list_ref, count_ref, source, seen)
    for i in range(W):
        for s in range(2):
            k = i * W + s * (W - 1)
            edge_ref[s, i * edge : (i + 1) * edge, :] = window(
                k, live, source, arrived_ref, row_ref, col_ref
            )
    rows = edge_ref.shape[1]
    chunk = rows // 4
    lane = lax.broadcasted_iota(jnp.int32, (chunk, 128), 1)
    left = jnp.zeros((chunk, 128), F32)
    right = jnp.zeros((chunk, 128), F32)
    for q in range(4):
        mine = (lane >= PAD * q) & (lane < PAD * (q + 1))
        part = edge_ref[0, q * chunk : (q + 1) * chunk, :]
        if q:
            part = pltpu.roll(part, PAD * q, 1)
        left = jnp.where(mine, part, left)
        part = edge_ref[1, q * chunk : (q + 1) * chunk, :]
        if q != 3:
            part = pltpu.roll(part, PAD * (q + 1), 1)
        right = jnp.where(mine, part, right)
    left_ref[...] = left.astype(BF16)
    right_ref[...] = right.astype(BF16)


def edges(block_list, block_count, arrived, row_weights, col_weights):
    slots, edge, _ = row_weights.shape
    side = W * edge
    shapes = [((2, side, edge), F32), ((side // 4, 128), BF16), ((side // 4, 128), BF16)]
    return pl.pallas_call(
        edges_kernel,
        out_shape=[jax.ShapeDtypeStruct(s, d) for s, d in shapes],
        in_specs=[SMEM, SMEM, VMEM, VMEM, VMEM],
        out_specs=[VMEM] * len(shapes),
        scratch_shapes=[
            pltpu.SMEM((slots,), jnp.int32),
            pltpu.SMEM((lax.axis_size("gy"),), jnp.int32),
        ],
        cost_estimate=cost(side * 256),
        compiler_params=pltpu.CompilerParams(vmem_limit_bytes=16 * MIB),
        name="edge_windows",
    )(block_list, block_count, arrived, row_weights, col_weights)


def middle_kernel(
    list_ref, count_ref, arrived_ref, row_ref, col_ref, edge_ref, down,
    inner_ref, low_ref, high_ref, band_ref, fall_ref, source, seen,
):
    edge = row_ref.shape[1]
    rows = band_ref.shape[0]
    live = find_sources(list_ref, count_ref, source, seen)
    for s in range(2):
        band_ref[:, s * (W - 1) * edge : (s * (W - 1) + 1) * edge] = edge_ref[s].astype(BF16)

    for i in range(W):
        span = slice(i * edge, (i + 1) * edge)
        for j in range(1, W - 1):
            value = window(i * W + j, live, source, arrived_ref, row_ref, col_ref)
            inner_ref[j - 1, span, :] = value
            band_ref[span, j * edge : (j + 1) * edge] = value.astype(BF16)
    for i in range((rows - 2 * PAD) // STEP):
        value = dot(down[...], band_ref[i * STEP : (i + 1) * STEP + 2 * PAD, :])
        fall_ref[i * STEP : (i + 1) * STEP, :] = value.astype(BF16)

    def one_span(q, carry):
        span = pl.ds(pl.multiple_of(q * edge, edge), edge)
        pieces = [edge_ref[0, span, :]]
        pieces += [inner_ref[j, span, :] for j in range(W - 2)] + [edge_ref[1, span, :]]
        lane = lax.broadcasted_iota(jnp.int32, pieces[0].shape, 1)
        lows = [pltpu.roll(piece, 1, 1) for piece in pieces]
        highs = [pltpu.roll(piece, 127, 1) for piece in pieces]
        for j in range(W):
            low_ref[j, span, :] = jnp.where(lane == 0, lows[j - 1], lows[j]) if j else lows[j]
            high_ref[j, span, :] = (
                jnp.where(lane == 127, highs[j + 1], highs[j]) if j < W - 1 else highs[j]
            )
        return carry

    lax.fori_loop(0, W, one_span, 0)


def middle(block_list, block_count, arrived, row_weights, col_weights, edge_values):
    slots, edge, _ = row_weights.shape
    side = W * edge
    shapes = [
        ((W - 2, side, edge), F32),
        ((W, side, edge), F32),
        ((W, side, edge), F32),
        ((side, side), BF16),
        ((side - 2 * PAD, side), BF16),
    ]
    return pl.pallas_call(
        middle_kernel,
        out_shape=[jax.ShapeDtypeStruct(s, d) for s, d in shapes],
        in_specs=[SMEM, SMEM] + [VMEM] * 5,
        out_specs=[VMEM] * len(shapes),
        scratch_shapes=[
            pltpu.SMEM((slots,), jnp.int32),
            pltpu.SMEM((lax.axis_size("gy"),), jnp.int32),
        ],
        cost_estimate=cost(side * side),
        compiler_params=pltpu.CompilerParams(vmem_limit_bytes=24 * MIB),
        name="middle_windows",
    )(block_list, block_count, arrived, row_weights, col_weights, edge_values, down_taps(STEP))


def tap(offset):
    value = np.exp(-(offset * offset).astype(np.float32) / np.float32(2.0 * SIGMA * SIGMA))
    return np.where(np.abs(offset) <= RIM, value, 0.0).astype(ml_dtypes.bfloat16)


def tap_total():
    return float(np.sum(tap(np.arange(-RIM, RIM + 1)).astype(np.float64)))


def across_taps(wide, out):
    return jnp.asarray(tap(np.arange(wide)[:, None] - np.arange(out)[None, :] - 128))


def down_taps(step):
    return jnp.asarray(tap(np.arange(step + 2 * PAD)[None, :] - np.arange(step)[:, None] - PAD))


def cells(mid, low, high):
    centre = mid(0)
    ul, uc, ur = low(-1), mid(-1), high(-1)
    cl, cr = low(0), high(0)
    dl, dc, dr = low(1), mid(1), high(1)
    one = dr - ul
    two = ur - dl
    grad_x = one + two + 2.0 * (cr - cl)
    grad_y = one - two + 2.0 * (dc - uc)
    square = 1.0 + (grad_x * grad_x + grad_y * grad_y) * (1.0 / 64.0)
    slope = square * lax.rsqrt(square)
    raised = centre + FLAT
    slant = centre * DIAG + FLAT
    flows = []
    for value, diagonal in (
        (ul, True), (uc, False), (ur, True), (cl, False),
        (cr, False), (dl, True), (dc, False), (dr, True),
    ):
        drop = slant - value * DIAG if diagonal else raised - value
        flows.append(jnp.maximum(drop, FLAT))
    total = (
        ((flows[0] + flows[1]) + (flows[2] + flows[3]))
        + ((flows[4] + flows[5]) + (flows[6] + flows[7]))
    )
    share = pl.reciprocal(total, approx=True)
    return slope, [(flow * share).astype(BF16) for flow in flows]


def sideways(centre, before, after):
    lane = lax.broadcasted_iota(jnp.int32, centre.shape, 1)
    low = jnp.where(lane == 0, pltpu.roll(before, 1, 1), pltpu.roll(centre, 1, 1))
    high = jnp.where(lane == 127, pltpu.roll(after, 127, 1), pltpu.roll(centre, 127, 1))
    return low, high


def dot(a, b):
    return jnp.dot(a, b, preferred_element_type=F32)


STEP = 176


def main_kernel(
    edge_ref, inner_ref, low_ref, high_ref, fall_ref, left_ref, right_ref, across, down,
    relief_hbm, slope_hbm, flow_hbm, relief, slope, flow, far, patched, sems,
):
    rows, cols = low_ref.shape[1], relief.shape[1]
    lanes = cols // 128
    steps = (rows - 2 * PAD) // STEP
    chunk = rows // 4
    inverse = 1.0 / (tap_total() ** 2)
    lane = lax.broadcasted_iota(jnp.int32, (chunk, 128), 1)
    for q in range(4):
        span = slice(q * chunk, (q + 1) * chunk)
        value = unpack_left(left_ref[...], q)
        far[0, span, :] = value.astype(BF16)
        patched[0, span, :] = jnp.where(lane == 0, pltpu.roll(value, 1, 1), low_ref[0, span, :])
        value = unpack_right(right_ref[...], q)
        far[1, span, :] = value.astype(BF16)
        patched[1, span, :] = jnp.where(
            lane == 127, pltpu.roll(value, 127, 1), high_ref[lanes - 1, span, :]
        )

    def copies(i):
        span = pl.ds(pl.multiple_of(i * STEP, 16), STEP)
        place = pl.ds(pl.multiple_of(PAD + i * STEP, 16), STEP)
        return (
            pltpu.make_async_copy(relief.at[span], relief_hbm.at[place], sems.at[i, 0]),
            pltpu.make_async_copy(slope.at[span], slope_hbm.at[place], sems.at[i, 1]),
            pltpu.make_async_copy(flow.at[:, span], flow_hbm.at[:, place], sems.at[i, 2]),
        )

    def mid(j, span):
        if j in (0, lanes - 1):
            return edge_ref[int(j > 0), span, :]
        return inner_ref[j - 1, span, :]

    def low(j, span):
        return low_ref[j, span, :] if j else patched[0, span, :]

    def high(j, span):
        return high_ref[j, span, :] if j < lanes - 1 else patched[1, span, :]

    def one_step(i, carry):
        base = pl.multiple_of(i * STEP, 16)
        tall = pl.ds(base, STEP + 2 * PAD)
        span = pl.ds(base, STEP)
        sides = [dot(down[...], far[s, tall, :]).astype(BF16) for s in range(2)]
        for j in range(lanes // 2):
            at = j * 256
            if j == 0:
                wide = jnp.concatenate([sides[0], fall_ref[span, 0:384]], axis=1)
            elif j == lanes // 2 - 1:
                wide = jnp.concatenate([fall_ref[span, at - 128 :], sides[1]], axis=1)
            else:
                wide = fall_ref[span, at - 128 : at + 384]
            value = dot(wide, across[...])
            for h in range(2):
                centre = mid(j * 2 + h, pl.ds(base + PAD, STEP))
                relief[span, at + h * 128 : at + h * 128 + 128] = (
                    centre - value[:, h * 128 : h * 128 + 128] * inverse
                )
        for q in range(STEP // 16):
            at = pl.multiple_of(base + q * 16, 16)
            for j in range(lanes):
                value, parts = cells(
                    lambda d: mid(j, pl.ds(at + PAD + d, 16)),
                    lambda d: low(j, pl.ds(at + PAD + d, 16)),
                    lambda d: high(j, pl.ds(at + PAD + d, 16)),
                )
                place = (pl.ds(at, 16), slice(j * 128, (j + 1) * 128))
                slope[place] = value
                for n, part in enumerate(parts):
                    flow[(n,) + place] = part
        for copy in copies(i):
            copy.start()
        return carry

    lax.fori_loop(0, steps, one_step, 0)
    for i in range(steps):
        for copy in copies(i):
            copy.wait()


def main(edge_values, inner, low, high, fall, left, right):
    lanes, rows, _ = low.shape
    cols = lanes * 128
    tall = rows - 2 * PAD
    return pl.pallas_call(
        main_kernel,
        out_shape=out_shapes(rows, cols),
        in_specs=[VMEM] * 9,
        out_specs=[ANY] * 3,
        scratch_shapes=[
            pltpu.VMEM((tall, cols), F32),
            pltpu.VMEM((tall, cols), F32),
            pltpu.VMEM((8, tall, cols), BF16),
            pltpu.VMEM((2, rows, 128), BF16),
            pltpu.VMEM((2, rows, 128), F32),
            pltpu.SemaphoreType.DMA((tall // STEP, 3)),
        ],
        cost_estimate=cost(tall * cols),
        compiler_params=pltpu.CompilerParams(vmem_limit_bytes=32 * MIB),
        name="main_cells",
    )(edge_values, inner, low, high, fall, left, right, across_taps(512, 256), down_taps(STEP))


def out_shapes(rows, cols):
    return [
        jax.ShapeDtypeStruct((rows, cols), F32),
        jax.ShapeDtypeStruct((rows, cols), F32),
        jax.ShapeDtypeStruct((8, rows, cols), BF16),
    ]


def cost(cells_done):
    return pl.CostEstimate(
        flops=cells_done * 4000, bytes_accessed=cells_done * 24, transcendentals=cells_done * 2
    )


def unpack_left(value, q):
    value = value.astype(F32)
    return value if q == 3 else pltpu.roll(value, 96 - PAD * q, 1)


def unpack_right(value, q):
    value = value.astype(F32)
    return value if q == 0 else pltpu.roll(value, 128 - PAD * q, 1)


def ends_kernel(
    edge_ref, inner_ref, band_ref, left_ref, right_ref, up_ref, down_ref, across, down,
    relief_in, slope_in, flow_in, relief_hbm, slope_hbm, flow_hbm,
    relief, slope, flow, wide, band, low_ref, high_ref, sems,
):
    rows, cols = band_ref.shape
    lanes = cols // 128
    near = 2 * PAD
    tall = PAD + 16
    inverse = 1.0 / (tap_total() ** 2)
    packed = left_ref.shape[0]
    for e in range(2):
        here = slice(PAD, PAD + near) if e == 0 else slice(0, near)
        there = slice(0, PAD) if e == 0 else slice(near, near + PAD)
        other = down_ref if e else up_ref
        top = e * tall
        own_rows = slice(rows - near, rows) if e else slice(0, near)
        pack_rows = slice(packed - near, packed) if e else slice(0, near)
        band[e, here, 128 : 128 + cols] = band_ref[own_rows, :]
        band[e, there, 128 : 128 + cols] = other[:, 0:cols]
        far_left = unpack_left(left_ref[pack_rows, :], 3 * e)
        far_right = unpack_right(right_ref[pack_rows, :], 3 * e)
        corner_left = unpack_left(other[:, cols : cols + 128], 0 if e else 3)
        corner_right = unpack_right(other[:, cols + 128 : cols + 256], 0 if e else 3)
        band[e, here, 0:128] = far_left.astype(BF16)
        band[e, there, 0:128] = corner_left.astype(BF16)
        band[e, here, 128 + cols :] = far_right.astype(BF16)
        band[e, there, 128 + cols :] = corner_right.astype(BF16)
        if e == 0:
            wide[0, top : top + 8, :] = corner_left[PAD - 8 : PAD]
            wide[0, top + 8 : top + 48, :] = far_left[0:40]
            wide[lanes + 1, top : top + 8, :] = corner_right[PAD - 8 : PAD]
            wide[lanes + 1, top + 8 : top + 48, :] = far_right[0:40]
        else:
            wide[0, top : top + 40, :] = far_left[near - 40 : near]
            wide[0, top + 40 : top + 48, :] = corner_left[0:8]
            wide[lanes + 1, top : top + 40, :] = far_right[near - 40 : near]
            wide[lanes + 1, top + 40 : top + 48, :] = corner_right[0:8]
        for j in range(lanes):
            part = other[:, j * 128 : (j + 1) * 128].astype(F32)
            own = edge_ref.at[int(j > 0)] if j in (0, lanes - 1) else inner_ref.at[j - 1]
            if e == 0:
                wide[j + 1, top : top + 8, :] = part[PAD - 8 : PAD]
                wide[j + 1, top + 8 : top + 48, :] = own[0:40, :]
            else:
                wide[j + 1, top : top + 40, :] = own[rows - 40 : rows, :]
                wide[j + 1, top + 40 : top + 48, :] = part[0:8]

    for e in range(2):
        smooth = dot(down[...], band[e]).astype(BF16)
        for j in range(lanes // 2):
            value = dot(smooth[:, j * 256 : j * 256 + 512], across[...])
            for h in range(2):
                at = j * 256 + h * 128
                relief[e, :, at : at + 128] = (
                    wide[j * 2 + h + 1, e * tall + 8 : e * tall + 8 + PAD, :] - value[:, h * 128 : h * 128 + 128] * inverse
                )
    for j in range(lanes):
        low, high = sideways(wide[j + 1], wide[j], wide[j + 2])
        low_ref[j] = low
        high_ref[j] = high

    def one_end(e, carry):
        for at in range(0, PAD, 16):
            top = pl.multiple_of(e * tall + 8 + at, 8)
            for j in range(lanes):
                value, parts = cells(
                    lambda d: wide[j + 1, pl.ds(top + d, 16), :],
                    lambda d: low_ref[j, pl.ds(top + d, 16), :],
                    lambda d: high_ref[j, pl.ds(top + d, 16), :],
                )
                place = (slice(at, at + 16), slice(j * 128, (j + 1) * 128))
                slope[(e,) + place] = value
                for n, part in enumerate(parts):
                    flow[(e, n) + place] = part
        place = pl.ds(pl.multiple_of(e * (rows - PAD), PAD), PAD)
        pltpu.make_async_copy(relief.at[e], relief_hbm.at[place], sems.at[e, 0]).start()
        pltpu.make_async_copy(slope.at[e], slope_hbm.at[place], sems.at[e, 1]).start()
        pltpu.make_async_copy(flow.at[e], flow_hbm.at[:, place], sems.at[e, 2]).start()
        return carry

    lax.fori_loop(0, 2, one_end, 0)
    for e in range(2):
        place = pl.ds(e * (rows - PAD), PAD)
        pltpu.make_async_copy(relief.at[e], relief_hbm.at[place], sems.at[e, 0]).wait()
        pltpu.make_async_copy(slope.at[e], slope_hbm.at[place], sems.at[e, 1]).wait()
        pltpu.make_async_copy(flow.at[e], flow_hbm.at[:, place], sems.at[e, 2]).wait()


def ends(edge_values, inner, band, left, right, up, down, outs):
    rows, cols = band.shape
    lanes = cols // 128
    return pl.pallas_call(
        ends_kernel,
        out_shape=out_shapes(rows, cols),
        in_specs=[VMEM] * 9 + [ANY] * 3,
        out_specs=[ANY] * 3,
        input_output_aliases={9: 0, 10: 1, 11: 2},
        scratch_shapes=[
            pltpu.VMEM((2, PAD, cols), F32),
            pltpu.VMEM((2, PAD, cols), F32),
            pltpu.VMEM((2, 8, PAD, cols), BF16),
            pltpu.VMEM((lanes + 2, 2 * (PAD + 16), 128), F32),
            pltpu.VMEM((2, 3 * PAD, cols + 256), BF16),
            pltpu.VMEM((lanes, 2 * (PAD + 16), 128), F32),
            pltpu.VMEM((lanes, 2 * (PAD + 16), 128), F32),
            pltpu.SemaphoreType.DMA((2, 3)),
        ],
        cost_estimate=cost(2 * PAD * cols),
        compiler_params=pltpu.CompilerParams(vmem_limit_bytes=16 * MIB),
        name="end_cells",
    )(
        edge_values, inner, band, left, right, up, down,
        across_taps(512, 256), down_taps(PAD), *outs,
    )


def exchange(low, high, axis):
    devices = lax.axis_size(axis)
    up = [(i, i + 1) for i in range(devices - 1)]
    down = [(j, i) for i, j in up]
    return lax.ppermute(high, axis, up), lax.ppermute(low, axis, down)


def local(source_blocks, block_scale, block_list, block_count, row_weights, col_weights):
    holders = lax.axis_size("gy")
    edge = source_blocks.shape[1]
    block_list = block_list.T
    outgoing = gather(block_list, block_count, block_scale, source_blocks)
    arrived = lax.all_to_all(
        outgoing, "gy", split_axis=0, concat_axis=0, tiled=True
    ).reshape(holders * CAP, edge, edge)
    weights = (row_weights, col_weights)
    edge_values, left, right = edges(block_list, block_count, arrived, *weights)
    before, after = exchange(left, right, "gx")
    inner, low, high, band, fall = middle(block_list, block_count, arrived, *weights, edge_values)
    top = jnp.concatenate([band[:PAD], before[:PAD], after[:PAD]], axis=1)
    bottom = jnp.concatenate([band[-PAD:], before[-PAD:], after[-PAD:]], axis=1)
    above, below = exchange(top, bottom, "gy")
    outs = main(edge_values, inner, low, high, fall, before, after)
    return tuple(ends(edge_values, inner, band, before, after, above, below, outs))


def solution(mesh):
    in_specs = (
        P(("gx", "gy"), None, None),
        P(("gx", "gy")),
        P(),
        P(),
        P(("gx", "gy"), None, None),
        P(("gx", "gy"), None, None),
    )
    out_specs = (P("gy", "gx"), P("gy", "gx"), P(None, "gy", "gx"))
    return jax.shard_map(local, mesh=mesh, in_specs=in_specs, out_specs=out_specs, check_vma=False)
```

time: 69 us -> 68.5 us (level)
  transfers between devices with their start and end apart: 4 -> 4, of which waited for: 0 -> 0; matrix products, arithmetic and copies ran while one was open for 0% -> 0% of each run, Pallas kernels for 16% -> 18%
where the time goes in v1:
time: 68.5 us; the launch traced here: 67.8 us
  blocking collectives  33.1 us (48%)
  Pallas kernels  18.8 us (27%)
  starting transfers between devices  14.9 us (22%)
  between operations  0.85 us (1%)
    all_to_all x1, blocking collectives, local(): lax.all_to_all(outgoing, 'gy', split_axis=0, concat_axis=0, tiled=True)  33.1 us
    ppermute x4, starting transfers between devices, exchange(): return (lax.ppermute(high, axis, up), lax.ppermute(low, axis, down))  14.9 us
    pallas_call x1, Pallas kernels, main(): pl.pallas_call(main_kernel, out_shape=out_shapes(rows, cols), in_specs=[V...  8.95 us
    pallas_call x1, Pallas kernels, middle(): pl.pallas_call(middle_kernel, out_shape=[jax.ShapeDtypeStruct(s, d) for s...  3.5 us
    pallas_call x1, Pallas kernels, gather(): pl.pallas_call(gather_kernel, out_shape=jax.ShapeDtypeStruct((holders, CA...  2.89 us
    pallas_call x1, Pallas kernels, ends(): pl.pallas_call(ends_kernel, out_shape=out_shapes(rows, cols), in_specs=[V...  1.9 us
    pallas_call x1, Pallas kernels, edges(): pl.pallas_call(edges_kernel, out_shape=[jax.ShapeDtypeStruct(s, d) for s,...  1.57 us
  transfers between devices with their start and end apart: 4, of which 0 were waited for; matrix products, arithmetic and copies ran while one was open for 0% of the time, Pallas kernels for 18%

profile of v1, /device:TPU:11, one launch (start us, length us, event | category | flops | bytes accessed | tf_op | source)
XLA Modules:
  0.0 67.8 jit_solution(5039754531071837069)
XLA Ops:
  0.6 2.9 %gather_blocks.1 = bf16[16,4,128,128]{3,2,1,0:T(8,128)(2,1)} custom-call(s32[36,128]{1,0:T(8,128)} %bitcast.5, s32[1,128]{1,0:T(1,128)} %bitcast.8, f32[32]{0:T(128)} %scale_hbm.1, bf16[32,128,128]{2,1,0:T(8,128)(2,1)} %blocks_hbm.1), custom_call_target="tpu_custom_call" | custom-call | tf_op jit(solution)/shard_map/gather_blocks/pallas_call | solution.py:79
  3.5 0.0 copy-start
  3.5 0.0 copy-start.1
  3.6 0.0 copy-start.4
  3.6 0.0 copy-start.6
  3.6 33.1 %all_to_all.5 = bf16[16,4,128,128]{3,2,1,0:T(8,128)(2,1)S(1)} all-to-all(bf16[16,4,128,128]{3,2,1,0:T(8,128)(2,1)} %gather_blocks.1), channel_id=1, replica_groups=mesh['gx'=8,'gy'=16] {'gy'}, dimensions={0} | all-to-all | bytes 4194304 | tf_op jit(solution)/shard_map/all_to_all | solution.py:551
  36.7 0.0 copy-start.3
  36.7 0.0 copy-done
  36.7 0.0 copy-done.1
  36.7 0.0 copy-done.4
  36.7 0.0 copy-done.6
  36.7 1.6 %edge_windows.1 = (f32[2,768,128]{2,1,0:T(8,128)S(1)}, bf16[192,128]{1,0:T(8,128)(2,1)S(1)}, bf16[192,128]{1,0:T(8,128)(2,1)S(1)}) custom-call(s32[36,128]{1,0:T(8,128)S(1)} %bitcast.6, s32[128]{0:T(128)S(1)} %copy-done.6, bf16[64,128,128]{2,1,0:T(8,128)(2,1)S(1)} %bitcast.3, bf16[36,128,128]{2,1,0:T(8,128)(2,1)S(1)} %copy-done, ...), custom_call_target="tpu_custom_call" | custom-call | flops 786432000 | bytes 4718592 | tf_op jit(solution)/shard_map/edge_windows/pallas_call | solution.py:157
  38.3 5.6 %collective-permute-start = (bf16[192,128]{1,0:T(8,128)(2,1)S(1)}, bf16[192,128]{1,0:T(8,128)(2,1)S(1)}, u32[]{:S(2)}, u32[]{:S(2)}) collective-permute-start(bf16[192,128]{1,0:T(8,128)(2,1)S(1)} %get-tuple-element.17), channel_id=1, source_target_pairs={{0,16},{16,32},{32,48},{48,64},{64,80},{80,96},{96,112},{1,17},{17... | collective-permute-start | bytes 147464 | tf_op jit(solution)/shard_map/ppermute | solution.py:543
  43.9 1.9 %collective-permute-start.1 = (bf16[192,128]{1,0:T(8,128)(2,1)S(1)}, bf16[192,128]{1,0:T(8,128)(2,1)S(1)}, u32[]{:S(2)}, u32[]{:S(2)}) collective-permute-start(bf16[192,128]{1,0:T(8,128)(2,1)S(1)} %get-tuple-element.18), channel_id=1, source_target_pairs={{16,0},{32,16},{48,32},{64,48},{80,64},{96,80},{112,96},{17,1},{33... | collective-permute-start | bytes 147464 | tf_op jit(solution)/shard_map/ppermute | solution.py:543
  45.8 0.0 copy-done.3
  45.8 0.0 copy-start.2
  45.9 3.5 %middle_windows.1 = (f32[4,768,128]{2,1,0:T(8,128)S(1)}, f32[6,768,128]{2,1,0:T(8,128)S(1)}, f32[6,768,128]{2,1,0:T(8,128)S(1)}, bf16[768,768]{1,0:T(8,128)(2,1)S(1)}, bf16[704,768]{1,0:T(8,128)(2,1)S(1)}) custom-call(s32[36,128]{1,0:T(8,128)S(1)} %bitcast.7, s32[128]{0:T(128)S(1)} %copy-done.6, bf16[64,128,128]{2,1,0:T(8,128)(2,1)S(1)} %bitcast.4, ...), custom_call_target="tpu_custom_call" | custom-call | flops 2359296000 | bytes 14155776 | tf_op jit(solution)/shard_map/middle_windows/pallas_call | solution.py:219
  49.4 0.0 collective-permute-done.left_ref
  49.4 0.0 collective-permute-done.1.right_ref
  49.4 2.0 %collective-permute-start.2 = (bf16[32,1024]{1,0:T(8,128)(2,1)S(1)}, bf16[32,1024]{1,0:T(8,128)(2,1)S(1)}, u32[]{:S(2)}, u32[]{:S(2)}) collective-permute-start(bf16[32,1024]{1,0:T(8,128)(2,1)S(1)} %pad_maximum_fusion), channel_id=1, source_target_pairs={{0,1},{1,2},{2,3},{3,4},{4,5},{5,6},{6,7},{7,8},{8,9},{9,10},{10,1... | collective-permute-start | bytes 196616 | tf_op jit(solution)/shard_map/ppermute | solution.py:543
  51.5 5.4 %collective-permute-start.3 = (bf16[32,1024]{1,0:T(8,128)(2,1)S(1)}, bf16[32,1024]{1,0:T(8,128)(2,1)S(1)}, u32[]{:S(2)}, u32[]{:S(2)}) collective-permute-start(bf16[32,1024]{1,0:T(8,128)(2,1)S(1)} %pad_maximum_fusion.1), channel_id=1, source_target_pairs={{1,0},{2,1},{3,2},{4,3},{5,4},{6,5},{7,6},{8,7},{9,8},{10,9},{11,1... | collective-permute-start | bytes 196616 | tf_op jit(solution)/shard_map/ppermute | solution.py:543
  56.9 0.0 copy-done.2
  56.9 0.0 copy-start.5
  56.9 8.9 %main_cells.1 = (f32[768,768]{1,0:T(8,128)}, f32[768,768]{1,0:T(8,128)}, bf16[8,768,768]{2,1,0:T(8,128)(2,1)}) custom-call(f32[2,768,128]{2,1,0:T(8,128)S(1)} %get-tuple-element.14.edge_ref, f32[4,768,128]{2,1,0:T(8,128)S(1)} %get-tuple-element.15.inner_ref, f32[6,768,128]{2,1,0:T(8,128)S(1)} %get-tuple-element.19.low_ref, ...), custom_call_target="tpu_custom_call" | custom-call | flops 2162688000 | bytes 12976128 | tf_op jit(solution)/shard_map/main_cells/pallas_call | solution.py:379
  65.8 0.0 collective-permute-done.2.up_ref
  65.9 0.0 collective-permute-done.3.down_ref
  65.9 0.0 copy-done.5
  65.9 1.9 %end_cells.1 = (f32[768,768]{1,0:T(8,128)}, f32[768,768]{1,0:T(8,128)}, bf16[8,768,768]{2,1,0:T(8,128)(2,1)}) custom-call(f32[2,768,128]{2,1,0:T(8,128)S(1)} %get-tuple-element.14.edge_ref, f32[4,768,128]{2,1,0:T(8,128)S(1)} %get-tuple-element.15.inner_ref, ...), custom_call_target="tpu_custom_call", output_to_operand_aliasing={{0}: (9, {}), {1}: (10, {}), {2}: (11, {})} | custom-call | flops 196608000 | bytes 1179648 | tf_op jit(solution)/shard_map/end_cells/pallas_call | solution.py:514
  (5 shorter events, 0.0 us)
Async XLA Ops:
  3.5 33.2 %copy-start = (bf16[36,128,128]{2,1,0:T(8,128)(2,1)S(1)}, bf16[36,128,128]{2,1,0:T(8,128)(2,1)}, u32[]{:S(2)}) copy-start(bf16[36,128,128]{2,1,0:T(8,128)(2,1)} %row_ref.3) | copy-start | bytes 3538948
  3.5 33.2 %copy-start.1 = (bf16[36,128,128]{2,1,0:T(8,128)(2,1)S(1)}, bf16[36,128,128]{2,1,0:T(8,128)(2,1)}, u32[]{:S(2)}) copy-start(bf16[36,128,128]{2,1,0:T(8,128)(2,1)} %col_ref.3) | copy-start | bytes 3538948
  3.6 33.2 %copy-start.4 = (s32[128,36]{0,1:T(8,128)S(1)}, s32[128,36]{0,1:T(8,128)}, u32[]{:S(2)}) copy-start(s32[128,36]{0,1:T(8,128)} %param.13) | copy-start | bytes 55300
  3.6 33.2 %copy-start.6 = (s32[128]{0:T(128)S(1)}, s32[128]{0:T(128)}, u32[]{:S(2)}) copy-start(s32[128]{0:T(128)} %count_ref.3) | copy-start | bytes 1540
  36.7 9.1 %copy-start.3 = (bf16[176,240]{1,0:T(8,128)(2,1)S(1)}, bf16[176,240]{1,0:T(8,128)(2,1)}, u32[]{:S(2)}) copy-start(bf16[176,240]{1,0:T(8,128)(2,1)} %constant.6.clone.down) | copy-start | bytes 253444
  38.3 11.1 %collective-permute-start = (bf16[192,128]{1,0:T(8,128)(2,1)S(1)}, bf16[192,128]{1,0:T(8,128)(2,1)S(1)}, u32[]{:S(2)}, u32[]{:S(2)}) collective-permute-start(bf16[192,128]{1,0:T(8,128)(2,1)S(1)} %get-tuple-element.17), channel_id=1, source_target_pairs={{0,16},{16,32},{32,48},{48,64},{64,80},{80,96},{96,112},{1,17},{17... | collective-permute-start | bytes 147464 | tf_op jit(solution)/shard_map/ppermute | solution.py:543
  43.9 5.5 %collective-permute-start.1 = (bf16[192,128]{1,0:T(8,128)(2,1)S(1)}, bf16[192,128]{1,0:T(8,128)(2,1)S(1)}, u32[]{:S(2)}, u32[]{:S(2)}) collective-permute-start(bf16[192,128]{1,0:T(8,128)(2,1)S(1)} %get-tuple-element.18), channel_id=1, source_target_pairs={{16,0},{32,16},{48,32},{64,48},{80,64},{96,80},{112,96},{17,1},{33... | collective-permute-start | bytes 147464 | tf_op jit(solution)/shard_map/ppermute | solution.py:543
  45.8 11.0 %copy-start.2 = (bf16[512,256]{1,0:T(8,128)(2,1)S(1)}, bf16[512,256]{1,0:T(8,128)(2,1)}, u32[]{:S(2)}) copy-start(bf16[512,256]{1,0:T(8,128)(2,1)} %constant.7.clone.across) | copy-start | bytes 786436
  49.4 16.4 %collective-permute-start.2 = (bf16[32,1024]{1,0:T(8,128)(2,1)S(1)}, bf16[32,1024]{1,0:T(8,128)(2,1)S(1)}, u32[]{:S(2)}, u32[]{:S(2)}) collective-permute-start(bf16[32,1024]{1,0:T(8,128)(2,1)S(1)} %pad_maximum_fusion), channel_id=1, source_target_pairs={{0,1},{1,2},{2,3},{3,4},{4,5},{5,6},{6,7},{7,8},{8,9},{9,10},{10,1... | collective-permute-start | bytes 196616 | tf_op jit(solution)/shard_map/ppermute | solution.py:543
  51.5 14.4 %collective-permute-start.3 = (bf16[32,1024]{1,0:T(8,128)(2,1)S(1)}, bf16[32,1024]{1,0:T(8,128)(2,1)S(1)}, u32[]{:S(2)}, u32[]{:S(2)}) collective-permute-start(bf16[32,1024]{1,0:T(8,128)(2,1)S(1)} %pad_maximum_fusion.1), channel_id=1, source_target_pairs={{1,0},{2,1},{3,2},{4,3},{5,4},{6,5},{7,6},{8,7},{9,8},{10,9},{11,1... | collective-permute-start | bytes 196616 | tf_op jit(solution)/shard_map/ppermute | solution.py:543
  56.9 9.0 %copy-start.5 = (bf16[32,96]{1,0:T(8,128)(2,1)S(1)}, bf16[32,96]{1,0:T(8,128)(2,1)}, u32[]{:S(2)}) copy-start(bf16[32,96]{1,0:T(8,128)(2,1)} %constant.8.clone.down) | copy-start | bytes 18436

commit v2 on v1

--- a/solution.py
+++ b/solution.py
@@ -259,21 +259,20 @@
     grad_y = one - two + 2.0 * (dc - uc)
     square = 1.0 + (grad_x * grad_x + grad_y * grad_y) * (1.0 / 64.0)
     slope = square * lax.rsqrt(square)
-    raised = centre + FLAT
-    slant = centre * DIAG + FLAT
     flows = []
+    own = centre.astype(BF16)
     for value, diagonal in (
         (ul, True), (uc, False), (ur, True), (cl, False),
         (cr, False), (dl, True), (dc, False), (dr, True),
     ):
-        drop = slant - value * DIAG if diagonal else raised - value
-        flows.append(jnp.maximum(drop, FLAT))
+        drop = jnp.maximum(own - value.astype(BF16), 0)
+        flows.append((drop * BF16(DIAG) if diagonal else drop) + BF16(FLAT))
     total = (
         ((flows[0] + flows[1]) + (flows[2] + flows[3]))
         + ((flows[4] + flows[5]) + (flows[6] + flows[7]))
     )
-    share = pl.reciprocal(total, approx=True)
-    return slope, [(flow * share).astype(BF16) for flow in flows]
+    share = pl.reciprocal(total.astype(F32), approx=True).astype(BF16)
+    return slope, [flow * share for flow in flows]
 
 
 def sideways(centre, before, after):

time: 68.5 us -> 67.2 us (0.981)
  Pallas kernels: 18.8 us -> 17.5 us
    pallas_call x1, Pallas kernels: 8.95 us -> 7.73 us  [main(): pl.pallas_call(main_kernel, out_shape=out_shapes(rows, cols), in_specs=[V...]
  transfers between devices with their start and end apart: 4 -> 4, of which waited for: 0 -> 0; matrix products, arithmetic and copies ran while one was open for 0% -> 0% of each run, Pallas kernels for 18% -> 17%
where the time goes in v2:
time: 67.2 us; the launch traced here: 66.4 us
  blocking collectives  33.1 us (49%)
  Pallas kernels  17.5 us (26%)
  starting transfers between devices  14.9 us (22%)
  between operations  0.85 us (1%)
    all_to_all x1, blocking collectives, local(): lax.all_to_all(outgoing, 'gy', split_axis=0, concat_axis=0, tiled=True)  33.1 us
    ppermute x4, starting transfers between devices, exchange(): return (lax.ppermute(high, axis, up), lax.ppermute(low, axis, down))  14.9 us
    pallas_call x1, Pallas kernels, main(): pl.pallas_call(main_kernel, out_shape=out_shapes(rows, cols), in_specs=[V...  7.73 us
    pallas_call x1, Pallas kernels, middle(): pl.pallas_call(middle_kernel, out_shape=[jax.ShapeDtypeStruct(s, d) for s...  3.5 us
    pallas_call x1, Pallas kernels, gather(): pl.pallas_call(gather_kernel, out_shape=jax.ShapeDtypeStruct((holders, CA...  2.89 us
    pallas_call x1, Pallas kernels, ends(): pl.pallas_call(ends_kernel, out_shape=out_shapes(rows, cols), in_specs=[V...  1.78 us
    pallas_call x1, Pallas kernels, edges(): pl.pallas_call(edges_kernel, out_shape=[jax.ShapeDtypeStruct(s, d) for s,...  1.57 us
  transfers between devices with their start and end apart: 4, of which 0 were waited for; matrix products, arithmetic and copies ran while one was open for 0% of the time, Pallas kernels for 17%

profile of v2, /device:TPU:11, one launch (start us, length us, event | category | flops | bytes accessed | tf_op | source)
XLA Modules:
  0.0 66.4 jit_solution(4469974618432077091)
XLA Ops:
  0.6 2.9 %gather_blocks.1 = bf16[16,4,128,128]{3,2,1,0:T(8,128)(2,1)} custom-call(s32[36,128]{1,0:T(8,128)} %bitcast.5, s32[1,128]{1,0:T(1,128)} %bitcast.8, f32[32]{0:T(128)} %scale_hbm.1, bf16[32,128,128]{2,1,0:T(8,128)(2,1)} %blocks_hbm.1), custom_call_target="tpu_custom_call" | custom-call | tf_op jit(solution)/shard_map/gather_blocks/pallas_call | solution.py:79
  3.5 0.0 copy-start
  3.5 0.0 copy-start.1
  3.6 0.0 copy-start.4
  3.6 0.0 copy-start.6
  3.6 33.1 %all_to_all.5 = bf16[16,4,128,128]{3,2,1,0:T(8,128)(2,1)S(1)} all-to-all(bf16[16,4,128,128]{3,2,1,0:T(8,128)(2,1)} %gather_blocks.1), channel_id=1, replica_groups=mesh['gx'=8,'gy'=16] {'gy'}, dimensions={0} | all-to-all | bytes 4194304 | tf_op jit(solution)/shard_map/all_to_all | solution.py:550
  36.7 0.0 copy-start.3
  36.7 0.0 copy-done
  36.7 0.0 copy-done.1
  36.7 0.0 copy-done.4
  36.7 0.0 copy-done.6
  36.7 1.6 %edge_windows.1 = (f32[2,768,128]{2,1,0:T(8,128)S(1)}, bf16[192,128]{1,0:T(8,128)(2,1)S(1)}, bf16[192,128]{1,0:T(8,128)(2,1)S(1)}) custom-call(s32[36,128]{1,0:T(8,128)S(1)} %bitcast.6, s32[128]{0:T(128)S(1)} %copy-done.6, bf16[64,128,128]{2,1,0:T(8,128)(2,1)S(1)} %bitcast.3, bf16[36,128,128]{2,1,0:T(8,128)(2,1)S(1)} %copy-done, ...), custom_call_target="tpu_custom_call" | custom-call | flops 786432000 | bytes 4718592 | tf_op jit(solution)/shard_map/edge_windows/pallas_call | solution.py:157
  38.3 5.6 %collective-permute-start = (bf16[192,128]{1,0:T(8,128)(2,1)S(1)}, bf16[192,128]{1,0:T(8,128)(2,1)S(1)}, u32[]{:S(2)}, u32[]{:S(2)}) collective-permute-start(bf16[192,128]{1,0:T(8,128)(2,1)S(1)} %get-tuple-element.17), channel_id=1, source_target_pairs={{0,16},{16,32},{32,48},{48,64},{64,80},{80,96},{96,112},{1,17},{17... | collective-permute-start | bytes 147464 | tf_op jit(solution)/shard_map/ppermute | solution.py:542
  43.9 1.9 %collective-permute-start.1 = (bf16[192,128]{1,0:T(8,128)(2,1)S(1)}, bf16[192,128]{1,0:T(8,128)(2,1)S(1)}, u32[]{:S(2)}, u32[]{:S(2)}) collective-permute-start(bf16[192,128]{1,0:T(8,128)(2,1)S(1)} %get-tuple-element.18), channel_id=1, source_target_pairs={{16,0},{32,16},{48,32},{64,48},{80,64},{96,80},{112,96},{17,1},{33... | collective-permute-start | bytes 147464 | tf_op jit(solution)/shard_map/ppermute | solution.py:542
  45.8 0.0 copy-done.3
  45.8 0.0 copy-start.2
  45.9 3.5 %middle_windows.1 = (f32[4,768,128]{2,1,0:T(8,128)S(1)}, f32[6,768,128]{2,1,0:T(8,128)S(1)}, f32[6,768,128]{2,1,0:T(8,128)S(1)}, bf16[768,768]{1,0:T(8,128)(2,1)S(1)}, bf16[704,768]{1,0:T(8,128)(2,1)S(1)}) custom-call(s32[36,128]{1,0:T(8,128)S(1)} %bitcast.7, s32[128]{0:T(128)S(1)} %copy-done.6, bf16[64,128,128]{2,1,0:T(8,128)(2,1)S(1)} %bitcast.4, ...), custom_call_target="tpu_custom_call" | custom-call | flops 2359296000 | bytes 14155776 | tf_op jit(solution)/shard_map/middle_windows/pallas_call | solution.py:219
  49.4 0.0 collective-permute-done.left_ref
  49.4 0.0 collective-permute-done.1.right_ref
  49.4 2.0 %collective-permute-start.2 = (bf16[32,1024]{1,0:T(8,128)(2,1)S(1)}, bf16[32,1024]{1,0:T(8,128)(2,1)S(1)}, u32[]{:S(2)}, u32[]{:S(2)}) collective-permute-start(bf16[32,1024]{1,0:T(8,128)(2,1)S(1)} %pad_maximum_fusion), channel_id=1, source_target_pairs={{0,1},{1,2},{2,3},{3,4},{4,5},{5,6},{6,7},{7,8},{8,9},{9,10},{10,1... | collective-permute-start | bytes 196616 | tf_op jit(solution)/shard_map/ppermute | solution.py:542
  51.5 5.4 %collective-permute-start.3 = (bf16[32,1024]{1,0:T(8,128)(2,1)S(1)}, bf16[32,1024]{1,0:T(8,128)(2,1)S(1)}, u32[]{:S(2)}, u32[]{:S(2)}) collective-permute-start(bf16[32,1024]{1,0:T(8,128)(2,1)S(1)} %pad_maximum_fusion.1), channel_id=1, source_target_pairs={{1,0},{2,1},{3,2},{4,3},{5,4},{6,5},{7,6},{8,7},{9,8},{10,9},{11,1... | collective-permute-start | bytes 196616 | tf_op jit(solution)/shard_map/ppermute | solution.py:542
  56.9 0.0 copy-done.2
  56.9 0.0 copy-start.5
  56.9 7.7 %main_cells.1 = (f32[768,768]{1,0:T(8,128)}, f32[768,768]{1,0:T(8,128)}, bf16[8,768,768]{2,1,0:T(8,128)(2,1)}) custom-call(f32[2,768,128]{2,1,0:T(8,128)S(1)} %get-tuple-element.14.edge_ref, f32[4,768,128]{2,1,0:T(8,128)S(1)} %get-tuple-element.15.inner_ref, f32[6,768,128]{2,1,0:T(8,128)S(1)} %get-tuple-element.19.low_ref, ...), custom_call_target="tpu_custom_call" | custom-call | flops 2162688000 | bytes 12976128 | tf_op jit(solution)/shard_map/main_cells/pallas_call | solution.py:378
  64.6 0.0 collective-permute-done.2.up_ref
  64.6 0.0 collective-permute-done.3.down_ref
  64.6 0.0 copy-done.5
  64.7 1.8 %end_cells.1 = (f32[768,768]{1,0:T(8,128)}, f32[768,768]{1,0:T(8,128)}, bf16[8,768,768]{2,1,0:T(8,128)(2,1)}) custom-call(f32[2,768,128]{2,1,0:T(8,128)S(1)} %get-tuple-element.14.edge_ref, f32[4,768,128]{2,1,0:T(8,128)S(1)} %get-tuple-element.15.inner_ref, ...), custom_call_target="tpu_custom_call", output_to_operand_aliasing={{0}: (9, {}), {1}: (10, {}), {2}: (11, {})} | custom-call | flops 196608000 | bytes 1179648 | tf_op jit(solution)/shard_map/end_cells/pallas_call | solution.py:513
  (5 shorter events, 0.0 us)
Async XLA Ops:
  3.5 33.2 %copy-start = (bf16[36,128,128]{2,1,0:T(8,128)(2,1)S(1)}, bf16[36,128,128]{2,1,0:T(8,128)(2,1)}, u32[]{:S(2)}) copy-start(bf16[36,128,128]{2,1,0:T(8,128)(2,1)} %row_ref.3) | copy-start | bytes 3538948
  3.5 33.2 %copy-start.1 = (bf16[36,128,128]{2,1,0:T(8,128)(2,1)S(1)}, bf16[36,128,128]{2,1,0:T(8,128)(2,1)}, u32[]{:S(2)}) copy-start(bf16[36,128,128]{2,1,0:T(8,128)(2,1)} %col_ref.3) | copy-start | bytes 3538948
  3.6 33.2 %copy-start.4 = (s32[128,36]{0,1:T(8,128)S(1)}, s32[128,36]{0,1:T(8,128)}, u32[]{:S(2)}) copy-start(s32[128,36]{0,1:T(8,128)} %param.13) | copy-start | bytes 55300
  3.6 33.2 %copy-start.6 = (s32[128]{0:T(128)S(1)}, s32[128]{0:T(128)}, u32[]{:S(2)}) copy-start(s32[128]{0:T(128)} %count_ref.3) | copy-start | bytes 1540
  36.7 9.1 %copy-start.3 = (bf16[176,240]{1,0:T(8,128)(2,1)S(1)}, bf16[176,240]{1,0:T(8,128)(2,1)}, u32[]{:S(2)}) copy-start(bf16[176,240]{1,0:T(8,128)(2,1)} %constant.6.clone.down) | copy-start | bytes 253444
  38.3 11.1 %collective-permute-start = (bf16[192,128]{1,0:T(8,128)(2,1)S(1)}, bf16[192,128]{1,0:T(8,128)(2,1)S(1)}, u32[]{:S(2)}, u32[]{:S(2)}) collective-permute-start(bf16[192,128]{1,0:T(8,128)(2,1)S(1)} %get-tuple-element.17), channel_id=1, source_target_pairs={{0,16},{16,32},{32,48},{48,64},{64,80},{80,96},{96,112},{1,17},{17... | collective-permute-start | bytes 147464 | tf_op jit(solution)/shard_map/ppermute | solution.py:542
  43.9 5.5 %collective-permute-start.1 = (bf16[192,128]{1,0:T(8,128)(2,1)S(1)}, bf16[192,128]{1,0:T(8,128)(2,1)S(1)}, u32[]{:S(2)}, u32[]{:S(2)}) collective-permute-start(bf16[192,128]{1,0:T(8,128)(2,1)S(1)} %get-tuple-element.18), channel_id=1, source_target_pairs={{16,0},{32,16},{48,32},{64,48},{80,64},{96,80},{112,96},{17,1},{33... | collective-permute-start | bytes 147464 | tf_op jit(solution)/shard_map/ppermute | solution.py:542
  45.8 11.0 %copy-start.2 = (bf16[512,256]{1,0:T(8,128)(2,1)S(1)}, bf16[512,256]{1,0:T(8,128)(2,1)}, u32[]{:S(2)}) copy-start(bf16[512,256]{1,0:T(8,128)(2,1)} %constant.7.clone.across) | copy-start | bytes 786436
  49.4 15.2 %collective-permute-start.2 = (bf16[32,1024]{1,0:T(8,128)(2,1)S(1)}, bf16[32,1024]{1,0:T(8,128)(2,1)S(1)}, u32[]{:S(2)}, u32[]{:S(2)}) collective-permute-start(bf16[32,1024]{1,0:T(8,128)(2,1)S(1)} %pad_maximum_fusion), channel_id=1, source_target_pairs={{0,1},{1,2},{2,3},{3,4},{4,5},{5,6},{6,7},{7,8},{8,9},{9,10},{10,1... | collective-permute-start | bytes 196616 | tf_op jit(solution)/shard_map/ppermute | solution.py:542
  51.5 13.2 %collective-permute-start.3 = (bf16[32,1024]{1,0:T(8,128)(2,1)S(1)}, bf16[32,1024]{1,0:T(8,128)(2,1)S(1)}, u32[]{:S(2)}, u32[]{:S(2)}) collective-permute-start(bf16[32,1024]{1,0:T(8,128)(2,1)S(1)} %pad_maximum_fusion.1), channel_id=1, source_target_pairs={{1,0},{2,1},{3,2},{4,3},{5,4},{6,5},{7,6},{8,7},{9,8},{10,9},{11,1... | collective-permute-start | bytes 196616 | tf_op jit(solution)/shard_map/ppermute | solution.py:542
  56.9 7.8 %copy-start.5 = (bf16[32,96]{1,0:T(8,128)(2,1)S(1)}, bf16[32,96]{1,0:T(8,128)(2,1)}, u32[]{:S(2)}) copy-start(bf16[32,96]{1,0:T(8,128)(2,1)} %constant.8.clone.down) | copy-start | bytes 18436

commit v3 on v2

--- a/solution.py
+++ b/solution.py
@@ -24,8 +24,9 @@
 
 
 def gather_kernel(
-    list_hbm, count_hbm, scale_hbm, blocks_hbm, out_hbm,
-    listed, counted, scale, blocks, found, table, staged, sems, out_sems,
+    list_hbm, count_hbm, scale_hbm, blocks_hbm, out_hbm, source_hbm,
+    listed, counted, scale, blocks, found, table, staged,
+    named, numbered, seen, source, sems, out_sems,
 ):
     holders = lax.axis_size("gy")
     first = lax.axis_index("gx") * holders
@@ -37,6 +38,8 @@
         pltpu.make_async_copy(count_hbm, counted, sems.at[1]),
         pltpu.make_async_copy(scale_hbm, scale, sems.at[2]),
         pltpu.make_async_copy(blocks_hbm, blocks, sems.at[3]),
+        pltpu.make_async_copy(list_hbm, named, sems.at[5]),
+        pltpu.make_async_copy(count_hbm, numbered, sems.at[6]),
     ]
     for copy in copies:
         copy.start()
@@ -55,6 +58,21 @@
     found[...] = chosen
     handed = pltpu.make_async_copy(found, table, sems.at[4])
     handed.start()
+    copies[4].wait()
+    copies[5].wait()
+    tile = first + lax.axis_index("gy")
+    count = numbered[0, tile]
+    for h in range(out_hbm.shape[0]):
+        seen[h] = 0
+    for k in range(slots):
+        block = jnp.clip(named[k, tile] - first * held, 0, out_hbm.shape[0] * held - 1)
+        owner = lax.shift_right_logical(block, jnp.int32(held.bit_length() - 1))
+        rank = seen[owner]
+        source[0, k] = owner * CAP + jnp.minimum(rank, CAP - 1)
+        seen[owner] = rank + (k < count).astype(jnp.int32)
+    source[0, slots] = count
+    told = pltpu.make_async_copy(source, source_hbm, sems.at[7])
+    told.start()
     handed.wait()
     copies[2].wait()
     copies[3].wait()
@@ -70,6 +88,7 @@
     lax.fori_loop(0, holders, one_tile, 0)
     for t in range(out_hbm.shape[0]):
         pltpu.make_async_copy(staged.at[t], out_hbm.at[t], out_sems.at[t]).wait()
+    told.wait()
 
 
 def gather(block_list, block_count, block_scale, source_blocks):
@@ -78,9 +97,12 @@
     slots, tiles = block_list.shape
     return pl.pallas_call(
         gather_kernel,
-        out_shape=jax.ShapeDtypeStruct((holders, CAP, edge, edge), BF16),
+        out_shape=[
+            jax.ShapeDtypeStruct((holders, CAP, edge, edge), BF16),
+            jax.ShapeDtypeStruct((1, tiles), jnp.int32),
+        ],
         in_specs=[ANY] * 4,
-        out_specs=ANY,
+        out_specs=[ANY] * 2,
         scratch_shapes=[
             pltpu.VMEM((slots, tiles), jnp.int32),
             pltpu.VMEM((1, tiles), jnp.int32),
@@ -89,7 +111,11 @@
             pltpu.VMEM((8, tiles), jnp.int32),
             pltpu.SMEM((8, tiles), jnp.int32),
             pltpu.VMEM((holders, CAP, edge, edge), BF16),
-            pltpu.SemaphoreType.DMA((5,)),
+            pltpu.SMEM((slots, tiles), jnp.int32),
+            pltpu.SMEM((1, tiles), jnp.int32),
+            pltpu.SMEM((holders,), jnp.int32),
+            pltpu.SMEM((1, tiles), jnp.int32),
+            pltpu.SemaphoreType.DMA((8,)),
             pltpu.SemaphoreType.DMA((holders,)),
         ],
         compiler_params=pltpu.CompilerParams(vmem_limit_bytes=56 * MIB),
@@ -97,39 +123,22 @@
     )(block_list, block_count.reshape(1, tiles), block_scale, source_blocks)
 
 
-def find_sources(list_ref, count_ref, source, seen):
-    holders = lax.axis_size("gy")
-    first = lax.axis_index("gx") * holders
-    tile = first + lax.axis_index("gy")
-    held = 32
-    live = count_ref[tile]
-    for h in range(holders):
-        seen[h] = 0
-    for k in range(list_ref.shape[0]):
-        owner = (list_ref[k, tile] - first * held) // held
-        owner = jnp.clip(owner, 0, holders - 1)
-        rank = seen[owner]
-        source[k] = owner * CAP + jnp.minimum(rank, CAP - 1)
-        seen[owner] = rank + (k < live).astype(jnp.int32)
-    return live
-
-
-def window(k, live, source, arrived_ref, row_ref, col_ref):
-    part = dot(row_ref[k], arrived_ref[source[k]])
+def window(k, source_ref, arrived_ref, row_ref, col_ref):
+    live = source_ref[0, row_ref.shape[0]]
+    part = dot(row_ref[k], arrived_ref[source_ref[0, k]])
     part = jnp.where(k < live, part, 0.0).astype(BF16)
     return dot(part, col_ref[k])
 
 
 def edges_kernel(
-    list_ref, count_ref, arrived_ref, row_ref, col_ref, edge_ref, left_ref, right_ref, source, seen
+    source_ref, arrived_ref, row_ref, col_ref, edge_ref, left_ref, right_ref
 ):
     edge = row_ref.shape[1]
-    live = find_sources(list_ref, count_ref, source, seen)
     for i in range(W):
         for s in range(2):
             k = i * W + s * (W - 1)
             edge_ref[s, i * edge : (i + 1) * edge, :] = window(
-                k, live, source, arrived_ref, row_ref, col_ref
+                k, source_ref, arrived_ref, row_ref, col_ref
             )
     rows = edge_ref.shape[1]
     chunk = rows // 4
@@ -150,39 +159,34 @@
     right_ref[...] = right.astype(BF16)
 
 
-def edges(block_list, block_count, arrived, row_weights, col_weights):
-    slots, edge, _ = row_weights.shape
+def edges(source, arrived, row_weights, col_weights):
+    edge = row_weights.shape[1]
     side = W * edge
     shapes = [((2, side, edge), F32), ((side // 4, 128), BF16), ((side // 4, 128), BF16)]
     return pl.pallas_call(
         edges_kernel,
         out_shape=[jax.ShapeDtypeStruct(s, d) for s, d in shapes],
-        in_specs=[SMEM, SMEM, VMEM, VMEM, VMEM],
+        in_specs=[SMEM, VMEM, VMEM, VMEM],
         out_specs=[VMEM] * len(shapes),
-        scratch_shapes=[
-            pltpu.SMEM((slots,), jnp.int32),
-            pltpu.SMEM((lax.axis_size("gy"),), jnp.int32),
-        ],
         cost_estimate=cost(side * 256),
         compiler_params=pltpu.CompilerParams(vmem_limit_bytes=16 * MIB),
         name="edge_windows",
-    )(block_list, block_count, arrived, row_weights, col_weights)
+    )(source, arrived, row_weights, col_weights)
 
 
 def middle_kernel(
-    list_ref, count_ref, arrived_ref, row_ref, col_ref, edge_ref, down,
-    inner_ref, low_ref, high_ref, band_ref, fall_ref, source, seen,
+    source_ref, arrived_ref, row_ref, col_ref, edge_ref, down,
+    inner_ref, low_ref, high_ref, band_ref, fall_ref,
 ):
     edge = row_ref.shape[1]
     rows = band_ref.shape[0]
-    live = find_sources(list_ref, count_ref, source, seen)
     for s in range(2):
         band_ref[:, s * (W - 1) * edge : (s * (W - 1) + 1) * edge] = edge_ref[s].astype(BF16)
 
     for i in range(W):
         span = slice(i * edge, (i + 1) * edge)
         for j in range(1, W - 1):
-            value = window(i * W + j, live, source, arrived_ref, row_ref, col_ref)
+            value = window(i * W + j, source_ref, arrived_ref, row_ref, col_ref)
             inner_ref[j - 1, span, :] = value
             band_ref[span, j * edge : (j + 1) * edge] = value.astype(BF16)
     for i in range((rows - 2 * PAD) // STEP):
@@ -206,8 +210,8 @@
     lax.fori_loop(0, W, one_span, 0)
 
 
-def middle(block_list, block_count, arrived, row_weights, col_weights, edge_values):
-    slots, edge, _ = row_weights.shape
+def middle(source, arrived, row_weights, col_weights, edge_values):
+    edge = row_weights.shape[1]
     side = W * edge
     shapes = [
         ((W - 2, side, edge), F32),
@@ -219,16 +223,12 @@
     return pl.pallas_call(
         middle_kernel,
         out_shape=[jax.ShapeDtypeStruct(s, d) for s, d in shapes],
-        in_specs=[SMEM, SMEM] + [VMEM] * 5,
+        in_specs=[SMEM] + [VMEM] * 5,
         out_specs=[VMEM] * len(shapes),
-        scratch_shapes=[
-            pltpu.SMEM((slots,), jnp.int32),
-            pltpu.SMEM((lax.axis_size("gy"),), jnp.int32),
-        ],
         cost_estimate=cost(side * side),
         compiler_params=pltpu.CompilerParams(vmem_limit_bytes=24 * MIB),
         name="middle_windows",
-    )(block_list, block_count, arrived, row_weights, col_weights, edge_values, down_taps(STEP))
+    )(source, arrived, row_weights, col_weights, edge_values, down_taps(STEP))
 
 
 def tap(offset):
@@ -249,23 +249,24 @@
 
 
 def cells(mid, low, high):
-    centre = mid(0)
-    ul, uc, ur = low(-1), mid(-1), high(-1)
-    cl, cr = low(0), high(0)
-    dl, dc, dr = low(1), mid(1), high(1)
+    centre, cl, cr = [load(0).astype(BF16) for load in (mid, low, high)]
+    uc, ul, ur = [load(-1).astype(BF16) for load in (mid, low, high)]
+    dc, dl, dr = [load(1).astype(BF16) for load in (mid, low, high)]
     one = dr - ul
     two = ur - dl
-    grad_x = one + two + 2.0 * (cr - cl)
-    grad_y = one - two + 2.0 * (dc - uc)
-    square = 1.0 + (grad_x * grad_x + grad_y * grad_y) * (1.0 / 64.0)
+    across = cr - cl
+    along = dc - uc
+    grad_x = (one + two) + (across + across)
+    grad_y = (one - two) + (along + along)
+    steep = (grad_x * grad_x + grad_y * grad_y).astype(F32)
+    square = 1.0 + steep * (1.0 / 64.0)
     slope = square * lax.rsqrt(square)
     flows = []
-    own = centre.astype(BF16)
     for value, diagonal in (
         (ul, True), (uc, False), (ur, True), (cl, False),
         (cr, False), (dl, True), (dc, False), (dr, True),
     ):
-        drop = jnp.maximum(own - value.astype(BF16), 0)
+        drop = jnp.maximum(centre - value, 0)
         flows.append((drop * BF16(DIAG) if diagonal else drop) + BF16(FLAT))
     total = (
         ((flows[0] + flows[1]) + (flows[2] + flows[3]))
@@ -537,23 +538,28 @@
 
 def exchange(low, high, axis):
     devices = lax.axis_size(axis)
-    up = [(i, i + 1) for i in range(devices - 1)]
-    down = [(j, i) for i, j in up]
-    return lax.ppermute(high, axis, up), lax.ppermute(low, axis, down)
+    even = lax.rem(lax.axis_index(axis), 2) == 0
+    swaps = []
+    for start in range(2):
+        pairs = [(i, i + 1) for i in range(start, devices - 1, 2)]
+        swaps.append(pairs + [(j, i) for i, j in pairs])
+    first = lax.ppermute(jnp.where(even, high, low), axis, swaps[0])
+    second = lax.ppermute(jnp.where(even, low, high), axis, swaps[1])
+    return jnp.where(even, second, first), jnp.where(even, first, second)
 
 
 def local(source_blocks, block_scale, block_list, block_count, row_weights, col_weights):
     holders = lax.axis_size("gy")
     edge = source_blocks.shape[1]
     block_list = block_list.T
-    outgoing = gather(block_list, block_count, block_scale, source_blocks)
+    outgoing, source = gather(block_list, block_count, block_scale, source_blocks)
     arrived = lax.all_to_all(
         outgoing, "gy", split_axis=0, concat_axis=0, tiled=True
     ).reshape(holders * CAP, edge, edge)
     weights = (row_weights, col_weights)
-    edge_values, left, right = edges(block_list, block_count, arrived, *weights)
+    edge_values, left, right = edges(source, arrived, *weights)
     before, after = exchange(left, right, "gx")
-    inner, low, high, band, fall = middle(block_list, block_count, arrived, *weights, edge_values)
+    inner, low, high, band, fall = middle(source, arrived, *weights, edge_values)
     top = jnp.concatenate([band[:PAD], before[:PAD], after[:PAD]], axis=1)
     bottom = jnp.concatenate([band[-PAD:], before[-PAD:], after[-PAD:]], axis=1)
     above, below = exchange(top, bottom, "gy")

time: 67.2 us -> 63.4 us (0.943)
  blocking collectives: 33.1 us -> 0 us
  waiting for transfers between devices: 0.01 us -> 25 us
  starting transfers between devices: 14.9 us -> 19.8 us
  Pallas kernels: 17.5 us -> 16.1 us
  local copies, waits for them, and re-layouts: 0.06 us -> 1.32 us
    all_to_all x1 -> x0, blocking collectives: 33.1 us -> none  [local(): lax.all_to_all(outgoing, 'gy', split_axis=0, concat_axis=0, tiled=True)]
    all_to_all x0 -> x1, waiting for transfers between devices: none -> 25 us  [local(): lax.all_to_all(outgoing, 'gy', split_axis=0, concat_axis=0, tiled=True)]
    all_to_all x0 -> x1, starting transfers between devices: none -> 7.91 us  [local(): lax.all_to_all(outgoing, 'gy', split_axis=0, concat_axis=0, tiled=True)]
    ppermute x4, starting transfers between devices: 14.9 us -> 11.9 us  [the longest x2 8.07 us: exchange(): second = lax.ppermute(jnp.where(even, low, high), axis, swaps[1])]
    unnamed x14, local copies, waits for them, and re-layouts: 0.04 us -> 1.31 us
  transfers between devices with their start and end apart: 4 -> 5, of which waited for: 0 -> 1; matrix products, arithmetic and copies ran while one was open for 0% -> 0% of each run, Pallas kernels for 17% -> 16%
where the time goes in v3:
time: 63.4 us; the launch traced here: 63.2 us
  waiting for transfers between devices  25 us (39%)
  starting transfers between devices  19.8 us (31%)
  Pallas kernels  16.1 us (25%)
  local copies, waits for them, and re-layouts  1.32 us (2%)
  between operations  0.83 us (1%)
    all_to_all x1, waiting for transfers between devices, local(): lax.all_to_all(outgoing, 'gy', split_axis=0, concat_axis=0, tiled=True)  25 us
    ppermute x2, starting transfers between devices, exchange(): second = lax.ppermute(jnp.where(even, low, high), axis, swaps[1])  8.07 us
    all_to_all x1, starting transfers between devices, local(): lax.all_to_all(outgoing, 'gy', split_axis=0, concat_axis=0, tiled=True)  7.91 us
    pallas_call x1, Pallas kernels, main(): pl.pallas_call(main_kernel, out_shape=out_shapes(rows, cols), in_specs=[V...  7.27 us
    ppermute x2, starting transfers between devices, exchange(): first = lax.ppermute(jnp.where(even, high, low), axis, swaps[0])  3.87 us
    pallas_call x1, Pallas kernels, middle(): pl.pallas_call(middle_kernel, out_shape=[jax.ShapeDtypeStruct(s, d) for s...  3.14 us
    pallas_call x1, Pallas kernels, gather(): pl.pallas_call(gather_kernel, out_shape=[jax.ShapeDtypeStruct((holders, C...  2.92 us
    pallas_call x1, Pallas kernels, ends(): pl.pallas_call(ends_kernel, out_shape=out_shapes(rows, cols), in_specs=[V...  1.76 us
  transfers between devices with their start and end apart: 5, of which 1 were waited for; matrix products, arithmetic and copies ran while one was open for 0% of the time, Pallas kernels for 16%

profile of v3, /device:TPU:11, one launch (start us, length us, event | category | flops | bytes accessed | tf_op | source)
XLA Modules:
  0.0 63.2 jit_solution(13404540410577814395)
XLA Ops:
  0.6 2.9 %gather_blocks.1 = (bf16[16,4,128,128]{3,2,1,0:T(8,128)(2,1)}, s32[1,128]{1,0:T(1,128)}) custom-call(s32[36,128]{1,0:T(8,128)} %bitcast.5, s32[1,128]{1,0:T(1,128)} %bitcast.6, f32[32]{0:T(128)} %scale_hbm.1, bf16[32,128,128]{2,1,0:T(8,128)(2,1)} %blocks_hbm.1), custom_call_target="tpu_custom_call" | custom-call | tf_op jit(solution)/shard_map/gather_blocks/pallas_call | solution.py:98
  3.6 0.0 copy-start
  3.6 0.0 copy-start.6
  3.6 0.0 copy-start.4
  3.6 7.9 %all-to-all-start = ((bf16[16,4,128,128]{3,2,1,0:T(8,128)(2,1)}), bf16[16,4,128,128]{3,2,1,0:T(8,128)(2,1)S(1)}, u32[]{:S(2)}, u32[]{:S(2)}) async-start(bf16[16,4,128,128]{3,2,1,0:T(8,128)(2,1)} %get-tuple-element.17), calls=%async_computation | async-start | bytes 4194304 | tf_op jit(solution)/shard_map/all_to_all | solution.py:556
  11.5 25.0 %all-to-all-done = bf16[16,4,128,128]{3,2,1,0:T(8,128)(2,1)S(1)} async-done(((bf16[16,4,128,128]{3,2,1,0:T(8,128)(2,1)}), bf16[16,4,128,128]{3,2,1,0:T(8,128)(2,1)S(1)}, u32[]{:S(2)}, u32[]{:S(2)}) %all-to-all-start) | async-done | bytes 2097184 | tf_op jit(solution)/shard_map/all_to_all | solution.py:556
  36.5 0.0 copy-done
  36.5 0.0 copy-done.6
  36.5 0.0 copy-start.1
  36.5 1.3 %copy-done.1 = bf16[36,128,128]{2,1,0:T(8,128)(2,1)S(1)} copy-done((bf16[36,128,128]{2,1,0:T(8,128)(2,1)S(1)}, bf16[36,128,128]{2,1,0:T(8,128)(2,1)}, u32[]{:S(2)}) %copy-start.1) | copy-done | bytes 1179672
  37.8 0.0 copy-start.2
  37.8 1.1 %edge_windows.1 = (f32[2,768,128]{2,1,0:T(8,128)S(1)}, bf16[192,128]{1,0:T(8,128)(2,1)S(1)}, bf16[192,128]{1,0:T(8,128)(2,1)S(1)}) custom-call(s32[1,128]{1,0:T(1,128)S(1)} %copy-done.6, bf16[64,128,128]{2,1,0:T(8,128)(2,1)S(1)} %bitcast.3, bf16[36,128,128]{2,1,0:T(8,128)(2,1)S(1)} %copy-done, bf16[36,128,128]{2,1,0:T(8,128)(2,1)S(1)} %copy-done.1), custom_call_target="tpu_custom_call" | custom-call | flops 786432000 | bytes 4718592 | tf_op jit(solution)/shard_map/edge_windows/pallas_call | solution.py:166
  38.8 3.5 %collective-permute-start.1 = (bf16[192,128]{1,0:T(8,128)(2,1)S(1)}, bf16[192,128]{1,0:T(8,128)(2,1)S(1)}, u32[]{:S(2)}, u32[]{:S(2)}) collective-permute-start(bf16[192,128]{1,0:T(8,128)(2,1)S(1)} %get-tuple-element.37), channel_id=1, source_target_pairs={{0,16},{32,48},{64,80},{96,112},{16,0},{48,32},{80,64},{112,96},{1... | collective-permute-start | bytes 147464 | tf_op jit(solution)/shard_map/ppermute | solution.py:546
  42.3 3.1 %collective-permute-start = (bf16[192,128]{1,0:T(8,128)(2,1)S(1)}, bf16[192,128]{1,0:T(8,128)(2,1)S(1)}, u32[]{:S(2)}, u32[]{:S(2)}) collective-permute-start(bf16[192,128]{1,0:T(8,128)(2,1)S(1)} %get-tuple-element.38), channel_id=1, source_target_pairs={{16,32},{48,64},{80,96},{32,16},{64,48},{96,80},{17,33},{49,65},{8... | collective-permute-start | bytes 147464 | tf_op jit(solution)/shard_map/ppermute | solution.py:547
  45.4 0.0 copy-done.4
  45.5 0.0 copy-done.2
  45.5 0.0 copy-start.3
  45.5 3.1 %middle_windows.1 = (f32[4,768,128]{2,1,0:T(8,128)S(1)}, f32[6,768,128]{2,1,0:T(8,128)S(1)}, f32[6,768,128]{2,1,0:T(8,128)S(1)}, bf16[768,768]{1,0:T(8,128)(2,1)S(1)}, bf16[704,768]{1,0:T(8,128)(2,1)S(1)}) custom-call(s32[1,128]{1,0:T(1,128)S(1)} %copy-done.6, bf16[64,128,128]{2,1,0:T(8,128)(2,1)S(1)} %bitcast.4, bf16[36,128,128]{2,1,0:T(8,128)(2,1)S(1)} %copy-done, ...), custom_call_target="tpu_custom_call" | custom-call | flops 2359296000 | bytes 14155776 | tf_op jit(solution)/shard_map/middle_windows/pallas_call | solution.py:223
  48.6 0.0 collective-permute-done.1
  48.6 0.0 collective-permute-done
  48.7 0.4 collective-permute-start.3
  49.1 5.0 %collective-permute-start.2 = (bf16[32,1024]{1,0:T(8,128)(2,1)S(1)}, bf16[32,1024]{1,0:T(8,128)(2,1)S(1)}, u32[]{:S(2)}, u32[]{:S(2)}) collective-permute-start(bf16[32,1024]{1,0:T(8,128)(2,1)S(1)} %get-tuple-element.34), channel_id=1, source_target_pairs={{1,2},{3,4},{5,6},{7,8},{9,10},{11,12},{13,14},{2,1},{4,3},{6,5},{... | collective-permute-start | bytes 196616 | tf_op jit(solution)/shard_map/ppermute | solution.py:547
  54.1 0.0 copy-done.3
  54.1 0.0 copy-start.5
  54.1 7.3 %main_cells.1 = (f32[768,768]{1,0:T(8,128)}, f32[768,768]{1,0:T(8,128)}, bf16[8,768,768]{2,1,0:T(8,128)(2,1)}) custom-call(f32[2,768,128]{2,1,0:T(8,128)S(1)} %get-tuple-element.18.edge_ref, f32[4,768,128]{2,1,0:T(8,128)S(1)} %get-tuple-element.19.inner_ref, f32[6,768,128]{2,1,0:T(8,128)S(1)} %get-tuple-element.23.low_ref, ...), custom_call_target="tpu_custom_call" | custom-call | flops 2162688000 | bytes 12976128 | tf_op jit(solution)/shard_map/main_cells/pallas_call | solution.py:379
  61.4 0.0 collective-permute-done.3
  61.4 0.0 collective-permute-done.2
  61.4 0.0 copy-done.5
  61.4 1.8 %end_cells.1 = (f32[768,768]{1,0:T(8,128)}, f32[768,768]{1,0:T(8,128)}, bf16[8,768,768]{2,1,0:T(8,128)(2,1)}) custom-call(f32[2,768,128]{2,1,0:T(8,128)S(1)} %get-tuple-element.18.edge_ref, f32[4,768,128]{2,1,0:T(8,128)S(1)} %get-tuple-element.19.inner_ref, ...), custom_call_target="tpu_custom_call", output_to_operand_aliasing={{0}: (9, {}), {1}: (10, {}), {2}: (11, {})} | custom-call | flops 196608000 | bytes 1179648 | tf_op jit(solution)/shard_map/end_cells/pallas_call | solution.py:514
  (6 shorter events, 0.1 us)
Async XLA Ops:
  3.6 32.9 %copy-start = (bf16[36,128,128]{2,1,0:T(8,128)(2,1)S(1)}, bf16[36,128,128]{2,1,0:T(8,128)(2,1)}, u32[]{:S(2)}) copy-start(bf16[36,128,128]{2,1,0:T(8,128)(2,1)} %row_ref.3) | copy-start | bytes 3538948
  3.6 32.9 %copy-start.6 = (s32[1,128]{1,0:T(1,128)S(1)}, s32[1,128]{1,0:T(1,128)}, u32[]{:S(2)}) copy-start(s32[1,128]{1,0:T(1,128)} %get-tuple-element.16.source_ref) | copy-start | bytes 1540
  3.6 41.9 %copy-start.4 = (bf16[176,240]{1,0:T(8,128)(2,1)S(1)}, bf16[176,240]{1,0:T(8,128)(2,1)}, u32[]{:S(2)}) copy-start(bf16[176,240]{1,0:T(8,128)(2,1)} %constant.23.clone.down) | copy-start | bytes 253444
  3.6 32.9 %all-to-all-start = ((bf16[16,4,128,128]{3,2,1,0:T(8,128)(2,1)}), bf16[16,4,128,128]{3,2,1,0:T(8,128)(2,1)S(1)}, u32[]{:S(2)}, u32[]{:S(2)}) async-start(bf16[16,4,128,128]{3,2,1,0:T(8,128)(2,1)} %get-tuple-element.17), calls=%async_computation | async-start | bytes 4194304 | tf_op jit(solution)/shard_map/all_to_all | solution.py:556
  36.5 1.3 %copy-start.1 = (bf16[36,128,128]{2,1,0:T(8,128)(2,1)S(1)}, bf16[36,128,128]{2,1,0:T(8,128)(2,1)}, u32[]{:S(2)}) copy-start(bf16[36,128,128]{2,1,0:T(8,128)(2,1)} %col_ref.3) | copy-start | bytes 3538948
  37.8 7.7 %copy-start.2 = (bf16[36,128,128]{2,1,0:T(8,128)(2,1)S(1)}, bf16[36,128,128]{2,1,0:T(8,128)(2,1)}, u32[]{:S(2)}) copy-start(bf16[36,128,128]{2,1,0:T(8,128)(2,1)} %col_ref.3) | copy-start | bytes 3538948
  38.8 9.8 %collective-permute-start.1 = (bf16[192,128]{1,0:T(8,128)(2,1)S(1)}, bf16[192,128]{1,0:T(8,128)(2,1)S(1)}, u32[]{:S(2)}, u32[]{:S(2)}) collective-permute-start(bf16[192,128]{1,0:T(8,128)(2,1)S(1)} %get-tuple-element.37), channel_id=1, source_target_pairs={{0,16},{32,48},{64,80},{96,112},{16,0},{48,32},{80,64},{112,96},{1... | collective-permute-start | bytes 147464 | tf_op jit(solution)/shard_map/ppermute | solution.py:546
  42.3 6.3 %collective-permute-start = (bf16[192,128]{1,0:T(8,128)(2,1)S(1)}, bf16[192,128]{1,0:T(8,128)(2,1)S(1)}, u32[]{:S(2)}, u32[]{:S(2)}) collective-permute-start(bf16[192,128]{1,0:T(8,128)(2,1)S(1)} %get-tuple-element.38), channel_id=1, source_target_pairs={{16,32},{48,64},{80,96},{32,16},{64,48},{96,80},{17,33},{49,65},{8... | collective-permute-start | bytes 147464 | tf_op jit(solution)/shard_map/ppermute | solution.py:547
  45.5 8.6 %copy-start.3 = (bf16[512,256]{1,0:T(8,128)(2,1)S(1)}, bf16[512,256]{1,0:T(8,128)(2,1)}, u32[]{:S(2)}) copy-start(bf16[512,256]{1,0:T(8,128)(2,1)} %constant.24.clone.across) | copy-start | bytes 786436
  48.7 12.6 %collective-permute-start.3 = (bf16[32,1024]{1,0:T(8,128)(2,1)S(1)}, bf16[32,1024]{1,0:T(8,128)(2,1)S(1)}, u32[]{:S(2)}, u32[]{:S(2)}) collective-permute-start(bf16[32,1024]{1,0:T(8,128)(2,1)S(1)} %get-tuple-element.33), channel_id=1, source_target_pairs={{0,1},{2,3},{4,5},{6,7},{8,9},{10,11},{12,13},{14,15},{1,0},{3,2},... | collective-permute-start | bytes 196616 | tf_op jit(solution)/shard_map/ppermute | solution.py:546
  49.1 12.3 %collective-permute-start.2 = (bf16[32,1024]{1,0:T(8,128)(2,1)S(1)}, bf16[32,1024]{1,0:T(8,128)(2,1)S(1)}, u32[]{:S(2)}, u32[]{:S(2)}) collective-permute-start(bf16[32,1024]{1,0:T(8,128)(2,1)S(1)} %get-tuple-element.34), channel_id=1, source_target_pairs={{1,2},{3,4},{5,6},{7,8},{9,10},{11,12},{13,14},{2,1},{4,3},{6,5},{... | collective-permute-start | bytes 196616 | tf_op jit(solution)/shard_map/ppermute | solution.py:547
  54.1 7.3 %copy-start.5 = (bf16[32,96]{1,0:T(8,128)(2,1)S(1)}, bf16[32,96]{1,0:T(8,128)(2,1)}, u32[]{:S(2)}) copy-start(bf16[32,96]{1,0:T(8,128)(2,1)} %constant.25.clone.down) | copy-start | bytes 18436

commit v4 on v3

--- a/solution.py
+++ b/solution.py
@@ -123,6 +123,16 @@
     )(block_list, block_count.reshape(1, tiles), block_scale, source_blocks)
 
 
+def is_even(axis):
+    return lax.rem(lax.axis_index(axis), 2) == 0
+
+
+def before_and_after(first, second, axis):
+    even = is_even(axis)
+    first, second = first.astype(F32), second.astype(F32)
+    return jnp.where(even, second, first), jnp.where(even, first, second)
+
+
 def window(k, source_ref, arrived_ref, row_ref, col_ref):
     live = source_ref[0, row_ref.shape[0]]
     part = dot(row_ref[k], arrived_ref[source_ref[0, k]])
@@ -131,7 +141,7 @@
 
 
 def edges_kernel(
-    source_ref, arrived_ref, row_ref, col_ref, edge_ref, left_ref, right_ref
+    source_ref, arrived_ref, row_ref, col_ref, edge_ref, first_ref, second_ref
 ):
     edge = row_ref.shape[1]
     for i in range(W):
@@ -155,8 +165,9 @@
         if q != 3:
             part = pltpu.roll(part, PAD * (q + 1), 1)
         right = jnp.where(mine, part, right)
-    left_ref[...] = left.astype(BF16)
-    right_ref[...] = right.astype(BF16)
+    even = is_even("gx")
+    first_ref[...] = jnp.where(even, right, left).astype(BF16)
+    second_ref[...] = jnp.where(even, left, right).astype(BF16)
 
 
 def edges(source, arrived, row_weights, col_weights):
@@ -176,10 +187,12 @@
 
 def middle_kernel(
     source_ref, arrived_ref, row_ref, col_ref, edge_ref, down,
-    inner_ref, low_ref, high_ref, band_ref, fall_ref,
+    inner_ref, low_ref, high_ref, band_ref, fall_ref, strips_ref, odd_ref,
 ):
     edge = row_ref.shape[1]
     rows = band_ref.shape[0]
+    odd = lax.rem(lax.axis_index("gy"), 2)
+    odd_ref[...] = jnp.full(odd_ref.shape, odd, jnp.int32)
     for s in range(2):
         band_ref[:, s * (W - 1) * edge : (s * (W - 1) + 1) * edge] = edge_ref[s].astype(BF16)
 
@@ -189,6 +202,9 @@
             value = window(i * W + j, source_ref, arrived_ref, row_ref, col_ref)
             inner_ref[j - 1, span, :] = value
             band_ref[span, j * edge : (j + 1) * edge] = value.astype(BF16)
+    for n in range(2):
+        at = pl.multiple_of(jnp.where(odd == n, rows - PAD, 0), PAD)
+        strips_ref[n] = band_ref[pl.ds(at, PAD), :]
     for i in range((rows - 2 * PAD) // STEP):
         value = dot(down[...], band_ref[i * STEP : (i + 1) * STEP + 2 * PAD, :])
         fall_ref[i * STEP : (i + 1) * STEP, :] = value.astype(BF16)
@@ -219,6 +235,8 @@
         ((W, side, edge), F32),
         ((side, side), BF16),
         ((side - 2 * PAD, side), BF16),
+        ((2, PAD, side), BF16),
+        ((8, 128), jnp.int32),
     ]
     return pl.pallas_call(
         middle_kernel,
@@ -291,7 +309,7 @@
 
 
 def main_kernel(
-    edge_ref, inner_ref, low_ref, high_ref, fall_ref, left_ref, right_ref, across, down,
+    edge_ref, inner_ref, low_ref, high_ref, fall_ref, first_ref, second_ref, across, down,
     relief_hbm, slope_hbm, flow_hbm, relief, slope, flow, far, patched, sems,
 ):
     rows, cols = low_ref.shape[1], relief.shape[1]
@@ -300,12 +318,13 @@
     chunk = rows // 4
     inverse = 1.0 / (tap_total() ** 2)
     lane = lax.broadcasted_iota(jnp.int32, (chunk, 128), 1)
+    left, right = before_and_after(first_ref[...], second_ref[...], "gx")
     for q in range(4):
         span = slice(q * chunk, (q + 1) * chunk)
-        value = unpack_left(left_ref[...], q)
+        value = unpack_left(left, q)
         far[0, span, :] = value.astype(BF16)
         patched[0, span, :] = jnp.where(lane == 0, pltpu.roll(value, 1, 1), low_ref[0, span, :])
-        value = unpack_right(right_ref[...], q)
+        value = unpack_right(right, q)
         far[1, span, :] = value.astype(BF16)
         patched[1, span, :] = jnp.where(
             lane == 127, pltpu.roll(value, 127, 1), high_ref[lanes - 1, span, :]
@@ -410,17 +429,15 @@
 
 
 def unpack_left(value, q):
-    value = value.astype(F32)
     return value if q == 3 else pltpu.roll(value, 96 - PAD * q, 1)
 
 
 def unpack_right(value, q):
-    value = value.astype(F32)
     return value if q == 0 else pltpu.roll(value, 128 - PAD * q, 1)
 
 
 def ends_kernel(
-    edge_ref, inner_ref, band_ref, left_ref, right_ref, up_ref, down_ref, across, down,
+    edge_ref, inner_ref, band_ref, first_ref, second_ref, near_ref, next_ref, across, down,
     relief_in, slope_in, flow_in, relief_hbm, slope_hbm, flow_hbm,
     relief, slope, flow, wide, band, low_ref, high_ref, sems,
 ):
@@ -429,20 +446,25 @@
     near = 2 * PAD
     tall = PAD + 16
     inverse = 1.0 / (tap_total() ** 2)
-    packed = left_ref.shape[0]
+    packed = first_ref.shape[0]
+    others = before_and_after(near_ref[...], next_ref[...], "gy")
     for e in range(2):
         here = slice(PAD, PAD + near) if e == 0 else slice(0, near)
         there = slice(0, PAD) if e == 0 else slice(near, near + PAD)
-        other = down_ref if e else up_ref
+        other = others[e]
         top = e * tall
         own_rows = slice(rows - near, rows) if e else slice(0, near)
         pack_rows = slice(packed - near, packed) if e else slice(0, near)
         band[e, here, 128 : 128 + cols] = band_ref[own_rows, :]
-        band[e, there, 128 : 128 + cols] = other[:, 0:cols]
-        far_left = unpack_left(left_ref[pack_rows, :], 3 * e)
-        far_right = unpack_right(right_ref[pack_rows, :], 3 * e)
-        corner_left = unpack_left(other[:, cols : cols + 128], 0 if e else 3)
-        corner_right = unpack_right(other[:, cols + 128 : cols + 256], 0 if e else 3)
+        band[e, there, 128 : 128 + cols] = other[:, 0:cols].astype(BF16)
+        left, right = before_and_after(first_ref[pack_rows, :], second_ref[pack_rows, :], "gx")
+        far_left = unpack_left(left, 3 * e)
+        far_right = unpack_right(right, 3 * e)
+        left, right = before_and_after(
+            other[:, cols : cols + 128], other[:, cols + 128 : cols + 256], "gx"
+        )
+        corner_left = unpack_left(left, 0 if e else 3)
+        corner_right = unpack_right(right, 0 if e else 3)
         band[e, here, 0:128] = far_left.astype(BF16)
         band[e, there, 0:128] = corner_left.astype(BF16)
         band[e, here, 128 + cols :] = far_right.astype(BF16)
@@ -458,7 +480,7 @@
             wide[lanes + 1, top : top + 40, :] = far_right[near - 40 : near]
             wide[lanes + 1, top + 40 : top + 48, :] = corner_right[0:8]
         for j in range(lanes):
-            part = other[:, j * 128 : (j + 1) * 128].astype(F32)
+            part = other[:, j * 128 : (j + 1) * 128]
             own = edge_ref.at[int(j > 0)] if j in (0, lanes - 1) else inner_ref.at[j - 1]
             if e == 0:
                 wide[j + 1, top : top + 8, :] = part[PAD - 8 : PAD]
@@ -536,35 +558,32 @@
     )
 
 
-def exchange(low, high, axis):
+def swap(first, second, axis):
     devices = lax.axis_size(axis)
-    even = lax.rem(lax.axis_index(axis), 2) == 0
-    swaps = []
-    for start in range(2):
+    received = []
+    for start, value in enumerate((first, second)):
         pairs = [(i, i + 1) for i in range(start, devices - 1, 2)]
-        swaps.append(pairs + [(j, i) for i, j in pairs])
-    first = lax.ppermute(jnp.where(even, high, low), axis, swaps[0])
-    second = lax.ppermute(jnp.where(even, low, high), axis, swaps[1])
-    return jnp.where(even, second, first), jnp.where(even, first, second)
+        received.append(lax.ppermute(value, axis, pairs + [(j, i) for i, j in pairs]))
+    return received
 
 
 def local(source_blocks, block_scale, block_list, block_count, row_weights, col_weights):
-    holders = lax.axis_size("gy")
-    edge = source_blocks.shape[1]
     block_list = block_list.T
     outgoing, source = gather(block_list, block_count, block_scale, source_blocks)
-    arrived = lax.all_to_all(
-        outgoing, "gy", split_axis=0, concat_axis=0, tiled=True
-    ).reshape(holders * CAP, edge, edge)
+    edge = source_blocks.shape[1]
+    arrived = lax.all_to_all(outgoing, "gy", split_axis=0, concat_axis=0, tiled=True)
+    arrived = arrived.reshape(-1, edge, edge)
     weights = (row_weights, col_weights)
-    edge_values, left, right = edges(source, arrived, *weights)
-    before, after = exchange(left, right, "gx")
-    inner, low, high, band, fall = middle(source, arrived, *weights, edge_values)
-    top = jnp.concatenate([band[:PAD], before[:PAD], after[:PAD]], axis=1)
-    bottom = jnp.concatenate([band[-PAD:], before[-PAD:], after[-PAD:]], axis=1)
-    above, below = exchange(top, bottom, "gy")
-    outs = main(edge_values, inner, low, high, fall, before, after)
-    return tuple(ends(edge_values, inner, band, before, after, above, below, outs))
+    edge_values, *messages = edges(source, arrived, *weights)
+    beside = swap(*messages, "gx")
+    inner, low, high, band, fall, strips, odd = middle(source, arrived, *weights, edge_values)
+    messages = []
+    for n in range(2):
+        corners = [jnp.where(odd[:1] == n, side[-PAD:], side[:PAD]) for side in beside]
+        messages.append(jnp.concatenate([strips[n], *corners], axis=1))
+    ahead = swap(*messages, "gy")
+    outs = main(edge_values, inner, low, high, fall, *beside)
+    return tuple(ends(edge_values, inner, band, *beside, *ahead, outs))
 
 
 def solution(mesh):

time: 63.4 us -> 60.8 us (0.959)
  blocking collectives: 0 us -> 33.1 us
  waiting for transfers between devices: 25 us -> 0.01 us
  starting transfers between devices: 19.8 us -> 10.4 us
  local copies, waits for them, and re-layouts: 1.32 us -> 0.05 us
    all_to_all x0 -> x1, blocking collectives: none -> 33.1 us  [local(): lax.all_to_all(outgoing, 'gy', split_axis=0, concat_axis=0, tiled=True)]
    all_to_all x1 -> x0, waiting for transfers between devices: 25 us -> none  [local(): lax.all_to_all(outgoing, 'gy', split_axis=0, concat_axis=0, tiled=True)]
    all_to_all x1 -> x0, starting transfers between devices: 7.91 us -> none  [local(): lax.all_to_all(outgoing, 'gy', split_axis=0, concat_axis=0, tiled=True)]
    ppermute x4, starting transfers between devices: 11.9 us -> 10.4 us  [swap(): lax.ppermute(value, axis, pairs + [(j, i) for i, j in pairs])]
    unnamed x14 -> x12, local copies, waits for them, and re-layouts: 1.31 us -> 0.04 us
  transfers between devices with their start and end apart: 5 -> 4, of which waited for: 1 -> 0; matrix products, arithmetic and copies ran while one was open for 0% -> 0% of each run, Pallas kernels for 16% -> 17%
where the time goes in v4:
time: 60.8 us; the launch traced here: 60.6 us
  blocking collectives  33.1 us (54%)
  Pallas kernels  16.1 us (26%)
  starting transfers between devices  10.4 us (17%)
  between operations  0.81 us (1%)
    all_to_all x1, blocking collectives, local(): lax.all_to_all(outgoing, 'gy', split_axis=0, concat_axis=0, tiled=True)  33.1 us
    ppermute x4, starting transfers between devices, swap(): lax.ppermute(value, axis, pairs + [(j, i) for i, j in pairs])  10.4 us
    pallas_call x1, Pallas kernels, main(): pl.pallas_call(main_kernel, out_shape=out_shapes(rows, cols), in_specs=[V...  7.23 us
    pallas_call x1, Pallas kernels, middle(): pl.pallas_call(middle_kernel, out_shape=[jax.ShapeDtypeStruct(s, d) for s...  3.15 us
    pallas_call x1, Pallas kernels, gather(): pl.pallas_call(gather_kernel, out_shape=[jax.ShapeDtypeStruct((holders, C...  2.92 us
    pallas_call x1, Pallas kernels, ends(): pl.pallas_call(ends_kernel, out_shape=out_shapes(rows, cols), in_specs=[V...  1.79 us
  transfers between devices with their start and end apart: 4, of which 0 were waited for; matrix products, arithmetic and copies ran while one was open for 0% of the time, Pallas kernels for 17%

profile of v4, /device:TPU:11, one launch (start us, length us, event | category | flops | bytes accessed | tf_op | source)
XLA Modules:
  0.0 60.6 jit_solution(6896036139269024362)
XLA Ops:
  0.6 2.9 %gather_blocks.1 = (bf16[16,4,128,128]{3,2,1,0:T(8,128)(2,1)}, s32[1,128]{1,0:T(1,128)}) custom-call(s32[36,128]{1,0:T(8,128)} %bitcast.13, s32[1,128]{1,0:T(1,128)} %bitcast.14, f32[32]{0:T(128)} %scale_hbm.1, bf16[32,128,128]{2,1,0:T(8,128)(2,1)} %blocks_hbm.1), custom_call_target="tpu_custom_call" | custom-call | tf_op jit(solution)/shard_map/gather_blocks/pallas_call | solution.py:98
  3.6 0.0 copy-start
  3.6 0.0 copy-start.1
  3.6 0.0 copy-start.5
  3.6 33.1 %all_to_all.5 = bf16[16,4,128,128]{3,2,1,0:T(8,128)(2,1)S(1)} all-to-all(bf16[16,4,128,128]{3,2,1,0:T(8,128)(2,1)} %get-tuple-element.19), channel_id=1, replica_groups=mesh['gx'=8,'gy'=16] {'gy'}, dimensions={0} | all-to-all | bytes 4194304 | tf_op jit(solution)/shard_map/all_to_all | solution.py:574
  36.7 0.0 copy-start.3
  36.7 0.0 copy-done
  36.7 0.0 copy-done.1
  36.7 0.0 copy-done.5
  36.7 1.1 %edge_windows.1 = (f32[2,768,128]{2,1,0:T(8,128)S(1)}, bf16[192,128]{1,0:T(8,128)(2,1)S(1)}, bf16[192,128]{1,0:T(8,128)(2,1)S(1)}) custom-call(s32[1,128]{1,0:T(1,128)S(1)} %copy-done.5, bf16[64,128,128]{2,1,0:T(8,128)(2,1)S(1)} %bitcast.11, bf16[36,128,128]{2,1,0:T(8,128)(2,1)S(1)} %copy-done, bf16[36,128,128]{2,1,0:T(8,128)(2,1)S(1)} %copy-done.1), custom_call_target="tpu_custom_call" | custom-call | flops 786432000 | bytes 4718592 | tf_op jit(solution)/shard_map/edge_windows/pallas_call | solution.py:177
  37.8 2.6 %collective-permute-start = (bf16[192,128]{1,0:T(8,128)(2,1)S(1)}, bf16[192,128]{1,0:T(8,128)(2,1)S(1)}, u32[]{:S(2)}, u32[]{:S(2)}) collective-permute-start(bf16[192,128]{1,0:T(8,128)(2,1)S(1)} %get-tuple-element.23), channel_id=1, source_target_pairs={{0,16},{32,48},{64,80},{96,112},{16,0},{48,32},{80,64},{112,96},{1... | collective-permute-start | bytes 147464 | tf_op jit(solution)/shard_map/ppermute | solution.py:566
  40.4 3.1 %collective-permute-start.1 = (bf16[192,128]{1,0:T(8,128)(2,1)S(1)}, bf16[192,128]{1,0:T(8,128)(2,1)S(1)}, u32[]{:S(2)}, u32[]{:S(2)}) collective-permute-start(bf16[192,128]{1,0:T(8,128)(2,1)S(1)} %get-tuple-element.24), channel_id=1, source_target_pairs={{16,32},{48,64},{80,96},{32,16},{64,48},{96,80},{17,33},{49,65},{8... | collective-permute-start | bytes 147464 | tf_op jit(solution)/shard_map/ppermute | solution.py:566
  43.5 0.0 copy-done.3
  43.5 0.0 copy-start.2
  43.5 3.1 %middle_windows.1 = (f32[4,768,128]{2,1,0:T(8,128)S(1)}, f32[6,768,128]{2,1,0:T(8,128)S(1)}, f32[6,768,128]{2,1,0:T(8,128)S(1)}, bf16[768,768]{1,0:T(8,128)(2,1)...) custom-call(s32[1,128]{1,0:T(1,128)S(1)} %copy-done.5, ...), custom_call_target="tpu_custom_call" | custom-call | flops 2359296000 | bytes 14155776 | tf_op jit(solution)/shard_map/middle_windows/pallas_call | solution.py:241
  46.7 0.0 collective-permute-done.first_ref
  46.7 0.0 collective-permute-done.1.second_ref
  46.8 0.2 collective-permute-start.2
  46.9 4.6 %collective-permute-start.3 = (bf16[32,1024]{1,0:T(8,128)(2,1)S(1)}, bf16[32,1024]{1,0:T(8,128)(2,1)S(1)}, u32[]{:S(2)}, u32[]{:S(2)}) collective-permute-start(bf16[32,1024]{1,0:T(8,128)(2,1)S(1)} %pad_maximum_fusion.1), channel_id=1, source_target_pairs={{1,2},{3,4},{5,6},{7,8},{9,10},{11,12},{13,14},{2,1},{4,3},{6,5},{... | collective-permute-start | bytes 196616 | tf_op jit(solution)/shard_map/ppermute | solution.py:566
  51.5 0.0 copy-done.2
  51.5 0.0 copy-start.4
  51.5 7.2 %main_cells.1 = (f32[768,768]{1,0:T(8,128)}, f32[768,768]{1,0:T(8,128)}, bf16[8,768,768]{2,1,0:T(8,128)(2,1)}) custom-call(f32[2,768,128]{2,1,0:T(8,128)S(1)} %get-tuple-element.20.edge_ref, f32[4,768,128]{2,1,0:T(8,128)S(1)} %get-tuple-element.21.inner_ref, f32[6,768,128]{2,1,0:T(8,128)S(1)} %get-tuple-element.27.low_ref, ...), custom_call_target="tpu_custom_call" | custom-call | flops 2162688000 | bytes 12976128 | tf_op jit(solution)/shard_map/main_cells/pallas_call | solution.py:398
  58.8 0.0 collective-permute-done.2.near_ref
  58.8 0.0 collective-permute-done.3.next_ref
  58.8 0.0 copy-done.4
  58.8 1.8 %end_cells.1 = (f32[768,768]{1,0:T(8,128)}, f32[768,768]{1,0:T(8,128)}, bf16[8,768,768]{2,1,0:T(8,128)(2,1)}) custom-call(f32[2,768,128]{2,1,0:T(8,128)S(1)} %get-tuple-element.20.edge_ref, f32[4,768,128]{2,1,0:T(8,128)S(1)} %get-tuple-element.21.inner_ref, ...), custom_call_target="tpu_custom_call", output_to_operand_aliasing={{0}: (9, {}), {1}: (10, {}), {2}: (11, {})} | custom-call | flops 196608000 | bytes 1179648 | tf_op jit(solution)/shard_map/end_cells/pallas_call | solution.py:536
  (5 shorter events, 0.0 us)
Async XLA Ops:
  3.6 33.2 %copy-start = (bf16[36,128,128]{2,1,0:T(8,128)(2,1)S(1)}, bf16[36,128,128]{2,1,0:T(8,128)(2,1)}, u32[]{:S(2)}) copy-start(bf16[36,128,128]{2,1,0:T(8,128)(2,1)} %row_ref.3) | copy-start | bytes 3538948
  3.6 33.2 %copy-start.1 = (bf16[36,128,128]{2,1,0:T(8,128)(2,1)S(1)}, bf16[36,128,128]{2,1,0:T(8,128)(2,1)}, u32[]{:S(2)}) copy-start(bf16[36,128,128]{2,1,0:T(8,128)(2,1)} %col_ref.3) | copy-start | bytes 3538948
  3.6 33.1 %copy-start.5 = (s32[1,128]{1,0:T(1,128)S(1)}, s32[1,128]{1,0:T(1,128)}, u32[]{:S(2)}) copy-start(s32[1,128]{1,0:T(1,128)} %get-tuple-element.18.source_ref) | copy-start | bytes 1540
  36.7 6.8 %copy-start.3 = (bf16[176,240]{1,0:T(8,128)(2,1)S(1)}, bf16[176,240]{1,0:T(8,128)(2,1)}, u32[]{:S(2)}) copy-start(bf16[176,240]{1,0:T(8,128)(2,1)} %constant.10.clone.down) | copy-start | bytes 253444
  37.8 8.9 %collective-permute-start = (bf16[192,128]{1,0:T(8,128)(2,1)S(1)}, bf16[192,128]{1,0:T(8,128)(2,1)S(1)}, u32[]{:S(2)}, u32[]{:S(2)}) collective-permute-start(bf16[192,128]{1,0:T(8,128)(2,1)S(1)} %get-tuple-element.23), channel_id=1, source_target_pairs={{0,16},{32,48},{64,80},{96,112},{16,0},{48,32},{80,64},{112,96},{1... | collective-permute-start | bytes 147464 | tf_op jit(solution)/shard_map/ppermute | solution.py:566
  40.4 6.3 %collective-permute-start.1 = (bf16[192,128]{1,0:T(8,128)(2,1)S(1)}, bf16[192,128]{1,0:T(8,128)(2,1)S(1)}, u32[]{:S(2)}, u32[]{:S(2)}) collective-permute-start(bf16[192,128]{1,0:T(8,128)(2,1)S(1)} %get-tuple-element.24), channel_id=1, source_target_pairs={{16,32},{48,64},{80,96},{32,16},{64,48},{96,80},{17,33},{49,65},{8... | collective-permute-start | bytes 147464 | tf_op jit(solution)/shard_map/ppermute | solution.py:566
  43.5 8.0 %copy-start.2 = (bf16[512,256]{1,0:T(8,128)(2,1)S(1)}, bf16[512,256]{1,0:T(8,128)(2,1)}, u32[]{:S(2)}) copy-start(bf16[512,256]{1,0:T(8,128)(2,1)} %constant.11.clone.across) | copy-start | bytes 786436
  46.8 12.0 %collective-permute-start.2 = (bf16[32,1024]{1,0:T(8,128)(2,1)S(1)}, bf16[32,1024]{1,0:T(8,128)(2,1)S(1)}, u32[]{:S(2)}, u32[]{:S(2)}) collective-permute-start(bf16[32,1024]{1,0:T(8,128)(2,1)S(1)} %pad_maximum_fusion), channel_id=1, source_target_pairs={{0,1},{2,3},{4,5},{6,7},{8,9},{10,11},{12,13},{14,15},{1,0},{3,2},... | collective-permute-start | bytes 196616 | tf_op jit(solution)/shard_map/ppermute | solution.py:566
  46.9 11.8 %collective-permute-start.3 = (bf16[32,1024]{1,0:T(8,128)(2,1)S(1)}, bf16[32,1024]{1,0:T(8,128)(2,1)S(1)}, u32[]{:S(2)}, u32[]{:S(2)}) collective-permute-start(bf16[32,1024]{1,0:T(8,128)(2,1)S(1)} %pad_maximum_fusion.1), channel_id=1, source_target_pairs={{1,2},{3,4},{5,6},{7,8},{9,10},{11,12},{13,14},{2,1},{4,3},{6,5},{... | collective-permute-start | bytes 196616 | tf_op jit(solution)/shard_map/ppermute | solution.py:566
  51.5 7.3 %copy-start.4 = (bf16[32,96]{1,0:T(8,128)(2,1)S(1)}, bf16[32,96]{1,0:T(8,128)(2,1)}, u32[]{:S(2)}) copy-start(bf16[32,96]{1,0:T(8,128)(2,1)} %constant.12.clone.down) | copy-start | bytes 18436

commit v5 on v4

--- a/solution.py
+++ b/solution.py
@@ -55,7 +55,7 @@
         hit = (block >= 0) & (block < held) & (k < live)
         chosen = jnp.where(hit & (rank == row), block, chosen)
         rank = rank + hit.astype(jnp.int32)
-    found[...] = chosen
+    found[...] = jnp.where(row < CAP, chosen, rank)
     handed = pltpu.make_async_copy(found, table, sems.at[4])
     handed.start()
     copies[4].wait()
@@ -78,16 +78,26 @@
     copies[3].wait()
 
     def one_tile(t, carry):
-        for j in range(CAP):
-            block = table[j, first + t]
-            value = blocks[block].astype(F32) * scale[block]
-            staged[t, j] = value.astype(BF16)
-        pltpu.make_async_copy(staged.at[t], out_hbm.at[t], out_sems.at[t]).start()
+        @pl.when(table[CAP, first + t] > 0)
+        def fill():
+            for j in range(CAP):
+                block = table[j, first + t]
+                value = blocks[block].astype(F32) * scale[block]
+                staged[t, j] = value.astype(BF16)
+            pltpu.make_async_copy(staged.at[t], out_hbm.at[t], out_sems.at[t]).start()
+
         return carry
 
     lax.fori_loop(0, holders, one_tile, 0)
-    for t in range(out_hbm.shape[0]):
-        pltpu.make_async_copy(staged.at[t], out_hbm.at[t], out_sems.at[t]).wait()
+
+    def one_wait(t, carry):
+        @pl.when(table[CAP, first + t] > 0)
+        def drain():
+            pltpu.make_async_copy(staged.at[t], out_hbm.at[t], out_sems.at[t]).wait()
+
+        return carry
+
+    lax.fori_loop(0, holders, one_wait, 0)
     told.wait()
 
 
@@ -276,9 +286,9 @@
     along = dc - uc
     grad_x = (one + two) + (across + across)
     grad_y = (one - two) + (along + along)
-    steep = (grad_x * grad_x + grad_y * grad_y).astype(F32)
-    square = 1.0 + steep * (1.0 / 64.0)
-    slope = square * lax.rsqrt(square)
+    steep = grad_x * grad_x + grad_y * grad_y
+    square = BF16(1.0) + steep * BF16(1.0 / 64.0)
+    slope = (square * lax.rsqrt(square)).astype(F32)
     flows = []
     for value, diagonal in (
         (ul, True), (uc, False), (ur, True), (cl, False),
@@ -330,13 +340,17 @@
             lane == 127, pltpu.roll(value, 127, 1), high_ref[lanes - 1, span, :]
         )
 
-    def copies(i):
-        span = pl.ds(pl.multiple_of(i * STEP, 16), STEP)
-        place = pl.ds(pl.multiple_of(PAD + i * STEP, 16), STEP)
+    halves = ((0, 96), (96, STEP - 96))
+
+    def copies(i, half):
+        start, size = halves[half]
+        span = pl.ds(pl.multiple_of(i * STEP + start, 16), size)
+        place = pl.ds(pl.multiple_of(PAD + i * STEP + start, 16), size)
+        sem = sems.at[i, half]
         return (
-            pltpu.make_async_copy(relief.at[span], relief_hbm.at[place], sems.at[i, 0]),
-            pltpu.make_async_copy(slope.at[span], slope_hbm.at[place], sems.at[i, 1]),
-            pltpu.make_async_copy(flow.at[:, span], flow_hbm.at[:, place], sems.at[i, 2]),
+            pltpu.make_async_copy(relief.at[span], relief_hbm.at[place], sem.at[0]),
+            pltpu.make_async_copy(slope.at[span], slope_hbm.at[place], sem.at[1]),
+            pltpu.make_async_copy(flow.at[:, span], flow_hbm.at[:, place], sem.at[2]),
         )
 
     def mid(j, span):
@@ -381,14 +395,17 @@
                 slope[place] = value
                 for n, part in enumerate(parts):
                     flow[(n,) + place] = part
-        for copy in copies(i):
-            copy.start()
+            for half, (start, size) in enumerate(halves):
+                if q * 16 + 16 == start + size:
+                    for copy in copies(i, half):
+                        copy.start()
         return carry
 
     lax.fori_loop(0, steps, one_step, 0)
     for i in range(steps):
-        for copy in copies(i):
-            copy.wait()
+        for half in range(2):
+            for copy in copies(i, half):
+                copy.wait()
 
 
 def main(edge_values, inner, low, high, fall, left, right):
@@ -406,7 +423,7 @@
             pltpu.VMEM((8, tall, cols), BF16),
             pltpu.VMEM((2, rows, 128), BF16),
             pltpu.VMEM((2, rows, 128), F32),
-            pltpu.SemaphoreType.DMA((tall // STEP, 3)),
+            pltpu.SemaphoreType.DMA((tall // STEP, 2, 3)),
         ],
         cost_estimate=cost(tall * cols),
         compiler_params=pltpu.CompilerParams(vmem_limit_bytes=32 * MIB),

time: 60.8 us -> 60.2 us (level)
  no operation moved by 1% of the time
where the time goes in v5:
time: 60.2 us; the launch traced here: 60 us
  blocking collectives  32.9 us (55%)
  Pallas kernels  15.6 us (26%)
  starting transfers between devices  10.7 us (18%)
  between operations  0.81 us (1%)
    all_to_all x1, blocking collectives, local(): lax.all_to_all(outgoing, 'gy', split_axis=0, concat_axis=0, tiled=True)  32.9 us
    ppermute x4, starting transfers between devices, swap(): lax.ppermute(value, axis, pairs + [(j, i) for i, j in pairs])  10.7 us
    pallas_call x1, Pallas kernels, main(): pl.pallas_call(main_kernel, out_shape=out_shapes(rows, cols), in_specs=[V...  6.93 us
    pallas_call x1, Pallas kernels, middle(): pl.pallas_call(middle_kernel, out_shape=[jax.ShapeDtypeStruct(s, d) for s...  3.15 us
    pallas_call x1, Pallas kernels, gather(): pl.pallas_call(gather_kernel, out_shape=[jax.ShapeDtypeStruct((holders, C...  2.63 us
    pallas_call x1, Pallas kernels, ends(): pl.pallas_call(ends_kernel, out_shape=out_shapes(rows, cols), in_specs=[V...  1.79 us
  transfers between devices with their start and end apart: 4, of which 0 were waited for; matrix products, arithmetic and copies ran while one was open for 0% of the time, Pallas kernels for 17%

profile of v5, /device:TPU:11, one launch (start us, length us, event | category | flops | bytes accessed | tf_op | source)
XLA Modules:
  0.0 60.0 jit_solution(5746502079959616845)
XLA Ops:
  0.6 2.6 %gather_blocks.1 = (bf16[16,4,128,128]{3,2,1,0:T(8,128)(2,1)}, s32[1,128]{1,0:T(1,128)}) custom-call(s32[36,128]{1,0:T(8,128)} %bitcast.13, s32[1,128]{1,0:T(1,128)} %bitcast.14, f32[32]{0:T(128)} %scale_hbm.1, bf16[32,128,128]{2,1,0:T(8,128)(2,1)} %blocks_hbm.1), custom_call_target="tpu_custom_call" | custom-call | tf_op jit(solution)/shard_map/gather_blocks/pallas_call | solution.py:108
  3.3 0.0 copy-start
  3.3 0.0 copy-start.1
  3.3 0.0 copy-start.5
  3.3 32.9 %all_to_all.5 = bf16[16,4,128,128]{3,2,1,0:T(8,128)(2,1)S(1)} all-to-all(bf16[16,4,128,128]{3,2,1,0:T(8,128)(2,1)} %get-tuple-element.19), channel_id=1, replica_groups=mesh['gx'=8,'gy'=16] {'gy'}, dimensions={0} | all-to-all | bytes 4194304 | tf_op jit(solution)/shard_map/all_to_all | solution.py:591
  36.2 0.0 copy-start.3
  36.2 0.0 copy-done
  36.2 0.0 copy-done.1
  36.2 0.0 copy-done.5
  36.2 1.1 %edge_windows.1 = (f32[2,768,128]{2,1,0:T(8,128)S(1)}, bf16[192,128]{1,0:T(8,128)(2,1)S(1)}, bf16[192,128]{1,0:T(8,128)(2,1)S(1)}) custom-call(s32[1,128]{1,0:T(1,128)S(1)} %copy-done.5, bf16[64,128,128]{2,1,0:T(8,128)(2,1)S(1)} %bitcast.11, bf16[36,128,128]{2,1,0:T(8,128)(2,1)S(1)} %copy-done, bf16[36,128,128]{2,1,0:T(8,128)(2,1)S(1)} %copy-done.1), custom_call_target="tpu_custom_call" | custom-call | flops 786432000 | bytes 4718592 | tf_op jit(solution)/shard_map/edge_windows/pallas_call | solution.py:187
  37.3 2.4 %collective-permute-start = (bf16[192,128]{1,0:T(8,128)(2,1)S(1)}, bf16[192,128]{1,0:T(8,128)(2,1)S(1)}, u32[]{:S(2)}, u32[]{:S(2)}) collective-permute-start(bf16[192,128]{1,0:T(8,128)(2,1)S(1)} %get-tuple-element.23), channel_id=1, source_target_pairs={{0,16},{32,48},{64,80},{96,112},{16,0},{48,32},{80,64},{112,96},{1... | collective-permute-start | bytes 147464 | tf_op jit(solution)/shard_map/ppermute | solution.py:583
  39.7 3.5 %collective-permute-start.1 = (bf16[192,128]{1,0:T(8,128)(2,1)S(1)}, bf16[192,128]{1,0:T(8,128)(2,1)S(1)}, u32[]{:S(2)}, u32[]{:S(2)}) collective-permute-start(bf16[192,128]{1,0:T(8,128)(2,1)S(1)} %get-tuple-element.24), channel_id=1, source_target_pairs={{16,32},{48,64},{80,96},{32,16},{64,48},{96,80},{17,33},{49,65},{8... | collective-permute-start | bytes 147464 | tf_op jit(solution)/shard_map/ppermute | solution.py:583
  43.3 0.0 copy-done.3
  43.3 0.0 copy-start.2
  43.3 3.1 %middle_windows.1 = (f32[4,768,128]{2,1,0:T(8,128)S(1)}, f32[6,768,128]{2,1,0:T(8,128)S(1)}, f32[6,768,128]{2,1,0:T(8,128)S(1)}, bf16[768,768]{1,0:T(8,128)(2,1)...) custom-call(s32[1,128]{1,0:T(1,128)S(1)} %copy-done.5, ...), custom_call_target="tpu_custom_call" | custom-call | flops 2359296000 | bytes 14155776 | tf_op jit(solution)/shard_map/middle_windows/pallas_call | solution.py:251
  46.5 0.0 collective-permute-done.first_ref
  46.5 0.0 collective-permute-done.1.second_ref
  46.5 0.2 collective-permute-start.2
  46.7 4.6 %collective-permute-start.3 = (bf16[32,1024]{1,0:T(8,128)(2,1)S(1)}, bf16[32,1024]{1,0:T(8,128)(2,1)S(1)}, u32[]{:S(2)}, u32[]{:S(2)}) collective-permute-start(bf16[32,1024]{1,0:T(8,128)(2,1)S(1)} %pad_maximum_fusion.1), channel_id=1, source_target_pairs={{1,2},{3,4},{5,6},{7,8},{9,10},{11,12},{13,14},{2,1},{4,3},{6,5},{... | collective-permute-start | bytes 196616 | tf_op jit(solution)/shard_map/ppermute | solution.py:583
  51.3 0.0 copy-done.2
  51.3 0.0 copy-start.4
  51.3 6.9 %main_cells.1 = (f32[768,768]{1,0:T(8,128)}, f32[768,768]{1,0:T(8,128)}, bf16[8,768,768]{2,1,0:T(8,128)(2,1)}) custom-call(f32[2,768,128]{2,1,0:T(8,128)S(1)} %get-tuple-element.20.edge_ref, f32[4,768,128]{2,1,0:T(8,128)S(1)} %get-tuple-element.21.inner_ref, f32[6,768,128]{2,1,0:T(8,128)S(1)} %get-tuple-element.27.low_ref, ...), custom_call_target="tpu_custom_call" | custom-call | flops 2162688000 | bytes 12976128 | tf_op jit(solution)/shard_map/main_cells/pallas_call | solution.py:415
  58.2 0.0 collective-permute-done.2.near_ref
  58.2 0.0 collective-permute-done.3.next_ref
  58.2 0.0 copy-done.4
  58.3 1.8 %end_cells.1 = (f32[768,768]{1,0:T(8,128)}, f32[768,768]{1,0:T(8,128)}, bf16[8,768,768]{2,1,0:T(8,128)(2,1)}) custom-call(f32[2,768,128]{2,1,0:T(8,128)S(1)} %get-tuple-element.20.edge_ref, f32[4,768,128]{2,1,0:T(8,128)S(1)} %get-tuple-element.21.inner_ref, ...), custom_call_target="tpu_custom_call", output_to_operand_aliasing={{0}: (9, {}), {1}: (10, {}), {2}: (11, {})} | custom-call | flops 196608000 | bytes 1179648 | tf_op jit(solution)/shard_map/end_cells/pallas_call | solution.py:553
  (5 shorter events, 0.0 us)
Async XLA Ops:
  3.3 32.9 %copy-start = (bf16[36,128,128]{2,1,0:T(8,128)(2,1)S(1)}, bf16[36,128,128]{2,1,0:T(8,128)(2,1)}, u32[]{:S(2)}) copy-start(bf16[36,128,128]{2,1,0:T(8,128)(2,1)} %row_ref.3) | copy-start | bytes 3538948
  3.3 32.9 %copy-start.1 = (bf16[36,128,128]{2,1,0:T(8,128)(2,1)S(1)}, bf16[36,128,128]{2,1,0:T(8,128)(2,1)}, u32[]{:S(2)}) copy-start(bf16[36,128,128]{2,1,0:T(8,128)(2,1)} %col_ref.3) | copy-start | bytes 3538948
  3.3 32.9 %copy-start.5 = (s32[1,128]{1,0:T(1,128)S(1)}, s32[1,128]{1,0:T(1,128)}, u32[]{:S(2)}) copy-start(s32[1,128]{1,0:T(1,128)} %get-tuple-element.18.source_ref) | copy-start | bytes 1540
  36.2 7.0 %copy-start.3 = (bf16[176,240]{1,0:T(8,128)(2,1)S(1)}, bf16[176,240]{1,0:T(8,128)(2,1)}, u32[]{:S(2)}) copy-start(bf16[176,240]{1,0:T(8,128)(2,1)} %constant.10.clone.down) | copy-start | bytes 253444
  37.3 9.2 %collective-permute-start = (bf16[192,128]{1,0:T(8,128)(2,1)S(1)}, bf16[192,128]{1,0:T(8,128)(2,1)S(1)}, u32[]{:S(2)}, u32[]{:S(2)}) collective-permute-start(bf16[192,128]{1,0:T(8,128)(2,1)S(1)} %get-tuple-element.23), channel_id=1, source_target_pairs={{0,16},{32,48},{64,80},{96,112},{16,0},{48,32},{80,64},{112,96},{1... | collective-permute-start | bytes 147464 | tf_op jit(solution)/shard_map/ppermute | solution.py:583
  39.7 6.8 %collective-permute-start.1 = (bf16[192,128]{1,0:T(8,128)(2,1)S(1)}, bf16[192,128]{1,0:T(8,128)(2,1)S(1)}, u32[]{:S(2)}, u32[]{:S(2)}) collective-permute-start(bf16[192,128]{1,0:T(8,128)(2,1)S(1)} %get-tuple-element.24), channel_id=1, source_target_pairs={{16,32},{48,64},{80,96},{32,16},{64,48},{96,80},{17,33},{49,65},{8... | collective-permute-start | bytes 147464 | tf_op jit(solution)/shard_map/ppermute | solution.py:583
  43.3 8.0 %copy-start.2 = (bf16[512,256]{1,0:T(8,128)(2,1)S(1)}, bf16[512,256]{1,0:T(8,128)(2,1)}, u32[]{:S(2)}) copy-start(bf16[512,256]{1,0:T(8,128)(2,1)} %constant.11.clone.across) | copy-start | bytes 786436
  46.5 11.7 %collective-permute-start.2 = (bf16[32,1024]{1,0:T(8,128)(2,1)S(1)}, bf16[32,1024]{1,0:T(8,128)(2,1)S(1)}, u32[]{:S(2)}, u32[]{:S(2)}) collective-permute-start(bf16[32,1024]{1,0:T(8,128)(2,1)S(1)} %pad_maximum_fusion), channel_id=1, source_target_pairs={{0,1},{2,3},{4,5},{6,7},{8,9},{10,11},{12,13},{14,15},{1,0},{3,2},... | collective-permute-start | bytes 196616 | tf_op jit(solution)/shard_map/ppermute | solution.py:583
  46.7 11.5 %collective-permute-start.3 = (bf16[32,1024]{1,0:T(8,128)(2,1)S(1)}, bf16[32,1024]{1,0:T(8,128)(2,1)S(1)}, u32[]{:S(2)}, u32[]{:S(2)}) collective-permute-start(bf16[32,1024]{1,0:T(8,128)(2,1)S(1)} %pad_maximum_fusion.1), channel_id=1, source_target_pairs={{1,2},{3,4},{5,6},{7,8},{9,10},{11,12},{13,14},{2,1},{4,3},{6,5},{... | collective-permute-start | bytes 196616 | tf_op jit(solution)/shard_map/ppermute | solution.py:583
  51.3 7.0 %copy-start.4 = (bf16[32,96]{1,0:T(8,128)(2,1)S(1)}, bf16[32,96]{1,0:T(8,128)(2,1)}, u32[]{:S(2)}) copy-start(bf16[32,96]{1,0:T(8,128)(2,1)} %constant.12.clone.down) | copy-start | bytes 18436

commit v6 on v5

--- a/solution.py
+++ b/solution.py
@@ -17,6 +17,7 @@
 F32 = jnp.float32
 BF16 = jnp.bfloat16
 MIB = 1 << 20
+ZERO_AT = W * W
 
 SMEM = pl.BlockSpec(memory_space=pltpu.SMEM)
 VMEM = pl.BlockSpec(memory_space=pltpu.VMEM)
@@ -206,21 +207,16 @@
     for s in range(2):
         band_ref[:, s * (W - 1) * edge : (s * (W - 1) + 1) * edge] = edge_ref[s].astype(BF16)
 
-    for i in range(W):
+
+    def windows(i):
         span = slice(i * edge, (i + 1) * edge)
         for j in range(1, W - 1):
             value = window(i * W + j, source_ref, arrived_ref, row_ref, col_ref)
             inner_ref[j - 1, span, :] = value
             band_ref[span, j * edge : (j + 1) * edge] = value.astype(BF16)
-    for n in range(2):
-        at = pl.multiple_of(jnp.where(odd == n, rows - PAD, 0), PAD)
-        strips_ref[n] = band_ref[pl.ds(at, PAD), :]
-    for i in range((rows - 2 * PAD) // STEP):
-        value = dot(down[...], band_ref[i * STEP : (i + 1) * STEP + 2 * PAD, :])
-        fall_ref[i * STEP : (i + 1) * STEP, :] = value.astype(BF16)
-
-    def one_span(q, carry):
-        span = pl.ds(pl.multiple_of(q * edge, edge), edge)
+
+    def shifts(i):
+        span = slice(i * edge, (i + 1) * edge)
         pieces = [edge_ref[0, span, :]]
         pieces += [inner_ref[j, span, :] for j in range(W - 2)] + [edge_ref[1, span, :]]
         lane = lax.broadcasted_iota(jnp.int32, pieces[0].shape, 1)
@@ -231,9 +227,20 @@
             high_ref[j, span, :] = (
                 jnp.where(lane == 127, highs[j + 1], highs[j]) if j < W - 1 else highs[j]
             )
-        return carry
-
-    lax.fori_loop(0, W, one_span, 0)
+
+    fallen = 0
+    for t in range(W + 1):
+        while fallen < rows - 2 * PAD and fallen + STEP + 2 * PAD <= t * edge:
+            value = dot(down[...], band_ref[fallen : fallen + STEP + 2 * PAD, :])
+            fall_ref[fallen : fallen + STEP, :] = value.astype(BF16)
+            fallen += STEP
+        if t:
+            shifts(t - 1)
+        if t < W:
+            windows(t)
+    for n in range(2):
+        at = pl.multiple_of(jnp.where(odd == n, rows - PAD, 0), PAD)
+        strips_ref[n] = band_ref[pl.ds(at, PAD), :]
 
 
 def middle(source, arrived, row_weights, col_weights, edge_values):
@@ -320,7 +327,7 @@
 
 def main_kernel(
     edge_ref, inner_ref, low_ref, high_ref, fall_ref, first_ref, second_ref, across, down,
-    relief_hbm, slope_hbm, flow_hbm, relief, slope, flow, far, patched, sems,
+    zero_ref, relief_hbm, slope_hbm, flow_hbm, relief, slope, flow, far, patched, sems, relief_sems,
 ):
     rows, cols = low_ref.shape[1], relief.shape[1]
     lanes = cols // 128
@@ -332,10 +339,10 @@
     for q in range(4):
         span = slice(q * chunk, (q + 1) * chunk)
         value = unpack_left(left, q)
-        far[0, span, :] = value.astype(BF16)
+        far[span, 0:128] = value.astype(BF16)
         patched[0, span, :] = jnp.where(lane == 0, pltpu.roll(value, 1, 1), low_ref[0, span, :])
         value = unpack_right(right, q)
-        far[1, span, :] = value.astype(BF16)
+        far[span, 128:256] = value.astype(BF16)
         patched[1, span, :] = jnp.where(
             lane == 127, pltpu.roll(value, 127, 1), high_ref[lanes - 1, span, :]
         )
@@ -344,13 +351,18 @@
 
     def copies(i, half):
         start, size = halves[half]
-        span = pl.ds(pl.multiple_of(i * STEP + start, 16), size)
-        place = pl.ds(pl.multiple_of(PAD + i * STEP + start, 16), size)
+        span = slice(i * STEP + start, i * STEP + start + size)
+        place = pl.ds(PAD + i * STEP + start, size)
         sem = sems.at[i, half]
         return (
-            pltpu.make_async_copy(relief.at[span], relief_hbm.at[place], sem.at[0]),
-            pltpu.make_async_copy(slope.at[span], slope_hbm.at[place], sem.at[1]),
-            pltpu.make_async_copy(flow.at[:, span], flow_hbm.at[:, place], sem.at[2]),
+            pltpu.make_async_copy(slope.at[span], slope_hbm.at[place], sem.at[0]),
+            pltpu.make_async_copy(flow.at[:, span], flow_hbm.at[:, place], sem.at[1]),
+        )
+
+    def relief_copy(j):
+        column = pl.ds(j * 256, 256)
+        return pltpu.make_async_copy(
+            relief.at[:, column], relief_hbm.at[pl.ds(PAD, rows - 2 * PAD), column], relief_sems.at[j]
         )
 
     def mid(j, span):
@@ -364,34 +376,38 @@
     def high(j, span):
         return high_ref[j, span, :] if j < lanes - 1 else patched[1, span, :]
 
-    def one_step(i, carry):
-        base = pl.multiple_of(i * STEP, 16)
-        tall = pl.ds(base, STEP + 2 * PAD)
-        span = pl.ds(base, STEP)
-        sides = [dot(down[...], far[s, tall, :]).astype(BF16) for s in range(2)]
-        for j in range(lanes // 2):
-            at = j * 256
-            if j == 0:
-                wide = jnp.concatenate([sides[0], fall_ref[span, 0:384]], axis=1)
-            elif j == lanes // 2 - 1:
-                wide = jnp.concatenate([fall_ref[span, at - 128 :], sides[1]], axis=1)
-            else:
-                wide = fall_ref[span, at - 128 : at + 384]
-            value = dot(wide, across[...])
-            for h in range(2):
-                centre = mid(j * 2 + h, pl.ds(base + PAD, STEP))
-                relief[span, at + h * 128 : at + h * 128 + 128] = (
-                    centre - value[:, h * 128 : h * 128 + 128] * inverse
-                )
+    def smooth(j):
+        at = j * 256
+        if j == 0:
+            wide = jnp.concatenate([sides[:, 0:128], fall_ref[:, 0:384]], axis=1)
+        elif j == lanes // 2 - 1:
+            wide = jnp.concatenate([fall_ref[:, at - 128 :], sides[:, 128:256]], axis=1)
+        else:
+            wide = fall_ref[:, at - 128 : at + 384]
+        value = dot(wide, across[...])
+        for h in range(2):
+            centre = mid(j * 2 + h, slice(PAD, rows - PAD))
+            relief[:, at + h * 128 : at + h * 128 + 128] = (
+                centre - value[:, h * 128 : h * 128 + 128] * inverse
+            )
+        relief_copy(j).start()
+
+    zero = jnp.minimum(zero_ref[0, ZERO_AT], 0)
+    sides = jnp.concatenate(
+        [dot(down[...], far[i * STEP : (i + 1) * STEP + 2 * PAD, :]).astype(BF16) for i in range(steps)],
+        axis=0,
+    )
+    for i in range(steps):
+        if i < lanes // 2:
+            smooth(i)
         for q in range(STEP // 16):
-            at = pl.multiple_of(base + q * 16, 16)
+            at = i * STEP + q * 16
             for j in range(lanes):
-                value, parts = cells(
-                    lambda d: mid(j, pl.ds(at + PAD + d, 16)),
-                    lambda d: low(j, pl.ds(at + PAD + d, 16)),
-                    lambda d: high(j, pl.ds(at + PAD + d, 16)),
-                )
-                place = (pl.ds(at, 16), slice(j * 128, (j + 1) * 128))
+                def load(piece):
+                    return lambda d: piece(j, pl.ds(at + PAD + (zero + d if d else 0), 16))
+
+                value, parts = cells(load(mid), load(low), load(high))
+                place = (slice(at, at + 16), slice(j * 128, (j + 1) * 128))
                 slope[place] = value
                 for n, part in enumerate(parts):
                     flow[(n,) + place] = part
@@ -399,36 +415,39 @@
                 if q * 16 + 16 == start + size:
                     for copy in copies(i, half):
                         copy.start()
-        return carry
-
-    lax.fori_loop(0, steps, one_step, 0)
+    for j in range(lanes // 2):
+        relief_copy(j).wait()
     for i in range(steps):
         for half in range(2):
             for copy in copies(i, half):
                 copy.wait()
 
 
-def main(edge_values, inner, low, high, fall, left, right):
+def main(edge_values, inner, low, high, fall, left, right, source):
     lanes, rows, _ = low.shape
     cols = lanes * 128
     tall = rows - 2 * PAD
     return pl.pallas_call(
         main_kernel,
         out_shape=out_shapes(rows, cols),
-        in_specs=[VMEM] * 9,
+        in_specs=[VMEM] * 9 + [SMEM],
         out_specs=[ANY] * 3,
         scratch_shapes=[
             pltpu.VMEM((tall, cols), F32),
             pltpu.VMEM((tall, cols), F32),
             pltpu.VMEM((8, tall, cols), BF16),
-            pltpu.VMEM((2, rows, 128), BF16),
+            pltpu.VMEM((rows, 256), BF16),
             pltpu.VMEM((2, rows, 128), F32),
-            pltpu.SemaphoreType.DMA((tall // STEP, 2, 3)),
+            pltpu.SemaphoreType.DMA((tall // STEP, 2, 2)),
+            pltpu.SemaphoreType.DMA((cols // 256,)),
         ],
         cost_estimate=cost(tall * cols),
         compiler_params=pltpu.CompilerParams(vmem_limit_bytes=32 * MIB),
         name="main_cells",
-    )(edge_values, inner, low, high, fall, left, right, across_taps(512, 256), down_taps(STEP))
+    )(
+        edge_values, inner, low, high, fall, left, right,
+        across_taps(512, 256), down_taps(STEP), source,
+    )
 
 
 def out_shapes(rows, cols):
@@ -506,15 +525,15 @@
                 wide[j + 1, top : top + 40, :] = own[rows - 40 : rows, :]
                 wide[j + 1, top + 40 : top + 48, :] = part[0:8]
 
-    for e in range(2):
-        smooth = dot(down[...], band[e]).astype(BF16)
-        for j in range(lanes // 2):
-            value = dot(smooth[:, j * 256 : j * 256 + 512], across[...])
+    smooth = jnp.concatenate([dot(down[...], band[e]).astype(BF16) for e in range(2)], axis=0)
+    for j in range(lanes // 2):
+        value = dot(smooth[:, j * 256 : j * 256 + 512], across[...])
+        for e in range(2):
             for h in range(2):
                 at = j * 256 + h * 128
-                relief[e, :, at : at + 128] = (
-                    wide[j * 2 + h + 1, e * tall + 8 : e * tall + 8 + PAD, :] - value[:, h * 128 : h * 128 + 128] * inverse
-                )
+                centre = wide[j * 2 + h + 1, e * tall + 8 : e * tall + 8 + PAD, :]
+                part = value[e * PAD : (e + 1) * PAD, h * 128 : h * 128 + 128]
+                relief[e, :, at : at + 128] = centre - part * inverse
     for j in range(lanes):
         low, high = sideways(wide[j + 1], wide[j], wide[j + 2])
         low_ref[j] = low
@@ -599,7 +618,7 @@
         corners = [jnp.where(odd[:1] == n, side[-PAD:], side[:PAD]) for side in beside]
         messages.append(jnp.concatenate([strips[n], *corners], axis=1))
     ahead = swap(*messages, "gy")
-    outs = main(edge_values, inner, low, high, fall, *beside)
+    outs = main(edge_values, inner, low, high, fall, *beside, source)
     return tuple(ends(edge_values, inner, band, *beside, *ahead, outs))
 
 

time: 60.2 us -> 59.4 us (0.987)
  Pallas kernels: 15.6 us -> 14.6 us
  transfers between devices with their start and end apart: 4 -> 4, of which waited for: 0 -> 0; matrix products, arithmetic and copies ran while one was open for 0% -> 0% of each run, Pallas kernels for 17% -> 16%
where the time goes in v6:
time: 59.4 us; the launch traced here: 59.2 us
  blocking collectives  33.2 us (56%)
  Pallas kernels  14.6 us (25%)
  starting transfers between devices  10.5 us (18%)
  between operations  0.81 us (1%)
    all_to_all x1, blocking collectives, local(): lax.all_to_all(outgoing, 'gy', split_axis=0, concat_axis=0, tiled=True)  33.2 us
    ppermute x4, starting transfers between devices, swap(): lax.ppermute(value, axis, pairs + [(j, i) for i, j in pairs])  10.5 us
    pallas_call x1, Pallas kernels, main(): pl.pallas_call(main_kernel, out_shape=out_shapes(rows, cols), in_specs=[V...  6.51 us
    pallas_call x1, Pallas kernels, middle(): pl.pallas_call(middle_kernel, out_shape=[jax.ShapeDtypeStruct(s, d) for s...  2.79 us
    pallas_call x1, Pallas kernels, gather(): pl.pallas_call(gather_kernel, out_shape=[jax.ShapeDtypeStruct((holders, C...  2.61 us
    pallas_call x1, Pallas kernels, ends(): pl.pallas_call(ends_kernel, out_shape=out_shapes(rows, cols), in_specs=[V...  1.64 us
  transfers between devices with their start and end apart: 4, of which 0 were waited for; matrix products, arithmetic and copies ran while one was open for 0% of the time, Pallas kernels for 16%

profile of v6, /device:TPU:11, one launch (start us, length us, event | category | flops | bytes accessed | tf_op | source)
XLA Modules:
  0.0 59.2 jit_solution(17546549244889526354)
XLA Ops:
  0.6 2.6 %gather_blocks.1 = (bf16[16,4,128,128]{3,2,1,0:T(8,128)(2,1)}, s32[1,128]{1,0:T(1,128)}) custom-call(s32[36,128]{1,0:T(8,128)} %bitcast.13, s32[1,128]{1,0:T(1,128)} %bitcast.14, f32[32]{0:T(128)} %scale_hbm.1, bf16[32,128,128]{2,1,0:T(8,128)(2,1)} %blocks_hbm.1), custom_call_target="tpu_custom_call" | custom-call | tf_op jit(solution)/shard_map/gather_blocks/pallas_call | solution.py:109
  3.2 0.0 copy-start
  3.3 0.0 copy-start.1
  3.3 0.0 copy-start.5
  3.3 33.2 %all_to_all.5 = bf16[16,4,128,128]{3,2,1,0:T(8,128)(2,1)S(1)} all-to-all(bf16[16,4,128,128]{3,2,1,0:T(8,128)(2,1)} %get-tuple-element.19), channel_id=1, replica_groups=mesh['gx'=8,'gy'=16] {'gy'}, dimensions={0} | all-to-all | bytes 4194304 | tf_op jit(solution)/shard_map/all_to_all | solution.py:610
  36.5 0.0 copy-start.3
  36.5 0.0 copy-done
  36.5 0.0 copy-done.1
  36.5 0.0 copy-done.5
  36.5 1.1 %edge_windows.1 = (f32[2,768,128]{2,1,0:T(8,128)S(1)}, bf16[192,128]{1,0:T(8,128)(2,1)S(1)}, bf16[192,128]{1,0:T(8,128)(2,1)S(1)}) custom-call(s32[1,128]{1,0:T(1,128)S(1)} %copy-done.5, bf16[64,128,128]{2,1,0:T(8,128)(2,1)S(1)} %bitcast.11, bf16[36,128,128]{2,1,0:T(8,128)(2,1)S(1)} %copy-done, bf16[36,128,128]{2,1,0:T(8,128)(2,1)S(1)} %copy-done.1), custom_call_target="tpu_custom_call" | custom-call | flops 786432000 | bytes 4718592 | tf_op jit(solution)/shard_map/edge_windows/pallas_call | solution.py:188
  37.6 2.6 %collective-permute-start = (bf16[192,128]{1,0:T(8,128)(2,1)S(1)}, bf16[192,128]{1,0:T(8,128)(2,1)S(1)}, u32[]{:S(2)}, u32[]{:S(2)}) collective-permute-start(bf16[192,128]{1,0:T(8,128)(2,1)S(1)} %get-tuple-element.23), channel_id=1, source_target_pairs={{0,16},{32,48},{64,80},{96,112},{16,0},{48,32},{80,64},{112,96},{1... | collective-permute-start | bytes 147464 | tf_op jit(solution)/shard_map/ppermute | solution.py:602
  40.2 3.2 %collective-permute-start.1 = (bf16[192,128]{1,0:T(8,128)(2,1)S(1)}, bf16[192,128]{1,0:T(8,128)(2,1)S(1)}, u32[]{:S(2)}, u32[]{:S(2)}) collective-permute-start(bf16[192,128]{1,0:T(8,128)(2,1)S(1)} %get-tuple-element.24), channel_id=1, source_target_pairs={{16,32},{48,64},{80,96},{32,16},{64,48},{96,80},{17,33},{49,65},{8... | collective-permute-start | bytes 147464 | tf_op jit(solution)/shard_map/ppermute | solution.py:602
  43.4 0.0 copy-done.3
  43.4 0.0 copy-start.2
  43.4 2.8 %middle_windows.1 = (f32[4,768,128]{2,1,0:T(8,128)S(1)}, f32[6,768,128]{2,1,0:T(8,128)S(1)}, f32[6,768,128]{2,1,0:T(8,128)S(1)}, bf16[768,768]{1,0:T(8,128)(2,1)...) custom-call(s32[1,128]{1,0:T(1,128)S(1)} %copy-done.5, ...), custom_call_target="tpu_custom_call" | custom-call | flops 2359296000 | bytes 14155776 | tf_op jit(solution)/shard_map/middle_windows/pallas_call | solution.py:258
  46.2 0.0 collective-permute-done.first_ref
  46.2 0.0 collective-permute-done.1.second_ref
  46.3 0.2 collective-permute-start.2
  46.5 4.6 %collective-permute-start.3 = (bf16[32,1024]{1,0:T(8,128)(2,1)S(1)}, bf16[32,1024]{1,0:T(8,128)(2,1)S(1)}, u32[]{:S(2)}, u32[]{:S(2)}) collective-permute-start(bf16[32,1024]{1,0:T(8,128)(2,1)S(1)} %pad_maximum_fusion.1), channel_id=1, source_target_pairs={{1,2},{3,4},{5,6},{7,8},{9,10},{11,12},{13,14},{2,1},{4,3},{6,5},{... | collective-permute-start | bytes 196616 | tf_op jit(solution)/shard_map/ppermute | solution.py:602
  51.0 0.0 copy-done.2
  51.0 0.0 copy-start.4
  51.0 6.5 %main_cells.1 = (f32[768,768]{1,0:T(8,128)}, f32[768,768]{1,0:T(8,128)}, bf16[8,768,768]{2,1,0:T(8,128)(2,1)}) custom-call(f32[2,768,128]{2,1,0:T(8,128)S(1)} %get-tuple-element.20.edge_ref, f32[4,768,128]{2,1,0:T(8,128)S(1)} %get-tuple-element.21.inner_ref, f32[6,768,128]{2,1,0:T(8,128)S(1)} %get-tuple-element.27.low_ref, ...), custom_call_target="tpu_custom_call" | custom-call | flops 2162688000 | bytes 12976128 | tf_op jit(solution)/shard_map/main_cells/pallas_call | solution.py:430
  57.6 0.0 collective-permute-done.2.near_ref
  57.6 0.0 collective-permute-done.3.next_ref
  57.6 0.0 copy-done.4
  57.6 1.6 %end_cells.1 = (f32[768,768]{1,0:T(8,128)}, f32[768,768]{1,0:T(8,128)}, bf16[8,768,768]{2,1,0:T(8,128)(2,1)}) custom-call(f32[2,768,128]{2,1,0:T(8,128)S(1)} %get-tuple-element.20.edge_ref, f32[4,768,128]{2,1,0:T(8,128)S(1)} %get-tuple-element.21.inner_ref, ...), custom_call_target="tpu_custom_call", output_to_operand_aliasing={{0}: (9, {}), {1}: (10, {}), {2}: (11, {})} | custom-call | flops 196608000 | bytes 1179648 | tf_op jit(solution)/shard_map/end_cells/pallas_call | solution.py:572
  (5 shorter events, 0.0 us)
Async XLA Ops:
  3.2 33.3 %copy-start = (bf16[36,128,128]{2,1,0:T(8,128)(2,1)S(1)}, bf16[36,128,128]{2,1,0:T(8,128)(2,1)}, u32[]{:S(2)}) copy-start(bf16[36,128,128]{2,1,0:T(8,128)(2,1)} %row_ref.3) | copy-start | bytes 3538948
  3.3 33.3 %copy-start.1 = (bf16[36,128,128]{2,1,0:T(8,128)(2,1)S(1)}, bf16[36,128,128]{2,1,0:T(8,128)(2,1)}, u32[]{:S(2)}) copy-start(bf16[36,128,128]{2,1,0:T(8,128)(2,1)} %col_ref.3) | copy-start | bytes 3538948
  3.3 33.3 %copy-start.5 = (s32[1,128]{1,0:T(1,128)S(1)}, s32[1,128]{1,0:T(1,128)}, u32[]{:S(2)}) copy-start(s32[1,128]{1,0:T(1,128)} %get-tuple-element.18.source_ref.zero_ref) | copy-start | bytes 1540
  36.5 6.8 %copy-start.3 = (bf16[176,240]{1,0:T(8,128)(2,1)S(1)}, bf16[176,240]{1,0:T(8,128)(2,1)}, u32[]{:S(2)}) copy-start(bf16[176,240]{1,0:T(8,128)(2,1)} %constant.10.clone.down) | copy-start | bytes 253444
  37.6 8.6 %collective-permute-start = (bf16[192,128]{1,0:T(8,128)(2,1)S(1)}, bf16[192,128]{1,0:T(8,128)(2,1)S(1)}, u32[]{:S(2)}, u32[]{:S(2)}) collective-permute-start(bf16[192,128]{1,0:T(8,128)(2,1)S(1)} %get-tuple-element.23), channel_id=1, source_target_pairs={{0,16},{32,48},{64,80},{96,112},{16,0},{48,32},{80,64},{112,96},{1... | collective-permute-start | bytes 147464 | tf_op jit(solution)/shard_map/ppermute | solution.py:602
  40.2 6.0 %collective-permute-start.1 = (bf16[192,128]{1,0:T(8,128)(2,1)S(1)}, bf16[192,128]{1,0:T(8,128)(2,1)S(1)}, u32[]{:S(2)}, u32[]{:S(2)}) collective-permute-start(bf16[192,128]{1,0:T(8,128)(2,1)S(1)} %get-tuple-element.24), channel_id=1, source_target_pairs={{16,32},{48,64},{80,96},{32,16},{64,48},{96,80},{17,33},{49,65},{8... | collective-permute-start | bytes 147464 | tf_op jit(solution)/shard_map/ppermute | solution.py:602
  43.4 7.6 %copy-start.2 = (bf16[512,256]{1,0:T(8,128)(2,1)S(1)}, bf16[512,256]{1,0:T(8,128)(2,1)}, u32[]{:S(2)}) copy-start(bf16[512,256]{1,0:T(8,128)(2,1)} %constant.11.clone.across) | copy-start | bytes 786436
  46.3 11.3 %collective-permute-start.2 = (bf16[32,1024]{1,0:T(8,128)(2,1)S(1)}, bf16[32,1024]{1,0:T(8,128)(2,1)S(1)}, u32[]{:S(2)}, u32[]{:S(2)}) collective-permute-start(bf16[32,1024]{1,0:T(8,128)(2,1)S(1)} %pad_maximum_fusion), channel_id=1, source_target_pairs={{0,1},{2,3},{4,5},{6,7},{8,9},{10,11},{12,13},{14,15},{1,0},{3,2},... | collective-permute-start | bytes 196616 | tf_op jit(solution)/shard_map/ppermute | solution.py:602
  46.5 11.1 %collective-permute-start.3 = (bf16[32,1024]{1,0:T(8,128)(2,1)S(1)}, bf16[32,1024]{1,0:T(8,128)(2,1)S(1)}, u32[]{:S(2)}, u32[]{:S(2)}) collective-permute-start(bf16[32,1024]{1,0:T(8,128)(2,1)S(1)} %pad_maximum_fusion.1), channel_id=1, source_target_pairs={{1,2},{3,4},{5,6},{7,8},{9,10},{11,12},{13,14},{2,1},{4,3},{6,5},{... | collective-permute-start | bytes 196616 | tf_op jit(solution)/shard_map/ppermute | solution.py:602
  51.0 6.6 %copy-start.4 = (bf16[32,96]{1,0:T(8,128)(2,1)S(1)}, bf16[32,96]{1,0:T(8,128)(2,1)}, u32[]{:S(2)}) copy-start(bf16[32,96]{1,0:T(8,128)(2,1)} %constant.12.clone.down) | copy-start | bytes 18436

commit v7 on v6

--- a/solution.py
+++ b/solution.py
@@ -144,23 +144,22 @@
     return jnp.where(even, second, first), jnp.where(even, first, second)
 
 
-def window(k, source_ref, arrived_ref, row_ref, col_ref):
+def first_products(windows, source_ref, arrived_ref, row_ref):
     live = source_ref[0, row_ref.shape[0]]
-    part = dot(row_ref[k], arrived_ref[source_ref[0, k]])
-    part = jnp.where(k < live, part, 0.0).astype(BF16)
-    return dot(part, col_ref[k])
+    values = [dot(row_ref[k], arrived_ref[source_ref[0, k]]) for k in windows]
+    return [jnp.where(k < live, value, 0.0).astype(BF16) for k, value in zip(windows, values)]
 
 
 def edges_kernel(
     source_ref, arrived_ref, row_ref, col_ref, edge_ref, first_ref, second_ref
 ):
     edge = row_ref.shape[1]
-    for i in range(W):
-        for s in range(2):
-            k = i * W + s * (W - 1)
-            edge_ref[s, i * edge : (i + 1) * edge, :] = window(
-                k, source_ref, arrived_ref, row_ref, col_ref
-            )
+    for s in range(2):
+        windows = [i * W + s * (W - 1) for i in range(W)]
+        parts = first_products(windows, source_ref, arrived_ref, row_ref)
+        values = [dot(part, col_ref[k]) for k, part in zip(windows, parts)]
+        for i, value in enumerate(values):
+            edge_ref[s, i * edge : (i + 1) * edge, :] = value
     rows = edge_ref.shape[1]
     chunk = rows // 4
     lane = lax.broadcasted_iota(jnp.int32, (chunk, 128), 1)
@@ -208,13 +207,6 @@
         band_ref[:, s * (W - 1) * edge : (s * (W - 1) + 1) * edge] = edge_ref[s].astype(BF16)
 
 
-    def windows(i):
-        span = slice(i * edge, (i + 1) * edge)
-        for j in range(1, W - 1):
-            value = window(i * W + j, source_ref, arrived_ref, row_ref, col_ref)
-            inner_ref[j - 1, span, :] = value
-            band_ref[span, j * edge : (j + 1) * edge] = value.astype(BF16)
-
     def shifts(i):
         span = slice(i * edge, (i + 1) * edge)
         pieces = [edge_ref[0, span, :]]
@@ -234,10 +226,15 @@
             value = dot(down[...], band_ref[fallen : fallen + STEP + 2 * PAD, :])
             fall_ref[fallen : fallen + STEP, :] = value.astype(BF16)
             fallen += STEP
+        windows = [t * W + j for j in range(1, W - 1)] if t < W else []
+        parts = first_products(windows, source_ref, arrived_ref, row_ref)
         if t:
             shifts(t - 1)
-        if t < W:
-            windows(t)
+        values = [dot(part, col_ref[k]) for k, part in zip(windows, parts)]
+        span = slice(t * edge, (t + 1) * edge)
+        for j, value in enumerate(values):
+            inner_ref[j, span, :] = value
+            band_ref[span, (j + 1) * edge : (j + 2) * edge] = value.astype(BF16)
     for n in range(2):
         at = pl.multiple_of(jnp.where(odd == n, rows - PAD, 0), PAD)
         strips_ref[n] = band_ref[pl.ds(at, PAD), :]
@@ -384,7 +381,10 @@
             wide = jnp.concatenate([fall_ref[:, at - 128 :], sides[:, 128:256]], axis=1)
         else:
             wide = fall_ref[:, at - 128 : at + 384]
-        value = dot(wide, across[...])
+        return dot(wide, across[...])
+
+    def relieve(j, value):
+        at = j * 256
         for h in range(2):
             centre = mid(j * 2 + h, slice(PAD, rows - PAD))
             relief[:, at + h * 128 : at + h * 128 + 128] = (
@@ -398,9 +398,10 @@
         axis=0,
     )
     for i in range(steps):
-        if i < lanes // 2:
-            smooth(i)
+        smoothed = smooth(i) if i < lanes // 2 else None
         for q in range(STEP // 16):
+            if q == 5 and smoothed is not None:
+                relieve(i, smoothed)
             at = i * STEP + q * 16
             for j in range(lanes):
                 def load(piece):

time: 59.4 us -> 59.2 us (level)
  transfers between devices with their start and end apart: 4 -> 4, of which waited for: 0 -> 0; matrix products, arithmetic and copies ran while one was open for 0% -> 0% of each run, Pallas kernels for 16% -> 15%
where the time goes in v7:
time: 59.2 us; the launch traced here: 59.1 us
  blocking collectives  33.1 us (56%)
  Pallas kernels  14.5 us (24%)
  starting transfers between devices  10.6 us (18%)
  between operations  0.81 us (1%)
    all_to_all x1, blocking collectives, local(): lax.all_to_all(outgoing, 'gy', split_axis=0, concat_axis=0, tiled=True)  33.1 us
    ppermute x4, starting transfers between devices, swap(): lax.ppermute(value, axis, pairs + [(j, i) for i, j in pairs])  10.6 us
    pallas_call x1, Pallas kernels, main(): pl.pallas_call(main_kernel, out_shape=out_shapes(rows, cols), in_specs=[V...  6.51 us
    pallas_call x1, Pallas kernels, gather(): pl.pallas_call(gather_kernel, out_shape=[jax.ShapeDtypeStruct((holders, C...  2.71 us
    pallas_call x1, Pallas kernels, middle(): pl.pallas_call(middle_kernel, out_shape=[jax.ShapeDtypeStruct(s, d) for s...  2.5 us
    pallas_call x1, Pallas kernels, ends(): pl.pallas_call(ends_kernel, out_shape=out_shapes(rows, cols), in_specs=[V...  1.64 us
  transfers between devices with their start and end apart: 4, of which 0 were waited for; matrix products, arithmetic and copies ran while one was open for 0% of the time, Pallas kernels for 15%

profile of v7, /device:TPU:11, one launch (start us, length us, event | category | flops | bytes accessed | tf_op | source)
XLA Modules:
  0.0 59.1 jit_solution(1655248196079166624)
XLA Ops:
  0.6 2.7 %gather_blocks.1 = (bf16[16,4,128,128]{3,2,1,0:T(8,128)(2,1)}, s32[1,128]{1,0:T(1,128)}) custom-call(s32[36,128]{1,0:T(8,128)} %bitcast.13, s32[1,128]{1,0:T(1,128)} %bitcast.14, f32[32]{0:T(128)} %scale_hbm.1, bf16[32,128,128]{2,1,0:T(8,128)(2,1)} %blocks_hbm.1), custom_call_target="tpu_custom_call" | custom-call | tf_op jit(solution)/shard_map/gather_blocks/pallas_call | solution.py:109
  3.4 0.0 copy-start
  3.4 0.0 copy-start.1
  3.4 0.0 copy-start.5
  3.4 33.1 %all_to_all.5 = bf16[16,4,128,128]{3,2,1,0:T(8,128)(2,1)S(1)} all-to-all(bf16[16,4,128,128]{3,2,1,0:T(8,128)(2,1)} %get-tuple-element.19), channel_id=1, replica_groups=mesh['gx'=8,'gy'=16] {'gy'}, dimensions={0} | all-to-all | bytes 4194304 | tf_op jit(solution)/shard_map/all_to_all | solution.py:611
  36.5 0.0 copy-start.3
  36.5 0.0 copy-done
  36.5 0.0 copy-done.1
  36.5 0.0 copy-done.5
  36.5 1.1 %edge_windows.1 = (f32[2,768,128]{2,1,0:T(8,128)S(1)}, bf16[192,128]{1,0:T(8,128)(2,1)S(1)}, bf16[192,128]{1,0:T(8,128)(2,1)S(1)}) custom-call(s32[1,128]{1,0:T(1,128)S(1)} %copy-done.5, bf16[64,128,128]{2,1,0:T(8,128)(2,1)S(1)} %bitcast.11, bf16[36,128,128]{2,1,0:T(8,128)(2,1)S(1)} %copy-done, bf16[36,128,128]{2,1,0:T(8,128)(2,1)S(1)} %copy-done.1), custom_call_target="tpu_custom_call" | custom-call | flops 786432000 | bytes 4718592 | tf_op jit(solution)/shard_map/edge_windows/pallas_call | solution.py:187
  37.7 2.6 %collective-permute-start = (bf16[192,128]{1,0:T(8,128)(2,1)S(1)}, bf16[192,128]{1,0:T(8,128)(2,1)S(1)}, u32[]{:S(2)}, u32[]{:S(2)}) collective-permute-start(bf16[192,128]{1,0:T(8,128)(2,1)S(1)} %get-tuple-element.23), channel_id=1, source_target_pairs={{0,16},{32,48},{64,80},{96,112},{16,0},{48,32},{80,64},{112,96},{1... | collective-permute-start | bytes 147464 | tf_op jit(solution)/shard_map/ppermute | solution.py:603
  40.2 3.2 %collective-permute-start.1 = (bf16[192,128]{1,0:T(8,128)(2,1)S(1)}, bf16[192,128]{1,0:T(8,128)(2,1)S(1)}, u32[]{:S(2)}, u32[]{:S(2)}) collective-permute-start(bf16[192,128]{1,0:T(8,128)(2,1)S(1)} %get-tuple-element.24), channel_id=1, source_target_pairs={{16,32},{48,64},{80,96},{32,16},{64,48},{96,80},{17,33},{49,65},{8... | collective-permute-start | bytes 147464 | tf_op jit(solution)/shard_map/ppermute | solution.py:603
  43.5 0.0 copy-done.3
  43.5 0.0 copy-start.2
  43.5 2.5 %middle_windows.1 = (f32[4,768,128]{2,1,0:T(8,128)S(1)}, f32[6,768,128]{2,1,0:T(8,128)S(1)}, f32[6,768,128]{2,1,0:T(8,128)S(1)}, bf16[768,768]{1,0:T(8,128)(2,1)...) custom-call(s32[1,128]{1,0:T(1,128)S(1)} %copy-done.5, ...), custom_call_target="tpu_custom_call" | custom-call | flops 2359296000 | bytes 14155776 | tf_op jit(solution)/shard_map/middle_windows/pallas_call | solution.py:255
  46.0 0.0 collective-permute-done.first_ref
  46.0 0.0 collective-permute-done.1.second_ref
  46.1 0.2 collective-permute-start.2
  46.3 4.6 %collective-permute-start.3 = (bf16[32,1024]{1,0:T(8,128)(2,1)S(1)}, bf16[32,1024]{1,0:T(8,128)(2,1)S(1)}, u32[]{:S(2)}, u32[]{:S(2)}) collective-permute-start(bf16[32,1024]{1,0:T(8,128)(2,1)S(1)} %pad_maximum_fusion.1), channel_id=1, source_target_pairs={{1,2},{3,4},{5,6},{7,8},{9,10},{11,12},{13,14},{2,1},{4,3},{6,5},{... | collective-permute-start | bytes 196616 | tf_op jit(solution)/shard_map/ppermute | solution.py:603
  50.9 0.0 copy-done.2
  50.9 0.0 copy-start.4
  50.9 6.5 %main_cells.1 = (f32[768,768]{1,0:T(8,128)}, f32[768,768]{1,0:T(8,128)}, bf16[8,768,768]{2,1,0:T(8,128)(2,1)}) custom-call(f32[2,768,128]{2,1,0:T(8,128)S(1)} %get-tuple-element.20.edge_ref, f32[4,768,128]{2,1,0:T(8,128)S(1)} %get-tuple-element.21.inner_ref, f32[6,768,128]{2,1,0:T(8,128)S(1)} %get-tuple-element.27.low_ref, ...), custom_call_target="tpu_custom_call" | custom-call | flops 2162688000 | bytes 12976128 | tf_op jit(solution)/shard_map/main_cells/pallas_call | solution.py:431
  57.4 0.0 collective-permute-done.2.near_ref
  57.4 0.0 collective-permute-done.3.next_ref
  57.5 0.0 copy-done.4
  57.5 1.6 %end_cells.1 = (f32[768,768]{1,0:T(8,128)}, f32[768,768]{1,0:T(8,128)}, bf16[8,768,768]{2,1,0:T(8,128)(2,1)}) custom-call(f32[2,768,128]{2,1,0:T(8,128)S(1)} %get-tuple-element.20.edge_ref, f32[4,768,128]{2,1,0:T(8,128)S(1)} %get-tuple-element.21.inner_ref, ...), custom_call_target="tpu_custom_call", output_to_operand_aliasing={{0}: (9, {}), {1}: (10, {}), {2}: (11, {})} | custom-call | flops 196608000 | bytes 1179648 | tf_op jit(solution)/shard_map/end_cells/pallas_call | solution.py:573
  (5 shorter events, 0.0 us)
Async XLA Ops:
  3.4 33.2 %copy-start = (bf16[36,128,128]{2,1,0:T(8,128)(2,1)S(1)}, bf16[36,128,128]{2,1,0:T(8,128)(2,1)}, u32[]{:S(2)}) copy-start(bf16[36,128,128]{2,1,0:T(8,128)(2,1)} %row_ref.3) | copy-start | bytes 3538948
  3.4 33.2 %copy-start.1 = (bf16[36,128,128]{2,1,0:T(8,128)(2,1)S(1)}, bf16[36,128,128]{2,1,0:T(8,128)(2,1)}, u32[]{:S(2)}) copy-start(bf16[36,128,128]{2,1,0:T(8,128)(2,1)} %col_ref.3) | copy-start | bytes 3538948
  3.4 33.2 %copy-start.5 = (s32[1,128]{1,0:T(1,128)S(1)}, s32[1,128]{1,0:T(1,128)}, u32[]{:S(2)}) copy-start(s32[1,128]{1,0:T(1,128)} %get-tuple-element.18.source_ref.zero_ref) | copy-start | bytes 1540
  36.5 6.9 %copy-start.3 = (bf16[176,240]{1,0:T(8,128)(2,1)S(1)}, bf16[176,240]{1,0:T(8,128)(2,1)}, u32[]{:S(2)}) copy-start(bf16[176,240]{1,0:T(8,128)(2,1)} %constant.10.clone.down) | copy-start | bytes 253444
  37.7 8.4 %collective-permute-start = (bf16[192,128]{1,0:T(8,128)(2,1)S(1)}, bf16[192,128]{1,0:T(8,128)(2,1)S(1)}, u32[]{:S(2)}, u32[]{:S(2)}) collective-permute-start(bf16[192,128]{1,0:T(8,128)(2,1)S(1)} %get-tuple-element.23), channel_id=1, source_target_pairs={{0,16},{32,48},{64,80},{96,112},{16,0},{48,32},{80,64},{112,96},{1... | collective-permute-start | bytes 147464 | tf_op jit(solution)/shard_map/ppermute | solution.py:603
  40.2 5.8 %collective-permute-start.1 = (bf16[192,128]{1,0:T(8,128)(2,1)S(1)}, bf16[192,128]{1,0:T(8,128)(2,1)S(1)}, u32[]{:S(2)}, u32[]{:S(2)}) collective-permute-start(bf16[192,128]{1,0:T(8,128)(2,1)S(1)} %get-tuple-element.24), channel_id=1, source_target_pairs={{16,32},{48,64},{80,96},{32,16},{64,48},{96,80},{17,33},{49,65},{8... | collective-permute-start | bytes 147464 | tf_op jit(solution)/shard_map/ppermute | solution.py:603
  43.5 7.4 %copy-start.2 = (bf16[512,256]{1,0:T(8,128)(2,1)S(1)}, bf16[512,256]{1,0:T(8,128)(2,1)}, u32[]{:S(2)}) copy-start(bf16[512,256]{1,0:T(8,128)(2,1)} %constant.11.clone.across) | copy-start | bytes 786436
  46.1 11.3 %collective-permute-start.2 = (bf16[32,1024]{1,0:T(8,128)(2,1)S(1)}, bf16[32,1024]{1,0:T(8,128)(2,1)S(1)}, u32[]{:S(2)}, u32[]{:S(2)}) collective-permute-start(bf16[32,1024]{1,0:T(8,128)(2,1)S(1)} %pad_maximum_fusion), channel_id=1, source_target_pairs={{0,1},{2,3},{4,5},{6,7},{8,9},{10,11},{12,13},{14,15},{1,0},{3,2},... | collective-permute-start | bytes 196616 | tf_op jit(solution)/shard_map/ppermute | solution.py:603
  46.3 11.1 %collective-permute-start.3 = (bf16[32,1024]{1,0:T(8,128)(2,1)S(1)}, bf16[32,1024]{1,0:T(8,128)(2,1)S(1)}, u32[]{:S(2)}, u32[]{:S(2)}) collective-permute-start(bf16[32,1024]{1,0:T(8,128)(2,1)S(1)} %pad_maximum_fusion.1), channel_id=1, source_target_pairs={{1,2},{3,4},{5,6},{7,8},{9,10},{11,12},{13,14},{2,1},{4,3},{6,5},{... | collective-permute-start | bytes 196616 | tf_op jit(solution)/shard_map/ppermute | solution.py:603
  50.9 6.6 %copy-start.4 = (bf16[32,96]{1,0:T(8,128)(2,1)S(1)}, bf16[32,96]{1,0:T(8,128)(2,1)}, u32[]{:S(2)}) copy-start(bf16[32,96]{1,0:T(8,128)(2,1)} %constant.12.clone.down) | copy-start | bytes 18436

commit v8 on v7

--- a/solution.py
+++ b/solution.py
@@ -17,6 +17,8 @@
 F32 = jnp.float32
 BF16 = jnp.bfloat16
 MIB = 1 << 20
+EARLY = 4
+EARLY_ROWS = EARLY * 128 - 16 - PAD
 ZERO_AT = W * W
 
 SMEM = pl.BlockSpec(memory_space=pltpu.SMEM)
@@ -197,7 +199,8 @@
 
 def middle_kernel(
     source_ref, arrived_ref, row_ref, col_ref, edge_ref, down,
-    inner_ref, low_ref, high_ref, band_ref, fall_ref, strips_ref, odd_ref,
+    inner_ref, low_ref, high_ref, band_ref, fall_ref, strips_ref, odd_ref, slope_hbm, flow_hbm,
+    slope, flow, sems,
 ):
     edge = row_ref.shape[1]
     rows = band_ref.shape[0]
@@ -220,6 +223,36 @@
                 jnp.where(lane == 127, highs[j + 1], highs[j]) if j < W - 1 else highs[j]
             )
 
+    zero = jnp.minimum(source_ref[0, ZERO_AT], 0)
+
+    def bounds(i):
+        return max(i * edge - 16, PAD), (i + 1) * edge - 16
+
+    def copies(i):
+        start, stop = bounds(i)
+        place = (pl.ds(start, stop - start), pl.ds(edge, (W - 2) * edge))
+        span = slice(start - PAD, stop - PAD)
+        return (
+            pltpu.make_async_copy(slope.at[span], slope_hbm.at[place], sems.at[i, 0]),
+            pltpu.make_async_copy(
+                flow.at[:, span], flow_hbm.at[(slice(None),) + place], sems.at[i, 1]
+            ),
+        )
+
+    def inner_cells(i):
+        for at in range(*bounds(i), 16):
+            for j in range(W - 2):
+                def load(ref, j):
+                    return lambda d: ref[j, pl.ds(at + (zero + d if d else 0), 16), :]
+
+                value, parts = cells(load(inner_ref, j), load(low_ref, j + 1), load(high_ref, j + 1))
+                place = (slice(at - PAD, at - PAD + 16), slice(j * edge, (j + 1) * edge))
+                slope[place] = value
+                for n, part in enumerate(parts):
+                    flow[(n,) + place] = part
+        for copy in copies(i):
+            copy.start()
+
     fallen = 0
     for t in range(W + 1):
         while fallen < rows - 2 * PAD and fallen + STEP + 2 * PAD <= t * edge:
@@ -228,6 +261,8 @@
             fallen += STEP
         windows = [t * W + j for j in range(1, W - 1)] if t < W else []
         parts = first_products(windows, source_ref, arrived_ref, row_ref)
+        if t >= 2 and t - 2 < EARLY:
+            inner_cells(t - 2)
         if t:
             shifts(t - 1)
         values = [dot(part, col_ref[k]) for k, part in zip(windows, parts)]
@@ -238,6 +273,9 @@
     for n in range(2):
         at = pl.multiple_of(jnp.where(odd == n, rows - PAD, 0), PAD)
         strips_ref[n] = band_ref[pl.ds(at, PAD), :]
+    for i in range(EARLY):
+        for copy in copies(i):
+            copy.wait()
 
 
 def middle(source, arrived, row_weights, col_weights, edge_values):
@@ -252,13 +290,19 @@
         ((2, PAD, side), BF16),
         ((8, 128), jnp.int32),
     ]
+    outs = out_shapes(side, side)[1:]
     return pl.pallas_call(
         middle_kernel,
-        out_shape=[jax.ShapeDtypeStruct(s, d) for s, d in shapes],
+        out_shape=[jax.ShapeDtypeStruct(s, d) for s, d in shapes] + outs,
         in_specs=[SMEM] + [VMEM] * 5,
-        out_specs=[VMEM] * len(shapes),
+        out_specs=[VMEM] * len(shapes) + [ANY] * len(outs),
+        scratch_shapes=[
+            pltpu.VMEM((EARLY_ROWS, (W - 2) * edge), F32),
+            pltpu.VMEM((8, EARLY_ROWS, (W - 2) * edge), BF16),
+            pltpu.SemaphoreType.DMA((EARLY, 2)),
+        ],
         cost_estimate=cost(side * side),
-        compiler_params=pltpu.CompilerParams(vmem_limit_bytes=24 * MIB),
+        compiler_params=pltpu.CompilerParams(vmem_limit_bytes=32 * MIB),
         name="middle_windows",
     )(source, arrived, row_weights, col_weights, edge_values, down_taps(STEP))
 
@@ -324,7 +368,7 @@
 
 def main_kernel(
     edge_ref, inner_ref, low_ref, high_ref, fall_ref, first_ref, second_ref, across, down,
-    zero_ref, relief_hbm, slope_hbm, flow_hbm, relief, slope, flow, far, patched, sems, relief_sems,
+    zero_ref, slope_in, flow_in, relief_hbm, slope_hbm, flow_hbm, relief, slope, flow, far, patched, sems, relief_sems,
 ):
     rows, cols = low_ref.shape[1], relief.shape[1]
     lanes = cols // 128
@@ -344,17 +388,28 @@
             lane == 127, pltpu.roll(value, 127, 1), high_ref[lanes - 1, span, :]
         )
 
-    halves = ((0, 96), (96, STEP - 96))
-
-    def copies(i, half):
-        start, size = halves[half]
-        span = slice(i * STEP + start, i * STEP + start + size)
-        place = pl.ds(PAD + i * STEP + start, size)
-        sem = sems.at[i, half]
-        return (
-            pltpu.make_async_copy(slope.at[span], slope_hbm.at[place], sem.at[0]),
-            pltpu.make_async_copy(flow.at[:, span], flow_hbm.at[:, place], sem.at[1]),
-        )
+    marks = (0, 96, 192, 288, 384, EARLY_ROWS, 544, 624, rows - 2 * PAD)
+    pieces = tuple(zip(marks[:-1], marks[1:]))
+
+    def copies(i):
+        start, stop = pieces[i]
+        span = slice(start, stop)
+        place = pl.ds(PAD + start, stop - start)
+        if start < EARLY_ROWS:
+            columns = (pl.ds(0, 128), pl.ds(cols - 128, 128))
+        else:
+            columns = (pl.ds(0, cols),)
+        found = []
+        for n, column in enumerate(columns):
+            found += [
+                pltpu.make_async_copy(
+                    slope.at[span, column], slope_hbm.at[place, column], sems.at[i, n, 0]
+                ),
+                pltpu.make_async_copy(
+                    flow.at[:, span, column], flow_hbm.at[:, place, column], sems.at[i, n, 1]
+                ),
+            ]
+        return found
 
     def relief_copy(j):
         column = pl.ds(j * 256, 256)
@@ -397,49 +452,51 @@
         [dot(down[...], far[i * STEP : (i + 1) * STEP + 2 * PAD, :]).astype(BF16) for i in range(steps)],
         axis=0,
     )
-    for i in range(steps):
-        smoothed = smooth(i) if i < lanes // 2 else None
-        for q in range(STEP // 16):
-            if q == 5 and smoothed is not None:
-                relieve(i, smoothed)
-            at = i * STEP + q * 16
-            for j in range(lanes):
-                def load(piece):
-                    return lambda d: piece(j, pl.ds(at + PAD + (zero + d if d else 0), 16))
-
-                value, parts = cells(load(mid), load(low), load(high))
-                place = (slice(at, at + 16), slice(j * 128, (j + 1) * 128))
-                slope[place] = value
-                for n, part in enumerate(parts):
-                    flow[(n,) + place] = part
-            for half, (start, size) in enumerate(halves):
-                if q * 16 + 16 == start + size:
-                    for copy in copies(i, half):
-                        copy.start()
+    piece = 0
+    for q in range((rows - 2 * PAD) // 16):
+        at = q * 16
+        if q % 8 == 0:
+            if q and q // 8 <= lanes // 2:
+                relieve(q // 8 - 1, smoothed)
+            if q // 8 < lanes // 2:
+                smoothed = smooth(q // 8)
+        for j in range(lanes) if at >= EARLY_ROWS else (0, lanes - 1):
+            def load(piece):
+                return lambda d: piece(j, pl.ds(at + PAD + (zero + d if d else 0), 16))
+
+            value, parts = cells(load(mid), load(low), load(high))
+            place = (slice(at, at + 16), slice(j * 128, (j + 1) * 128))
+            slope[place] = value
+            for n, part in enumerate(parts):
+                flow[(n,) + place] = part
+        if at + 16 == pieces[piece][1]:
+            for copy in copies(piece):
+                copy.start()
+            piece += 1
     for j in range(lanes // 2):
         relief_copy(j).wait()
-    for i in range(steps):
-        for half in range(2):
-            for copy in copies(i, half):
-                copy.wait()
-
-
-def main(edge_values, inner, low, high, fall, left, right, source):
+    for i in range(len(pieces)):
+        for copy in copies(i):
+            copy.wait()
+
+
+def main(edge_values, inner, low, high, fall, left, right, source, slope, flow):
     lanes, rows, _ = low.shape
     cols = lanes * 128
     tall = rows - 2 * PAD
     return pl.pallas_call(
         main_kernel,
         out_shape=out_shapes(rows, cols),
-        in_specs=[VMEM] * 9 + [SMEM],
+        in_specs=[VMEM] * 9 + [SMEM] + [ANY] * 2,
         out_specs=[ANY] * 3,
+        input_output_aliases={10: 1, 11: 2},
         scratch_shapes=[
             pltpu.VMEM((tall, cols), F32),
             pltpu.VMEM((tall, cols), F32),
             pltpu.VMEM((8, tall, cols), BF16),
             pltpu.VMEM((rows, 256), BF16),
             pltpu.VMEM((2, rows, 128), F32),
-            pltpu.SemaphoreType.DMA((tall // STEP, 2, 2)),
+            pltpu.SemaphoreType.DMA((8, 2, 2)),
             pltpu.SemaphoreType.DMA((cols // 256,)),
         ],
         cost_estimate=cost(tall * cols),
@@ -447,7 +504,7 @@
         name="main_cells",
     )(
         edge_values, inner, low, high, fall, left, right,
-        across_taps(512, 256), down_taps(STEP), source,
+        across_taps(512, 256), down_taps(STEP), source, slope, flow,
     )
 
 
@@ -613,13 +670,15 @@
     weights = (row_weights, col_weights)
     edge_values, *messages = edges(source, arrived, *weights)
     beside = swap(*messages, "gx")
-    inner, low, high, band, fall, strips, odd = middle(source, arrived, *weights, edge_values)
+    inner, low, high, band, fall, strips, odd, *outs = middle(
+        source, arrived, *weights, edge_values
+    )
     messages = []
     for n in range(2):
         corners = [jnp.where(odd[:1] == n, side[-PAD:], side[:PAD]) for side in beside]
         messages.append(jnp.concatenate([strips[n], *corners], axis=1))
     ahead = swap(*messages, "gy")
-    outs = main(edge_values, inner, low, high, fall, *beside, source)
+    outs = main(edge_values, inner, low, high, fall, *beside, source, *outs)
     return tuple(ends(edge_values, inner, band, *beside, *ahead, outs))
 
 

time: 59.2 us -> 60 us (1.014); the launches traced: 59.1 us -> 58.9 us
  starting transfers between devices: 10.6 us -> 9.68 us
    pallas_call x1, Pallas kernels: 2.5 us -> 4.73 us  [middle(): pl.pallas_call(middle_kernel, out_shape=[jax.ShapeDtypeStruct(s, d) for s...]
    pallas_call x1, Pallas kernels: 6.51 us -> 4.93 us  [main(): pl.pallas_call(main_kernel, out_shape=out_shapes(rows, cols), in_specs=[V...]
    ppermute x4, starting transfers between devices: 10.6 us -> 9.68 us  [swap(): lax.ppermute(value, axis, pairs + [(j, i) for i, j in pairs])]
  transfers between devices with their start and end apart: 4 -> 4, of which waited for: 0 -> 0; matrix products, arithmetic and copies ran while one was open for 0% -> 0% of each run, Pallas kernels for 15% -> 16%
where the time goes in v8:
time: 60 us; the launch traced here: 58.9 us
  blocking collectives  33.3 us (55%)
  Pallas kernels  15 us (25%)
  starting transfers between devices  9.68 us (16%)
  between operations  0.82 us (1%)
    all_to_all x1, blocking collectives, local(): lax.all_to_all(outgoing, 'gy', split_axis=0, concat_axis=0, tiled=True)  33.3 us
    ppermute x4, starting transfers between devices, swap(): lax.ppermute(value, axis, pairs + [(j, i) for i, j in pairs])  9.68 us
    pallas_call x1, Pallas kernels, main(): pl.pallas_call(main_kernel, out_shape=out_shapes(rows, cols), in_specs=[V...  4.93 us
    pallas_call x1, Pallas kernels, middle(): pl.pallas_call(middle_kernel, out_shape=[jax.ShapeDtypeStruct(s, d) for s...  4.73 us
    pallas_call x1, Pallas kernels, gather(): pl.pallas_call(gather_kernel, out_shape=[jax.ShapeDtypeStruct((holders, C...  2.6 us
    pallas_call x1, Pallas kernels, ends(): pl.pallas_call(ends_kernel, out_shape=out_shapes(rows, cols), in_specs=[V...  1.64 us
  transfers between devices with their start and end apart: 4, of which 0 were waited for; matrix products, arithmetic and copies ran while one was open for 0% of the time, Pallas kernels for 16%

profile of v8, /device:TPU:11, one launch (start us, length us, event | category | flops | bytes accessed | tf_op | source)
XLA Modules:
  0.0 58.9 jit_solution(13037734438568580445)
XLA Ops:
  0.6 2.6 %gather_blocks.1 = (bf16[16,4,128,128]{3,2,1,0:T(8,128)(2,1)}, s32[1,128]{1,0:T(1,128)}) custom-call(s32[36,128]{1,0:T(8,128)} %bitcast.13, s32[1,128]{1,0:T(1,128)} %bitcast.14, f32[32]{0:T(128)} %scale_hbm.1, bf16[32,128,128]{2,1,0:T(8,128)(2,1)} %blocks_hbm.1), custom_call_target="tpu_custom_call" | custom-call | tf_op jit(solution)/shard_map/gather_blocks/pallas_call | solution.py:111
  3.2 0.0 copy-start
  3.2 0.0 copy-start.1
  3.3 0.0 copy-start.5
  3.3 33.3 %all_to_all.5 = bf16[16,4,128,128]{3,2,1,0:T(8,128)(2,1)S(1)} all-to-all(bf16[16,4,128,128]{3,2,1,0:T(8,128)(2,1)} %get-tuple-element.21), channel_id=1, replica_groups=mesh['gx'=8,'gy'=16] {'gy'}, dimensions={0} | all-to-all | bytes 4194304 | tf_op jit(solution)/shard_map/all_to_all | solution.py:668
  36.5 0.0 copy-start.3
  36.5 0.0 copy-done
  36.5 0.0 copy-done.1
  36.5 0.0 copy-done.5
  36.6 1.1 %edge_windows.1 = (f32[2,768,128]{2,1,0:T(8,128)S(1)}, bf16[192,128]{1,0:T(8,128)(2,1)S(1)}, bf16[192,128]{1,0:T(8,128)(2,1)S(1)}) custom-call(s32[1,128]{1,0:T(1,128)S(1)} %copy-done.5, bf16[64,128,128]{2,1,0:T(8,128)(2,1)S(1)} %bitcast.11, bf16[36,128,128]{2,1,0:T(8,128)(2,1)S(1)} %copy-done, bf16[36,128,128]{2,1,0:T(8,128)(2,1)S(1)} %copy-done.1), custom_call_target="tpu_custom_call" | custom-call | flops 786432000 | bytes 4718592 | tf_op jit(solution)/shard_map/edge_windows/pallas_call | solution.py:189
  37.7 2.6 %collective-permute-start = (bf16[192,128]{1,0:T(8,128)(2,1)S(1)}, bf16[192,128]{1,0:T(8,128)(2,1)S(1)}, u32[]{:S(2)}, u32[]{:S(2)}) collective-permute-start(bf16[192,128]{1,0:T(8,128)(2,1)S(1)} %get-tuple-element.25), channel_id=1, source_target_pairs={{0,16},{32,48},{64,80},{96,112},{16,0},{48,32},{80,64},{112,96},{1... | collective-permute-start | bytes 147464 | tf_op jit(solution)/shard_map/ppermute | solution.py:660
  40.3 3.1 %collective-permute-start.1 = (bf16[192,128]{1,0:T(8,128)(2,1)S(1)}, bf16[192,128]{1,0:T(8,128)(2,1)S(1)}, u32[]{:S(2)}, u32[]{:S(2)}) collective-permute-start(bf16[192,128]{1,0:T(8,128)(2,1)S(1)} %get-tuple-element.26), channel_id=1, source_target_pairs={{16,32},{48,64},{80,96},{32,16},{64,48},{96,80},{17,33},{49,65},{8... | collective-permute-start | bytes 147464 | tf_op jit(solution)/shard_map/ppermute | solution.py:660
  43.4 0.0 copy-done.3
  43.4 0.0 copy-start.2
  43.4 4.7 %middle_windows.1 = (f32[4,768,128]{2,1,0:T(8,128)S(1)}, f32[6,768,128]{2,1,0:T(8,128)S(1)}, f32[6,768,128]{2,1,0:T(8,128)S(1)}, bf16[768,768]{1,0:T(8,128)(2,1)...) custom-call(s32[1,128]{1,0:T(1,128)S(1)} %copy-done.5, ...), custom_call_target="tpu_custom_call" | custom-call | flops 2359296000 | bytes 14155776 | tf_op jit(solution)/shard_map/middle_windows/pallas_call | solution.py:294
  48.2 0.0 collective-permute-done.first_ref
  48.2 0.0 collective-permute-done.1.second_ref
  48.2 3.9 %collective-permute-start.3 = (bf16[32,1024]{1,0:T(8,128)(2,1)S(1)}, bf16[32,1024]{1,0:T(8,128)(2,1)S(1)}, u32[]{:S(2)}, u32[]{:S(2)}) collective-permute-start(bf16[32,1024]{1,0:T(8,128)(2,1)S(1)} %pad_maximum_fusion.1), channel_id=1, source_target_pairs={{1,2},{3,4},{5,6},{7,8},{9,10},{11,12},{13,14},{2,1},{4,3},{6,5},{... | collective-permute-start | bytes 196616 | tf_op jit(solution)/shard_map/ppermute | solution.py:660
  52.1 0.1 collective-permute-start.2
  52.2 0.0 copy-done.2
  52.3 0.0 copy-start.4
  52.3 4.9 %main_cells.1 = (f32[768,768]{1,0:T(8,128)}, f32[768,768]{1,0:T(8,128)}, bf16[8,768,768]{2,1,0:T(8,128)(2,1)}) custom-call(f32[2,768,128]{2,1,0:T(8,128)S(1)} %get-tuple-element.22.edge_ref, f32[4,768,128]{2,1,0:T(8,128)S(1)} %get-tuple-element.23.inner_ref, ...), custom_call_target="tpu_custom_call", output_to_operand_aliasing={{1}: (10, {}), {2}: (11, {})} | custom-call | flops 2162688000 | bytes 12976128 | tf_op jit(solution)/shard_map/main_cells/pallas_call | solution.py:487
  57.2 0.0 collective-permute-done.3.next_ref
  57.2 0.0 collective-permute-done.2.near_ref
  57.2 0.0 copy-done.4
  57.2 1.6 %end_cells.1 = (f32[768,768]{1,0:T(8,128)}, f32[768,768]{1,0:T(8,128)}, bf16[8,768,768]{2,1,0:T(8,128)(2,1)}) custom-call(f32[2,768,128]{2,1,0:T(8,128)S(1)} %get-tuple-element.22.edge_ref, f32[4,768,128]{2,1,0:T(8,128)S(1)} %get-tuple-element.23.inner_ref, ...), custom_call_target="tpu_custom_call", output_to_operand_aliasing={{0}: (9, {}), {1}: (10, {}), {2}: (11, {})} | custom-call | flops 196608000 | bytes 1179648 | tf_op jit(solution)/shard_map/end_cells/pallas_call | solution.py:630
  (5 shorter events, 0.0 us)
Async XLA Ops:
  3.2 33.3 %copy-start = (bf16[36,128,128]{2,1,0:T(8,128)(2,1)S(1)}, bf16[36,128,128]{2,1,0:T(8,128)(2,1)}, u32[]{:S(2)}) copy-start(bf16[36,128,128]{2,1,0:T(8,128)(2,1)} %row_ref.3) | copy-start | bytes 3538948
  3.2 33.3 %copy-start.1 = (bf16[36,128,128]{2,1,0:T(8,128)(2,1)S(1)}, bf16[36,128,128]{2,1,0:T(8,128)(2,1)}, u32[]{:S(2)}) copy-start(bf16[36,128,128]{2,1,0:T(8,128)(2,1)} %col_ref.3) | copy-start | bytes 3538948
  3.3 33.3 %copy-start.5 = (s32[1,128]{1,0:T(1,128)S(1)}, s32[1,128]{1,0:T(1,128)}, u32[]{:S(2)}) copy-start(s32[1,128]{1,0:T(1,128)} %get-tuple-element.20.source_ref.zero_ref) | copy-start | bytes 1540
  36.5 6.8 %copy-start.3 = (bf16[176,240]{1,0:T(8,128)(2,1)S(1)}, bf16[176,240]{1,0:T(8,128)(2,1)}, u32[]{:S(2)}) copy-start(bf16[176,240]{1,0:T(8,128)(2,1)} %constant.10.clone.down) | copy-start | bytes 253444
  37.7 10.5 %collective-permute-start = (bf16[192,128]{1,0:T(8,128)(2,1)S(1)}, bf16[192,128]{1,0:T(8,128)(2,1)S(1)}, u32[]{:S(2)}, u32[]{:S(2)}) collective-permute-start(bf16[192,128]{1,0:T(8,128)(2,1)S(1)} %get-tuple-element.25), channel_id=1, source_target_pairs={{0,16},{32,48},{64,80},{96,112},{16,0},{48,32},{80,64},{112,96},{1... | collective-permute-start | bytes 147464 | tf_op jit(solution)/shard_map/ppermute | solution.py:660
  40.3 7.9 %collective-permute-start.1 = (bf16[192,128]{1,0:T(8,128)(2,1)S(1)}, bf16[192,128]{1,0:T(8,128)(2,1)S(1)}, u32[]{:S(2)}, u32[]{:S(2)}) collective-permute-start(bf16[192,128]{1,0:T(8,128)(2,1)S(1)} %get-tuple-element.26), channel_id=1, source_target_pairs={{16,32},{48,64},{80,96},{32,16},{64,48},{96,80},{17,33},{49,65},{8... | collective-permute-start | bytes 147464 | tf_op jit(solution)/shard_map/ppermute | solution.py:660
  43.4 8.9 %copy-start.2 = (bf16[512,256]{1,0:T(8,128)(2,1)S(1)}, bf16[512,256]{1,0:T(8,128)(2,1)}, u32[]{:S(2)}) copy-start(bf16[512,256]{1,0:T(8,128)(2,1)} %constant.11.clone.across) | copy-start | bytes 786436
  48.2 9.0 %collective-permute-start.3 = (bf16[32,1024]{1,0:T(8,128)(2,1)S(1)}, bf16[32,1024]{1,0:T(8,128)(2,1)S(1)}, u32[]{:S(2)}, u32[]{:S(2)}) collective-permute-start(bf16[32,1024]{1,0:T(8,128)(2,1)S(1)} %pad_maximum_fusion.1), channel_id=1, source_target_pairs={{1,2},{3,4},{5,6},{7,8},{9,10},{11,12},{13,14},{2,1},{4,3},{6,5},{... | collective-permute-start | bytes 196616 | tf_op jit(solution)/shard_map/ppermute | solution.py:660
  52.1 5.1 %collective-permute-start.2 = (bf16[32,1024]{1,0:T(8,128)(2,1)S(1)}, bf16[32,1024]{1,0:T(8,128)(2,1)S(1)}, u32[]{:S(2)}, u32[]{:S(2)}) collective-permute-start(bf16[32,1024]{1,0:T(8,128)(2,1)S(1)} %pad_maximum_fusion), channel_id=1, source_target_pairs={{0,1},{2,3},{4,5},{6,7},{8,9},{10,11},{12,13},{14,15},{1,0},{3,2},... | collective-permute-start | bytes 196616 | tf_op jit(solution)/shard_map/ppermute | solution.py:660
  52.3 5.0 %copy-start.4 = (bf16[32,96]{1,0:T(8,128)(2,1)S(1)}, bf16[32,96]{1,0:T(8,128)(2,1)}, u32[]{:S(2)}) copy-start(bf16[32,96]{1,0:T(8,128)(2,1)} %constant.12.clone.down) | copy-start | bytes 18436

commit v9 on v7

--- a/solution.py
+++ b/solution.py
@@ -344,16 +344,16 @@
             lane == 127, pltpu.roll(value, 127, 1), high_ref[lanes - 1, span, :]
         )
 
-    halves = ((0, 96), (96, STEP - 96))
-
-    def copies(i, half):
-        start, size = halves[half]
-        span = slice(i * STEP + start, i * STEP + start + size)
-        place = pl.ds(PAD + i * STEP + start, size)
-        sem = sems.at[i, half]
+    marks = (0, 48, 112, 208, 304, 400, 496, 576, 640, 688, rows - 2 * PAD)
+    pieces = tuple(zip(marks[:-1], marks[1:]))
+
+    def copies(i):
+        start, stop = pieces[i]
+        span = slice(start, stop)
+        place = pl.ds(PAD + start, stop - start)
         return (
-            pltpu.make_async_copy(slope.at[span], slope_hbm.at[place], sem.at[0]),
-            pltpu.make_async_copy(flow.at[:, span], flow_hbm.at[:, place], sem.at[1]),
+            pltpu.make_async_copy(slope.at[span], slope_hbm.at[place], sems.at[i, 0]),
+            pltpu.make_async_copy(flow.at[:, span], flow_hbm.at[:, place], sems.at[i, 1]),
         )
 
     def relief_copy(j):
@@ -393,35 +393,36 @@
         relief_copy(j).start()
 
     zero = jnp.minimum(zero_ref[0, ZERO_AT], 0)
-    sides = jnp.concatenate(
-        [dot(down[...], far[i * STEP : (i + 1) * STEP + 2 * PAD, :]).astype(BF16) for i in range(steps)],
-        axis=0,
-    )
-    for i in range(steps):
-        smoothed = smooth(i) if i < lanes // 2 else None
-        for q in range(STEP // 16):
-            if q == 5 and smoothed is not None:
-                relieve(i, smoothed)
-            at = i * STEP + q * 16
-            for j in range(lanes):
-                def load(piece):
-                    return lambda d: piece(j, pl.ds(at + PAD + (zero + d if d else 0), 16))
-
-                value, parts = cells(load(mid), load(low), load(high))
-                place = (slice(at, at + 16), slice(j * 128, (j + 1) * 128))
-                slope[place] = value
-                for n, part in enumerate(parts):
-                    flow[(n,) + place] = part
-            for half, (start, size) in enumerate(halves):
-                if q * 16 + 16 == start + size:
-                    for copy in copies(i, half):
-                        copy.start()
+    piece = 0
+    for q in range((rows - 2 * PAD) // 16):
+        at = q * 16
+        if q == 3:
+            sides = jnp.concatenate(
+                [dot(down[...], far[i * STEP : (i + 1) * STEP + 2 * PAD, :]).astype(BF16) for i in range(steps)],
+                axis=0,
+            )
+        if q in (3, 13, 23):
+            smoothed = smooth(q // 10)
+        if q in (8, 18, 28):
+            relieve(q // 10, smoothed)
+        for j in range(lanes):
+            def load(piece):
+                return lambda d: piece(j, pl.ds(at + PAD + (zero + d if d else 0), 16))
+
+            value, parts = cells(load(mid), load(low), load(high))
+            place = (slice(at, at + 16), slice(j * 128, (j + 1) * 128))
+            slope[place] = value
+            for n, part in enumerate(parts):
+                flow[(n,) + place] = part
+        if at + 16 == pieces[piece][1]:
+            for copy in copies(piece):
+                copy.start()
+            piece += 1
     for j in range(lanes // 2):
         relief_copy(j).wait()
-    for i in range(steps):
-        for half in range(2):
-            for copy in copies(i, half):
-                copy.wait()
+    for i in range(len(pieces)):
+        for copy in copies(i):
+            copy.wait()
 
 
 def main(edge_values, inner, low, high, fall, left, right, source):
@@ -439,7 +440,7 @@
             pltpu.VMEM((8, tall, cols), BF16),
             pltpu.VMEM((rows, 256), BF16),
             pltpu.VMEM((2, rows, 128), F32),
-            pltpu.SemaphoreType.DMA((tall // STEP, 2, 2)),
+            pltpu.SemaphoreType.DMA((10, 2)),
             pltpu.SemaphoreType.DMA((cols // 256,)),
         ],
         cost_estimate=cost(tall * cols),

time: 59.2 us -> 59.2 us (level)
  no operation moved by 1% of the time
where the time goes in v9:
time: 59.2 us; the launch traced here: 58.7 us
  blocking collectives  33.2 us (56%)
  Pallas kernels  14.5 us (24%)
  starting transfers between devices  10.1 us (17%)
  between operations  0.81 us (1%)
    all_to_all x1, blocking collectives, local(): lax.all_to_all(outgoing, 'gy', split_axis=0, concat_axis=0, tiled=True)  33.2 us
    ppermute x4, starting transfers between devices, swap(): lax.ppermute(value, axis, pairs + [(j, i) for i, j in pairs])  10.1 us
    pallas_call x1, Pallas kernels, main(): pl.pallas_call(main_kernel, out_shape=out_shapes(rows, cols), in_specs=[V...  6.54 us
    pallas_call x1, Pallas kernels, gather(): pl.pallas_call(gather_kernel, out_shape=[jax.ShapeDtypeStruct((holders, C...  2.67 us
    pallas_call x1, Pallas kernels, middle(): pl.pallas_call(middle_kernel, out_shape=[jax.ShapeDtypeStruct(s, d) for s...  2.51 us
    pallas_call x1, Pallas kernels, ends(): pl.pallas_call(ends_kernel, out_shape=out_shapes(rows, cols), in_specs=[V...  1.64 us
  transfers between devices with their start and end apart: 4, of which 0 were waited for; matrix products, arithmetic and copies ran while one was open for 0% of the time, Pallas kernels for 15%

profile of v9, /device:TPU:11, one launch (start us, length us, event | category | flops | bytes accessed | tf_op | source)
XLA Modules:
  0.0 58.7 jit_solution(6360178554148705991)
XLA Ops:
  0.6 2.7 %gather_blocks.1 = (bf16[16,4,128,128]{3,2,1,0:T(8,128)(2,1)}, s32[1,128]{1,0:T(1,128)}) custom-call(s32[36,128]{1,0:T(8,128)} %bitcast.13, s32[1,128]{1,0:T(1,128)} %bitcast.14, f32[32]{0:T(128)} %scale_hbm.1, bf16[32,128,128]{2,1,0:T(8,128)(2,1)} %blocks_hbm.1), custom_call_target="tpu_custom_call" | custom-call | tf_op jit(solution)/shard_map/gather_blocks/pallas_call | solution.py:109
  3.3 0.0 copy-start
  3.3 0.0 copy-start.1
  3.3 0.0 copy-start.5
  3.3 33.2 %all_to_all.5 = bf16[16,4,128,128]{3,2,1,0:T(8,128)(2,1)S(1)} all-to-all(bf16[16,4,128,128]{3,2,1,0:T(8,128)(2,1)} %get-tuple-element.19), channel_id=1, replica_groups=mesh['gx'=8,'gy'=16] {'gy'}, dimensions={0} | all-to-all | bytes 4194304 | tf_op jit(solution)/shard_map/all_to_all | solution.py:612
  36.5 0.0 copy-start.3
  36.5 0.0 copy-done
  36.5 0.0 copy-done.1
  36.5 0.0 copy-done.5
  36.6 1.1 %edge_windows.1 = (f32[2,768,128]{2,1,0:T(8,128)S(1)}, bf16[192,128]{1,0:T(8,128)(2,1)S(1)}, bf16[192,128]{1,0:T(8,128)(2,1)S(1)}) custom-call(s32[1,128]{1,0:T(1,128)S(1)} %copy-done.5, bf16[64,128,128]{2,1,0:T(8,128)(2,1)S(1)} %bitcast.11, bf16[36,128,128]{2,1,0:T(8,128)(2,1)S(1)} %copy-done, bf16[36,128,128]{2,1,0:T(8,128)(2,1)S(1)} %copy-done.1), custom_call_target="tpu_custom_call" | custom-call | flops 786432000 | bytes 4718592 | tf_op jit(solution)/shard_map/edge_windows/pallas_call | solution.py:187
  37.7 2.6 %collective-permute-start = (bf16[192,128]{1,0:T(8,128)(2,1)S(1)}, bf16[192,128]{1,0:T(8,128)(2,1)S(1)}, u32[]{:S(2)}, u32[]{:S(2)}) collective-permute-start(bf16[192,128]{1,0:T(8,128)(2,1)S(1)} %get-tuple-element.23), channel_id=1, source_target_pairs={{0,16},{32,48},{64,80},{96,112},{16,0},{48,32},{80,64},{112,96},{1... | collective-permute-start | bytes 147464 | tf_op jit(solution)/shard_map/ppermute | solution.py:604
  40.3 2.9 %collective-permute-start.1 = (bf16[192,128]{1,0:T(8,128)(2,1)S(1)}, bf16[192,128]{1,0:T(8,128)(2,1)S(1)}, u32[]{:S(2)}, u32[]{:S(2)}) collective-permute-start(bf16[192,128]{1,0:T(8,128)(2,1)S(1)} %get-tuple-element.24), channel_id=1, source_target_pairs={{16,32},{48,64},{80,96},{32,16},{64,48},{96,80},{17,33},{49,65},{8... | collective-permute-start | bytes 147464 | tf_op jit(solution)/shard_map/ppermute | solution.py:604
  43.2 0.0 copy-done.3
  43.2 0.0 copy-start.2
  43.2 2.5 %middle_windows.1 = (f32[4,768,128]{2,1,0:T(8,128)S(1)}, f32[6,768,128]{2,1,0:T(8,128)S(1)}, f32[6,768,128]{2,1,0:T(8,128)S(1)}, bf16[768,768]{1,0:T(8,128)(2,1)...) custom-call(s32[1,128]{1,0:T(1,128)S(1)} %copy-done.5, ...), custom_call_target="tpu_custom_call" | custom-call | flops 2359296000 | bytes 14155776 | tf_op jit(solution)/shard_map/middle_windows/pallas_call | solution.py:255
  45.8 0.0 collective-permute-done.first_ref
  45.8 0.0 collective-permute-done.1.second_ref
  45.8 0.2 collective-permute-start.2
  46.0 4.4 %collective-permute-start.3 = (bf16[32,1024]{1,0:T(8,128)(2,1)S(1)}, bf16[32,1024]{1,0:T(8,128)(2,1)S(1)}, u32[]{:S(2)}, u32[]{:S(2)}) collective-permute-start(bf16[32,1024]{1,0:T(8,128)(2,1)S(1)} %pad_maximum_fusion.1), channel_id=1, source_target_pairs={{1,2},{3,4},{5,6},{7,8},{9,10},{11,12},{13,14},{2,1},{4,3},{6,5},{... | collective-permute-start | bytes 196616 | tf_op jit(solution)/shard_map/ppermute | solution.py:604
  50.4 0.0 copy-done.2
  50.5 0.0 copy-start.4
  50.5 6.5 %main_cells.1 = (f32[768,768]{1,0:T(8,128)}, f32[768,768]{1,0:T(8,128)}, bf16[8,768,768]{2,1,0:T(8,128)(2,1)}) custom-call(f32[2,768,128]{2,1,0:T(8,128)S(1)} %get-tuple-element.20.edge_ref, f32[4,768,128]{2,1,0:T(8,128)S(1)} %get-tuple-element.21.inner_ref, f32[6,768,128]{2,1,0:T(8,128)S(1)} %get-tuple-element.27.low_ref, ...), custom_call_target="tpu_custom_call" | custom-call | flops 2162688000 | bytes 12976128 | tf_op jit(solution)/shard_map/main_cells/pallas_call | solution.py:432
  57.0 0.0 collective-permute-done.2.near_ref
  57.0 0.0 collective-permute-done.3.next_ref
  57.0 0.0 copy-done.4
  57.0 1.6 %end_cells.1 = (f32[768,768]{1,0:T(8,128)}, f32[768,768]{1,0:T(8,128)}, bf16[8,768,768]{2,1,0:T(8,128)(2,1)}) custom-call(f32[2,768,128]{2,1,0:T(8,128)S(1)} %get-tuple-element.20.edge_ref, f32[4,768,128]{2,1,0:T(8,128)S(1)} %get-tuple-element.21.inner_ref, ...), custom_call_target="tpu_custom_call", output_to_operand_aliasing={{0}: (9, {}), {1}: (10, {}), {2}: (11, {})} | custom-call | flops 196608000 | bytes 1179648 | tf_op jit(solution)/shard_map/end_cells/pallas_call | solution.py:574
  (5 shorter events, 0.0 us)
Async XLA Ops:
  3.3 33.2 %copy-start = (bf16[36,128,128]{2,1,0:T(8,128)(2,1)S(1)}, bf16[36,128,128]{2,1,0:T(8,128)(2,1)}, u32[]{:S(2)}) copy-start(bf16[36,128,128]{2,1,0:T(8,128)(2,1)} %row_ref.3) | copy-start | bytes 3538948
  3.3 33.2 %copy-start.1 = (bf16[36,128,128]{2,1,0:T(8,128)(2,1)S(1)}, bf16[36,128,128]{2,1,0:T(8,128)(2,1)}, u32[]{:S(2)}) copy-start(bf16[36,128,128]{2,1,0:T(8,128)(2,1)} %col_ref.3) | copy-start | bytes 3538948
  3.3 33.2 %copy-start.5 = (s32[1,128]{1,0:T(1,128)S(1)}, s32[1,128]{1,0:T(1,128)}, u32[]{:S(2)}) copy-start(s32[1,128]{1,0:T(1,128)} %get-tuple-element.18.source_ref.zero_ref) | copy-start | bytes 1540
  36.5 6.7 %copy-start.3 = (bf16[176,240]{1,0:T(8,128)(2,1)S(1)}, bf16[176,240]{1,0:T(8,128)(2,1)}, u32[]{:S(2)}) copy-start(bf16[176,240]{1,0:T(8,128)(2,1)} %constant.10.clone.down) | copy-start | bytes 253444
  37.7 8.1 %collective-permute-start = (bf16[192,128]{1,0:T(8,128)(2,1)S(1)}, bf16[192,128]{1,0:T(8,128)(2,1)S(1)}, u32[]{:S(2)}, u32[]{:S(2)}) collective-permute-start(bf16[192,128]{1,0:T(8,128)(2,1)S(1)} %get-tuple-element.23), channel_id=1, source_target_pairs={{0,16},{32,48},{64,80},{96,112},{16,0},{48,32},{80,64},{112,96},{1... | collective-permute-start | bytes 147464 | tf_op jit(solution)/shard_map/ppermute | solution.py:604
  40.3 5.5 %collective-permute-start.1 = (bf16[192,128]{1,0:T(8,128)(2,1)S(1)}, bf16[192,128]{1,0:T(8,128)(2,1)S(1)}, u32[]{:S(2)}, u32[]{:S(2)}) collective-permute-start(bf16[192,128]{1,0:T(8,128)(2,1)S(1)} %get-tuple-element.24), channel_id=1, source_target_pairs={{16,32},{48,64},{80,96},{32,16},{64,48},{96,80},{17,33},{49,65},{8... | collective-permute-start | bytes 147464 | tf_op jit(solution)/shard_map/ppermute | solution.py:604
  43.2 7.2 %copy-start.2 = (bf16[512,256]{1,0:T(8,128)(2,1)S(1)}, bf16[512,256]{1,0:T(8,128)(2,1)}, u32[]{:S(2)}) copy-start(bf16[512,256]{1,0:T(8,128)(2,1)} %constant.11.clone.across) | copy-start | bytes 786436
  45.8 11.2 %collective-permute-start.2 = (bf16[32,1024]{1,0:T(8,128)(2,1)S(1)}, bf16[32,1024]{1,0:T(8,128)(2,1)S(1)}, u32[]{:S(2)}, u32[]{:S(2)}) collective-permute-start(bf16[32,1024]{1,0:T(8,128)(2,1)S(1)} %pad_maximum_fusion), channel_id=1, source_target_pairs={{0,1},{2,3},{4,5},{6,7},{8,9},{10,11},{12,13},{14,15},{1,0},{3,2},... | collective-permute-start | bytes 196616 | tf_op jit(solution)/shard_map/ppermute | solution.py:604
  46.0 11.0 %collective-permute-start.3 = (bf16[32,1024]{1,0:T(8,128)(2,1)S(1)}, bf16[32,1024]{1,0:T(8,128)(2,1)S(1)}, u32[]{:S(2)}, u32[]{:S(2)}) collective-permute-start(bf16[32,1024]{1,0:T(8,128)(2,1)S(1)} %pad_maximum_fusion.1), channel_id=1, source_target_pairs={{1,2},{3,4},{5,6},{7,8},{9,10},{11,12},{13,14},{2,1},{4,3},{6,5},{... | collective-permute-start | bytes 196616 | tf_op jit(solution)/shard_map/ppermute | solution.py:604
  50.5 6.6 %copy-start.4 = (bf16[32,96]{1,0:T(8,128)(2,1)S(1)}, bf16[32,96]{1,0:T(8,128)(2,1)}, u32[]{:S(2)}) copy-start(bf16[32,96]{1,0:T(8,128)(2,1)} %constant.12.clone.down) | copy-start | bytes 18436
